TPU v7x, 32 devices: a whole 2x2x4 slice. The times are simulated.
32 devices in a mesh: branch: 2 (over core), dp: 8 (over z, x), tensor: 2 (over y).
Axes of the slice: x: 2, y: 2, z: 4, core: 2. Of those that a mesh axis runs over, the one named last changes fastest.
Arguments:
- crops: bfloat16 [2, 64, 256, 384], P('branch', 'dp'), may hold values from -6 to 6
- segment_ids: int32 [2, 64, 256], P(None, 'dp'), may hold values from 0 to 6, as said below
- cotangent: bfloat16 [64, 256, 384], P('dp'), may hold values from -6 to 6
- qkv_weight: float32 [2, 384, 3, 384], P('branch', 'dp', None, 'tensor'), may hold values from -0.4375 to 0.4375
- out_weight: float32 [2, 384, 384], P('branch', 'tensor', 'dp'), may hold values from -2 to 2
- up_weight: float32 [2, 384, 1536], P('branch', 'dp', 'tensor'), may hold values from -0.3125 to 0.3125
- down_weight: float32 [2, 1536, 384], P('branch', 'tensor', 'dp'), may hold values from -0.21875 to 0.21875
- gain_rows: float32 [2, 2, 384], P('branch', None, 'dp'), may hold values from 0.5 to 1.5
- biases: float32 [2, 4, 384], P('branch', None, 'dp'), may hold values from -1.8 to 1.8
Outputs:
- encoded: bfloat16 [2, 64, 256, 384], P('branch', 'dp')
- crop_grad: float32 [64, 256, 384], P('dp', None, 'branch')
- qkv_weight_grad: float32 [384, 3, 384], P(('branch', 'dp'), None, 'tensor')
- out_weight_grad: float32 [384, 384], P('tensor', ('branch', 'dp'))
- up_weight_grad: float32 [384, 1536], P(('branch', 'dp'), 'tensor')
- down_weight_grad: float32 [1536, 384], P('tensor', ('branch', 'dp'))
- gain_grad: float32 [2, 384], P(None, ('branch', 'dp'))
- bias_grad: float32 [4, 384], P(None, ('branch', 'dp'))
Inputs may be any that keep to these rules, and one draw needn't show every extreme that they name: `segment_ids`: each sequence holds 6 crops of exactly 37 consecutive slots, numbered 1 to 6 in order; every other slot is padding with id 0, in gaps before, between and after the crops.
All inputs are finite; a program needn't handle non-finite values.
Results may differ from a plain program's by a relative error of at most 0.02.
Values may be sent and summed in bfloat16 or wider, within the bound.
No kernel may reach another device: no remote copies, remote signals or barrier semaphores. Data moves between devices by JAX's collectives and lax.ppermute only.
A program may use at most 128 MiB of HBM per device.

v0:
```python
import functools
import math

import jax
import jax.numpy as jnp
from jax import lax
from jax.sharding import PartitionSpec as P

HD = 32


EPSILON = 1e-06
MASKED_SCORE = -1e30


def from_partner(block, axis, stride):
    count = lax.axis_size(axis)
    route = []
    for low in range(count):
        high = low | 1 << stride
        if high != low and high < count:
            route += [(low, high), (high, low)]
    return lax.ppermute(block, axis, route)


def shifted(shard, axis, by):
    peers = lax.axis_size(axis)
    pairs = [(i, i + by) for i in range(peers) if 0 <= i + by < peers]
    return lax.ppermute(shard, axis, pairs)


def layer_norm(values, gain_row, bias_row):
    centred = values - jnp.mean(values, axis=-1, keepdims=True)
    spread = jnp.mean(centred * centred, axis=-1, keepdims=True)
    return centred * lax.rsqrt(spread + EPSILON) * gain_row + bias_row


def norm_back(values, gain_row, bias_row, upstream):
    normed_out, pullback = jax.vjp(layer_norm, values, gain_row, bias_row)
    return pullback(upstream)


def head_sum(partial_rows):
    return lax.psum(partial_rows.astype(jnp.bfloat16), "tensor").astype(jnp.float32)


def back_sum(partial_rows):
    return lax.psum(partial_rows.astype(jnp.bfloat16), "tensor").astype(jnp.float32)


def masked_scores(queries, keys_part, seg_block):
    same_doc = (seg_block[:, :, None] == seg_block[:, None, :])[:, None]
    scores = jnp.einsum("bqhe,bkhe->bhqk", queries, keys_part, preferred_element_type=jnp.float32)
    scores = scores * queries.shape[-1] ** (-0.5)
    return jnp.where(same_doc, scores, MASKED_SCORE)


def attend_block(member):
    queries, keys_part, values_part, seg_block = member
    scores = masked_scores(queries, keys_part, seg_block)
    row_max = jnp.max(scores, axis=-1, keepdims=True)
    weights = jnp.exp(scores - row_max)
    row_sum = jnp.sum(weights, axis=-1, keepdims=True)
    probs_low = (weights / row_sum).astype(jnp.bfloat16)
    context = jnp.einsum(
        "bhqk,bkhe->bqhe", probs_low, values_part, preferred_element_type=jnp.float32
    )
    return (context.astype(jnp.bfloat16), row_max + jnp.log(row_sum))


def attend_back(member):
    queries, keys_part, values_part, seg_block, log_total, d_context = member
    scores = masked_scores(queries, keys_part, seg_block)
    probs = jnp.exp(scores - log_total)
    probs_low = probs.astype(jnp.bfloat16)
    d_probs = jnp.einsum(
        "bqhe,bkhe->bhqk", d_context, values_part, preferred_element_type=jnp.float32
    )
    d_values = jnp.einsum(
        "bhqk,bqhe->bkhe", probs_low, d_context, preferred_element_type=jnp.float32
    )
    row_delta = jnp.sum(probs * d_probs, axis=-1, keepdims=True)
    d_scores = (probs * (d_probs - row_delta)).astype(jnp.bfloat16)
    score_scale = queries.shape[-1] ** (-0.5)
    d_queries = (
        jnp.einsum("bhqk,bkhe->bqhe", d_scores, keys_part, preferred_element_type=jnp.float32)
        * score_scale
    )
    d_keys = (
        jnp.einsum("bhqk,bqhe->bkhe", d_scores, queries, preferred_element_type=jnp.float32)
        * score_scale
    )
    return (d_queries, d_keys, d_values)


def on_device(
    crops, segment_ids, cotangent, qkv_weight, out_weight, up_weight, down_weight, gain_rows, biases
):
    branch = lax.axis_index("branch")
    own_shards = (
        qkv_weight[0].astype(jnp.bfloat16),
        out_weight[0].astype(jnp.bfloat16),
        up_weight[0].astype(jnp.bfloat16),
        down_weight[0].astype(jnp.bfloat16),
        gain_rows[0].astype(jnp.bfloat16),
        biases[0].astype(jnp.bfloat16),
    )
    inputs = from_partner(crops, "branch", 0)[0]
    input_ids = lax.dynamic_index_in_dim(segment_ids, 1 - branch, 0, keepdims=False)
    query_branch = 0
    sequences, slot_count, model_width = inputs.shape
    row_count = sequences * slot_count
    block_seqs = math.gcd(sequences, max(1, 512 // slot_count))
    block_count = sequences // block_seqs
    params = (
        lax.all_gather(own_shards[0], "dp", axis=0, tiled=True),
        lax.all_gather(own_shards[1], "dp", axis=1, tiled=True),
        lax.all_gather(own_shards[2], "dp", axis=0, tiled=True),
        lax.all_gather(own_shards[3], "dp", axis=1, tiled=True),
        lax.all_gather(own_shards[4], "dp", axis=1, tiled=True),
        lax.all_gather(own_shards[5], "dp", axis=1, tiled=True),
    )
    qkv_full, out_full, up_full, down_full, gain_full, bias_full = params
    gain_float = gain_full.astype(jnp.float32)
    bias_float = bias_full.astype(jnp.float32)
    flat_rows = inputs.reshape(row_count, model_width).astype(jnp.float32)
    normed = layer_norm(flat_rows, gain_float[0], bias_float[0]).astype(jnp.bfloat16)
    projected = jnp.einsum(
        "nd,dce->nce", normed, qkv_full, preferred_element_type=jnp.float32
    ).astype(jnp.bfloat16)
    head_width = projected.shape[2]
    local_heads = head_width // HD

    def split_heads(matrix):
        return matrix.reshape(block_count, block_seqs, slot_count, local_heads, HD)

    queries = split_heads(projected[:, 0])
    keys_part = split_heads(projected[:, 1])
    values_part = split_heads(projected[:, 2])
    seg_blocks = input_ids.reshape(block_count, block_seqs, slot_count)
    context, log_total = lax.map(attend_block, (queries, keys_part, values_part, seg_blocks))
    context_flat = context.reshape(row_count, head_width)
    attn_total = head_sum(jnp.dot(context_flat, out_full, preferred_element_type=jnp.float32))
    residual = flat_rows + attn_total + bias_float[1]
    normed_two = layer_norm(residual, gain_float[1], bias_float[2]).astype(jnp.bfloat16)
    pre_act = jnp.dot(normed_two, up_full, preferred_element_type=jnp.float32)
    hidden = jax.nn.gelu(pre_act, approximate=False).astype(jnp.bfloat16)
    mlp_total = head_sum(jnp.dot(hidden, down_full, preferred_element_type=jnp.float32))
    output = residual + mlp_total + bias_float[3]
    output_low = output.astype(jnp.bfloat16).reshape(1, sequences, slot_count, model_width)
    encoded = from_partner(output_low, "branch", 0)
    params_back = (
        lax.all_gather(own_shards[0], "dp", axis=0, tiled=True),
        lax.all_gather(own_shards[1], "dp", axis=1, tiled=True),
        lax.all_gather(own_shards[2], "dp", axis=0, tiled=True),
        lax.all_gather(own_shards[3], "dp", axis=1, tiled=True),
        lax.all_gather(own_shards[4], "dp", axis=1, tiled=True),
        lax.all_gather(own_shards[5], "dp", axis=1, tiled=True),
    )
    qkv_back, out_back, up_back, down_back, gain_back, bias_back = params_back
    gain_again = gain_back.astype(jnp.float32)
    bias_again = bias_back.astype(jnp.float32)
    cot_low = cotangent.reshape(row_count, model_width)
    cot_float = cot_low.astype(jnp.float32)
    down_weight_grad = jnp.dot(hidden.T, cot_low, preferred_element_type=jnp.float32)
    d_hidden = jnp.dot(cot_low, down_back.T, preferred_element_type=jnp.float32)
    gelu_out, gelu_pull = jax.vjp(functools.partial(jax.nn.gelu, approximate=False), pre_act)
    d_pre = gelu_pull(d_hidden)[0].astype(jnp.bfloat16)
    up_weight_grad = jnp.dot(normed_two.T, d_pre, preferred_element_type=jnp.float32)
    d_normed_two = back_sum(jnp.dot(d_pre, up_back.T, preferred_element_type=jnp.float32))
    d_residual_norm, d_gain_two, d_bias_two = norm_back(
        residual, gain_again[1], bias_again[2], d_normed_two
    )
    d_residual = cot_float + d_residual_norm
    d_attn = d_residual.astype(jnp.bfloat16)
    out_weight_grad = jnp.dot(context_flat.T, d_attn, preferred_element_type=jnp.float32)
    d_context = jnp.dot(d_attn, out_back.T, preferred_element_type=jnp.float32).astype(jnp.bfloat16)
    d_queries, d_keys, d_values = lax.map(
        attend_back,
        (queries, keys_part, values_part, seg_blocks, log_total, split_heads(d_context)),
    )
    d_projected = jnp.stack(
        [
            d_queries.reshape(row_count, head_width),
            d_keys.reshape(row_count, head_width),
            d_values.reshape(row_count, head_width),
        ],
        axis=1,
    ).astype(jnp.bfloat16)
    qkv_weight_grad = jnp.einsum(
        "nd,nce->dce", normed, d_projected, preferred_element_type=jnp.float32
    )
    d_normed = back_sum(
        jnp.einsum("nce,dce->nd", d_projected, qkv_back, preferred_element_type=jnp.float32)
    )
    d_rows_norm, d_gain_one, d_bias_one = norm_back(
        flat_rows, gain_again[0], bias_again[0], d_normed
    )
    input_grad = (d_residual + d_rows_norm).reshape(sequences, slot_count, model_width)
    gain_grad = jnp.stack([d_gain_one, d_gain_two])
    bias_grad = jnp.stack(
        [d_bias_one, jnp.sum(d_residual, axis=0), d_bias_two, jnp.sum(cot_float, axis=0)]
    )
    half_width = model_width // 2
    lower_features = input_grad[:, :, :half_width]
    upper_features = input_grad[:, :, half_width:]
    hand_step = 1
    on_query = branch == query_branch
    query_only = on_query.astype(jnp.float32)
    shares = (
        lax.psum_scatter(
            qkv_weight_grad * query_only, ("branch", "dp"), scatter_dimension=0, tiled=True
        ),
        lax.psum_scatter(
            out_weight_grad * query_only, ("branch", "dp"), scatter_dimension=1, tiled=True
        ),
        lax.psum_scatter(
            up_weight_grad * query_only, ("branch", "dp"), scatter_dimension=0, tiled=True
        ),
        lax.psum_scatter(
            down_weight_grad * query_only, ("branch", "dp"), scatter_dimension=1, tiled=True
        ),
        lax.psum_scatter(gain_grad * query_only, ("branch", "dp"), scatter_dimension=1, tiled=True),
        lax.psum_scatter(bias_grad * query_only, ("branch", "dp"), scatter_dimension=1, tiled=True),
    )
    moved_input = shifted(upper_features.astype(jnp.bfloat16), "branch", hand_step).astype(
        upper_features.dtype
    )
    crop_share = jnp.where(on_query, lower_features, moved_input)
    return (encoded, crop_share, shares[0], shares[1], shares[2], shares[3], shares[4], shares[5])


def solution(mesh):
    placed = (
        P("branch", "dp", None, None),
        P(None, "dp", None),
        P("dp", None, None),
        P("branch", "dp", None, "tensor"),
        P("branch", "tensor", "dp"),
        P("branch", "dp", "tensor"),
        P("branch", "tensor", "dp"),
        P("branch", None, "dp"),
        P("branch", None, "dp"),
    )
    return jax.shard_map(
        on_device,
        mesh=mesh,
        in_specs=placed,
        out_specs=(
            P("branch", "dp", None, None),
            P("dp", None, "branch"),
            P(("branch", "dp"), None, "tensor"),
            P("tensor", ("branch", "dp")),
            P(("branch", "dp"), "tensor"),
            P("tensor", ("branch", "dp")),
            P(None, ("branch", "dp")),
            P(None, ("branch", "dp")),
        ),
        check_vma=False,
    )
```

profile of v0, /device:TPU:0, one launch (start us, length us, event | category | flops | bytes accessed | tf_op | source)
XLA Modules:
  0.0 746.1 jit_solution(10382168555793994549)
XLA Ops:
  8.6 32.1 %all-gather = bf16[1,2,384]{1,0,2:T(2,128)(2,1)S(1)} all-gather(bf16[1,2,48]{1,0,2:T(2,128)(2,1)S(1)} %copy.100), channel_id=2, replica_groups=mesh['branch'=2,'dp'=8,'tensor'=2] {'dp'}, dimensions={2}, use_global_device_ids=true | all-gather | bytes 1728 | tf_op jit(solution)/shard_map/all_gather | solution.py:120
  41.6 30.6 %all-gather.1 = bf16[1,4,384]{1,0,2:T(2,128)(2,1)S(1)} all-gather(bf16[1,4,48]{1,0,2:T(2,128)(2,1)S(1)} %copy.101), channel_id=3, replica_groups=mesh['branch'=2,'dp'=8,'tensor'=2] {'dp'}, dimensions={2}, use_global_device_ids=true | all-gather | bytes 3456 | tf_op jit(solution)/shard_map/all_gather | solution.py:121
  73.4 31.4 %all-gather.2 = bf16[1,384,3,192]{3,1,2,0:T(8,128)(2,1)S(1)} all-gather(bf16[1,48,3,192]{3,1,2,0:T(8,128)(2,1)S(1)} %convert_element_type.140), channel_id=4, replica_groups=mesh['branch'=2,'dp'=8,'tensor'=2] {'dp'}, dimensions={1}, use_global_device_ids=true | all-gather | bytes 497664 | tf_op jit(solution)/shard_map/all_gather | solution.py:116
  105.2 30.6 %all-gather.3 = bf16[1,192,384]{1,2,0:T(8,128)(2,1)S(1)} all-gather(bf16[1,192,48]{1,2,0:T(8,128)(2,1)S(1)} %convert_element_type.143), channel_id=5, replica_groups=mesh['branch'=2,'dp'=8,'tensor'=2] {'dp'}, dimensions={2}, use_global_device_ids=true | all-gather | bytes 165888 | tf_op jit(solution)/shard_map/all_gather | solution.py:117
  137.6 5.6 slice_reduce_fusion
  149.3 3.2 reshape_squeeze.10
  160.2 19.6 %while.26 = (s32[]{:T(128)}, bf16[4,2,256,6,32]{2,1,0,4,3:T(2,128)(2,1)}, f32[4,2,6,256,1]{3,2,1,4,0:T(8,128)}, bf16[4,2,256,6,32]{2,4,3,1,0:T(8,128)(2,1)}, s32...) while((s32[]{:T(128)}, ...), condition=%wide.region_5.6_spmd, body=%wide.region_2.5_spmd.sunk | while | flops 110326784 | bytes 11252313 | solution.py:141
  179.8 3.2 reshape.167
  183.0 3.1 convolution_convert_fusion.2
  187.1 33.5 %all-gather.4 = bf16[1,384,768]{2,1,0:T(8,128)(2,1)} all-gather(bf16[1,48,768]{2,1,0:T(8,128)(2,1)S(1)} %convert_element_type.148), channel_id=6, replica_groups=mesh['branch'=2,'dp'=8,'tensor'=2] {'dp'}, dimensions={1}, use_global_device_ids=true | all-gather | bytes 663552 | tf_op jit(solution)/shard_map/all_gather | solution.py:118
  220.6 33.3 %all-gather.5 = bf16[1,768,384]{1,2,0:T(8,128)(2,1)} all-gather(bf16[1,768,48]{1,2,0:T(8,128)(2,1)S(1)} %convert_element_type.151), channel_id=7, replica_groups=mesh['branch'=2,'dp'=8,'tensor'=2] {'dp'}, dimensions={2}, use_global_device_ids=true | all-gather | bytes 663552 | tf_op jit(solution)/shard_map/all_gather | solution.py:119
  257.1 16.7 %multiply_convert_fusion.1 = (bf16[2048,768]{1,0:T(8,128)(2,1)}, f32[2048,768]{1,0:T(8,128)S(1)}, f32[2048,768]{1,0:T(8,128)S(1)}) fusion(bf16[1,384,768]{2,1,0:T(8,128)(2,1)S(1)} %copy-done.22, f32[2048,384]{1,0:T(8,128)S(1)} %get-tuple-element.247, f32[384]{0:T(512)S(1)} %get-tuple-element.199, f32[384]{0:T(512)S(1)} %get-tuple-element.202, ...), kind=kOutput, calls=%fused_computation.60 | convolution fusion | flops 1313341440 | bytes 19475456 | tf_op jit(solution)/shard_map/dot_general | solution.py:146
  273.8 3.2 add_convert_fusion
  278.6 3.0 convolution_convert_fusion
  281.7 5.0 convolution_convert_fusion.1
  286.7 48.0 %all-reduce.10.cloned.1.call-done = bf16[2048,384]{1,0:T(8,128)(2,1)} async-done(((bf16[2048,384]{1,0:T(8,128)(2,1)}), bf16[2048,384]{1,0:T(8,128)(2,1)}) %all-reduce.10.cloned.1.call-update) | async-done | bytes 1572880 | tf_op jit(solution)/shard_map/psum | solution.py:48
  334.7 3.2 convert_reduce_fusion.1
  345.0 3.3 reshape.170
  348.3 35.7 %while.27 = (s32[]{:T(128)}, bf16[4,2,256,6,32]{2,4,3,1,0:T(8,128)(2,1)}, bf16[4,2,256,6,32]{2,4,3,1,0:T(8,128)(2,1)}, bf16[4,2,256,6,32]{2,4,3,1,0:T(8,128)(2,1...) while((s32[]{:T(128)}, ...), condition=%wide.region_15.16_spmd, body=%wide.region_13.15_spmd.sunk | while | flops 259060736 | bytes 39463144 | solution.py:178
  397.5 4.8 bitcast_convert_fusion
  402.4 5.4 convolution_multiply_fusion.3
  407.9 5.3 convolution_multiply_fusion.2
  413.3 3.4 convolution_multiply_fusion.4
  416.8 71.6 %all-reduce.12.cloned.1.call-done = (bf16[2048,384]{1,0:T(8,128)(2,1)}, bf16[2048,384]{1,0:T(8,128)(2,1)}) async-done(((bf16[2048,384]{1,0:T(8,128)(2,1)}, bf16[2048,384]{1,0:T(8,128)(2,1)}), (bf16[2048,384]{1,0:T(8,128)(2,1)}, bf16[2048,384]{1,0:T(8,128)(2,1)})) %all-reduce.12.cloned.1.call-update) | async-done | bytes 3145744 | tf_op jit(solution)/shard_map/psum | solution.py:44
  488.4 2.8 convert_reduce_fusion
  493.1 5.3 add_add_fusion.2
  507.6 3.1 slice.62
  512.6 34.1 %all-reduce.2 = (f32[2,384]{1,0:T(2,128)S(1)}, f32[4,384]{1,0:T(4,128)S(1)}) all-reduce(f32[2,384]{1,0:T(2,128)S(1)} %maximum_multiply_fusion.1, f32[4,384]{1,0:T(4,128)S(1)} %maximum_multiply_fusion), channel_id=12, replica_groups=mesh['branch'=2,'dp'=8,'tensor'=2] {'branch','dp'}, use_global_device_ids=true, to_apply=%region_25.26.clone | all-reduce | flops 2304 | bytes 18432
  549.3 5.0 reduce-scatter.11.cloned.1.call-done
  554.3 61.5 %reduce-scatter.13.cloned.1.call-done = f32[768,24]{0,1:T(8,128)} async-done(((f32[768,384]{0,1:T(8,128)}), f32[768,24]{0,1:T(8,128)}) %reduce-scatter.13.cloned.1.call-update) | async-done | bytes 73744 | tf_op jit(solution)/shard_map/reduce_scatter | solution.py:220
  615.8 59.0 %reduce-scatter.9.cloned.1.call-done = f32[192,24]{0,1:T(8,128)} async-done(((f32[192,384]{0,1:T(8,128)}), f32[192,24]{0,1:T(8,128)}) %reduce-scatter.9.cloned.1.call-update) | async-done | bytes 18448 | tf_op jit(solution)/shard_map/reduce_scatter | solution.py:214
  674.8 61.4 %reduce-scatter.7.cloned.1.call-done = f32[24,3,192]{2,0,1:T(8,128)} async-done(((f32[384,3,192]{2,0,1:T(8,128)}), f32[24,3,192]{2,0,1:T(8,128)}) %reduce-scatter.7.cloned.1.call-update) | async-done | bytes 55312 | tf_op jit(solution)/shard_map/reduce_scatter | solution.py:211
  (261 shorter events, 118.1 us)
Async XLA Ops:
  7.2 98.0 %copy-start = (s32[2,8,256]{2,1,0:T(8,128)S(1)}, s32[2,8,256]{2,1,0:T(8,128)}, u32[]{:S(2)}) copy-start(s32[2,8,256]{2,1,0:T(8,128)} %param.14) | copy-start | bytes 49156
  7.2 98.0 %copy-start.33 = (f32[1,192,48]{1,2,0:T(8,128)S(1)}, f32[1,192,48]{1,2,0:T(8,128)}, u32[]{:S(2)}) copy-start(f32[1,192,48]{1,2,0:T(8,128)} %param.17) | copy-start | bytes 110596
  7.2 246.7 %all-reduce.8.cloned.1.call-start = ((), (), s32[]{:S(2)}) async-start(), calls=%async_computation.4 | async-start | bytes 3145728 | tf_op jit(solution)/shard_map/psum | solution.py:44
  7.2 135.9 %collective-permute-start = (bf16[1,8,256,384]{3,2,1,0:T(8,128)(2,1)}, bf16[1,8,256,384]{3,2,1,0:T(8,128)(2,1)S(1)}, u32[]{:S(2)}, u32[]{:S(2)}) collective-permute-start(bf16[1,8,256,384]{3,2,1,0:T(8,128)(2,1)} %param.13), channel_id=1, source_target_pairs={{0,16},{16,0},{1,17},{17,1},{2,18},{18,2},{3,19},{19,3},{4,20},{20... | collective-permute-start | bytes 4718600 | tf_op jit(solution)/shard_map/ppermute | solution.py:23
  104.8 41.5 %copy-start.16 = (bf16[1,384,3,192]{3,1,2,0:T(8,128)(2,1)}, bf16[1,384,3,192]{3,1,2,0:T(8,128)(2,1)S(1)}, u32[]{:S(2)}) copy-start(bf16[1,384,3,192]{3,1,2,0:T(8,128)(2,1)S(1)} %all-gather.2) | copy-start | bytes 1327108
  137.5 8.8 %copy-start.31 = (f32[384]{0:T(512)}, f32[384]{0:T(512)S(1)}, u32[]{:S(2)}) copy-start(f32[384]{0:T(512)S(1)} %get-tuple-element.203) | copy-start | bytes 4612
  179.8 6.3 copy-start.26
  186.1 148.7 %all-reduce.10.cloned.1.call-start = ((), (), s32[]{:S(2)}) async-start(), calls=%async_computation.5 | async-start | bytes 3145728 | tf_op jit(solution)/shard_map/psum | solution.py:48
  257.0 16.8 %copy-start.4 = (f32[2048,384]{1,0:T(8,128)}, f32[2048,384]{1,0:T(8,128)S(1)}, u32[]{:S(2)}) copy-start(f32[2048,384]{1,0:T(8,128)S(1)} %get-tuple-element.247) | copy-start | bytes 9437188
  257.1 16.8 %copy-start.13 = (bf16[8,256,384]{2,1,0:T(8,128)(2,1)S(1)}, bf16[8,256,384]{2,1,0:T(8,128)(2,1)}, u32[]{:S(2)}) copy-start(bf16[8,256,384]{2,1,0:T(8,128)(2,1)} %param.15) | copy-start | bytes 4718596
  257.1 16.8 %copy-start.21 = (bf16[1,768,384]{1,2,0:T(8,128)(2,1)S(1)}, bf16[1,768,384]{1,2,0:T(8,128)(2,1)}, u32[]{:S(2)}) copy-start(bf16[1,768,384]{1,2,0:T(8,128)(2,1)} %all-gather.5) | copy-start | bytes 1769476
  281.7 206.8 %all-reduce.12.cloned.1.call-start = ((), (), s32[]{:S(2)}) async-start(), calls=%async_computation.10 | async-start | bytes 6291456 | tf_op jit(solution)/shard_map/psum | solution.py:44
  334.7 3.8 copy-start.6
  402.3 152.0 %reduce-scatter.11.cloned.1.call-start = ((), (), s32[]{:S(2)}) async-start(), calls=%async_computation.8 | async-start | bytes 1253376 | tf_op jit(solution)/shard_map/reduce_scatter | solution.py:217
  407.8 5.5 copy-start.12
  407.8 208.0 %reduce-scatter.13.cloned.1.call-start = ((), (), s32[]{:S(2)}) async-start(), calls=%async_computation.9 | async-start | bytes 1253376 | tf_op jit(solution)/shard_map/reduce_scatter | solution.py:220
  413.2 75.2 %copy-start.25 = (f32[1,2,8,128]{3,1,2,0:T(2,128)S(1)}, f32[1,2,8,128]{3,1,2,0:T(2,128)}, u32[]{:S(2)}) copy-start(f32[1,2,8,128]{3,1,2,0:T(2,128)} %copy-done.24) | copy-start | bytes 24580
  413.2 75.2 %copy-start.32 = (f32[384]{0:T(512)S(1)}, f32[384]{0:T(512)}, u32[]{:S(2)}) copy-start(f32[384]{0:T(512)} %copy-done.31) | copy-start | bytes 4612
  413.2 78.1 %copy-start.30 = (f32[1,2,8,128]{3,1,2,0:T(2,128)S(1)}, f32[1,2,8,128]{3,1,2,0:T(2,128)}, u32[]{:S(2)}) copy-start(f32[1,2,8,128]{3,1,2,0:T(2,128)} %copy-done.29) | copy-start | bytes 24580
  413.2 78.1 %copy-start.28 = (f32[2048]{0:T(1024)S(1)}, f32[2048]{0:T(1024)}, u32[]{:S(2)}) copy-start(f32[2048]{0:T(1024)} %copy-done.27) | copy-start | bytes 24580
  413.2 261.5 %reduce-scatter.9.cloned.1.call-start = ((), (), s32[]{:S(2)}) async-start(), calls=%async_computation.7 | async-start | bytes 417792 | tf_op jit(solution)/shard_map/reduce_scatter | solution.py:214
  416.7 319.4 %reduce-scatter.7.cloned.1.call-start = ((), (), s32[]{:S(2)}) async-start(), calls=%async_computation.6 | async-start | bytes 1253376 | tf_op jit(solution)/shard_map/reduce_scatter | solution.py:211
  488.4 4.6 copy-start.3
  488.4 4.6 copy-start.9
  488.4 4.6 copy-start.34
  493.1 5.3 copy-start.11
  493.1 5.3 copy-start.23
  498.4 50.9 %collective-permute-start.1 = (bf16[1,8,256,384]{3,2,1,0:T(8,128)(2,1)}, bf16[1,8,256,384]{3,2,1,0:T(8,128)(2,1)}, u32[]{:S(2)}, u32[]{:S(2)}) collective-permute-start(bf16[1,8,256,384]{3,2,1,0:T(8,128)(2,1)} %bitcast.26), channel_id=1, source_target_pairs={{0,16},{16,0},{1,17},{17,1},{2,18},{18,2},{3,19},{19,3},{4,20},{20... | collective-permute-start | bytes 4718600 | tf_op jit(solution)/shard_map/ppermute | solution.py:23
  500.8 5.1 copy-start.15
  500.8 5.4 copy-start.35
  503.5 44.5 %collective-permute-start.2 = (bf16[8,256,192]{1,2,0:T(8,128)(2,1)S(1)}, bf16[8,256,192]{1,2,0:T(8,128)(2,1)S(1)}, u32[]{:S(2)}, u32[]{:S(2)}) collective-permute-start(bf16[8,256,192]{1,2,0:T(8,128)(2,1)S(1)} %copy.131), channel_id=1, source_target_pairs={{0,16},{1,17},{2,18},{3,19},{4,20},{5,21},{6,22},{7,23},{8,24},{9,... | collective-permute-start | bytes 2359304 | tf_op jit(solution)/shard_map/ppermute | solution.py:29
  547.4 191.5 %copy-start.1 = (s32[2,8,256]{2,1,0:T(8,128)S(1)}, s32[2,8,256]{2,1,0:T(8,128)}, u32[]{:S(2)}) copy-start(s32[2,8,256]{2,1,0:T(8,128)} %param.14) | copy-start | bytes 49156
  (27 other events, 43.2 us)
Sparse Core Ops, SparseCore 0:
  186.2 52.6 all-reduce.7
  281.8 52.9 all-reduce.9
  402.4 85.9 all-reduce.11
  492.9 61.3 reduce-scatter.10
  558.8 57.0 reduce-scatter.12
  620.1 54.5 reduce-scatter.8
  679.0 57.1 reduce-scatter.6
where the time goes:
time: 754 us; the launch traced here: 746 us
  waiting for transfers between devices  307 us (41%)
  blocking collectives  226 us (30%)
  matrix products  84.8 us (11%)
  local copies, waits for them, and re-layouts  73.1 us (10%)
  other arithmetic  36.4 us (5%)
  between operations  15.9 us (2%)
    psum x2, waiting for transfers between devices, head_sum(): lax.psum(partial_rows.astype(jnp.bfloat16), 'tensor').astype(jnp.float32)  71.6 us
    reduce_scatter x1, waiting for transfers between devices, on_device(): lax.psum_scatter(down_weight_grad * query_only, ('branch', 'dp'), scatter...  61.5 us
    reduce_scatter x1, waiting for transfers between devices, on_device(): lax.psum_scatter(qkv_weight_grad * query_only, ('branch', 'dp'), scatter_...  61.4 us
    reduce_scatter x1, waiting for transfers between devices, on_device(): lax.psum_scatter(out_weight_grad * query_only, ('branch', 'dp'), scatter_...  59 us
    psum x1, waiting for transfers between devices, back_sum(): lax.psum(partial_rows.astype(jnp.bfloat16), 'tensor').astype(jnp.float32)  48 us
    unnamed x1, blocking collectives  34.1 us
    all_gather x1, blocking collectives, on_device(): lax.all_gather(own_shards[2], 'dp', axis=0, tiled=True)  33.5 us
    all_gather x1, blocking collectives, on_device(): lax.all_gather(own_shards[3], 'dp', axis=1, tiled=True)  33.3 us
  transfers between devices with their start and end apart: 10, of which 6 were waited for; matrix products, arithmetic and copies ran while one was open for 7% of the time, Pallas kernels for 0%

commit v1 on v0

v1 whole, which is shorter than its diff:
```python
import functools
import math

import jax
import jax.numpy as jnp
from jax import lax
from jax.experimental import pallas as pl
from jax.experimental.pallas import tpu as pltpu
from jax.sharding import PartitionSpec as P

HD = 32
EPSILON = 1e-06
MASKED_SCORE = -1e30
LOG2E = 1.4426950408889634
BF16 = jnp.bfloat16
F32 = jnp.float32
VMEM_LIMIT = 48 * 1024 * 1024


def nn(left, right):
    return lax.dot_general(left, right, (((1,), (0,)), ((), ())), preferred_element_type=F32)


def nt(left, right):
    return lax.dot_general(left, right, (((1,), (1,)), ((), ())), preferred_element_type=F32)


def tn(left, right):
    return lax.dot_general(left, right, (((0,), (0,)), ((), ())), preferred_element_type=F32)


def gelu_parts(v):
    a = jnp.abs(v)
    t = 1.0 / (1.0 + (0.3275911 / math.sqrt(2.0)) * a)
    bell = jnp.exp2(v * v * (-0.5 * LOG2E))
    poly = t * (
        0.5 * 0.254829592
        + t * (0.5 * -0.284496736 + t * (0.5 * 1.421413741 + t * (0.5 * -1.453152027 + t * (0.5 * 1.061405429))))
    )
    tail = poly * bell
    return jnp.where(v < 0, tail, 1.0 - tail), bell


def norm_cols(values, gain, shift):
    centred = values - jnp.mean(values, axis=0, keepdims=True)
    spread = jnp.mean(centred * centred, axis=0, keepdims=True)
    rstd = lax.rsqrt(spread + EPSILON)
    hat = centred * rstd
    return hat, rstd, hat * gain + shift


def norm_cols_back(upstream, hat, rstd, gain):
    t = upstream * gain
    return rstd * (t - jnp.mean(t, axis=0, keepdims=True) - hat * jnp.mean(t * hat, axis=0, keepdims=True))


def columns_of(vec_ref, scratch):
    scratch[...] = jnp.zeros_like(scratch)
    scratch[0:8, :] = vec_ref[...]
    return scratch[...].T


def attend(x_ref, seg_ref, w1_ref, cols, q_ref, k_ref, v_ref, bias_ref, ctx_ref, pb_ref, inv_ref):
    tensors, width = w1_ref.shape[1], w1_ref.shape[2]
    group = width // tensors
    heads_g = group // HD
    nseq, slots = seg_ref.shape
    x_t = x_ref[...].astype(F32).T
    hat, rstd, normed = norm_cols(x_t, cols[:, 0:1], cols[:, 2:3])
    normed_low = normed.astype(BF16)
    rows = x_t.shape[1]
    for t in range(tensors):
        qk = tn(w1_ref[0, t], normed_low).astype(BF16)
        q_ref[t * heads_g : (t + 1) * heads_g] = qk[:group].reshape(heads_g, HD, rows)
        k_ref[t * heads_g : (t + 1) * heads_g] = qk[group:].reshape(heads_g, HD, rows)
        vo = tn(w1_ref[1, t], normed_low).astype(BF16)
        v_ref[t * heads_g : (t + 1) * heads_g, 0:HD] = vo[:group].reshape(heads_g, HD, rows)
    v_ref[:, HD:, :] = jnp.ones((v_ref.shape[0], v_ref.shape[1] - HD, rows), BF16)
    for s in range(nseq):
        across = jnp.broadcast_to(seg_ref[s : s + 1, :].astype(F32), (slots, slots))
        bias_ref[s] = jnp.where(across == across.T, 0.0, MASKED_SCORE)
    heads = tensors * heads_g

    def one_head(h, carry):
        for s in range(nseq):
            part = slice(s * slots, (s + 1) * slots)
            scores = tn(k_ref[h, :, part], q_ref[h, :, part]) + bias_ref[s]
            top = jnp.max(scores, axis=0, keepdims=True)
            weights = jnp.exp2((scores - top) * (HD**-0.5 * LOG2E)).astype(BF16)
            if pb_ref is not None:
                pb_ref[h, s] = weights
            both = nn(v_ref[h, :, part], weights)
            inv = 1.0 / both[HD : HD + 1]
            if inv_ref is not None:
                inv_ref[h, :, part] = jnp.broadcast_to(inv, (8, slots))
            ctx_ref[h // heads_g, heads_g + h % heads_g, :, part] = (both[:HD] * inv).astype(BF16)
        return carry

    ctx_ref[:, :heads_g] = jnp.zeros((tensors, heads_g, HD, rows), BF16)
    lax.fori_loop(0, heads, one_head, 0)
    attn = sum(nn(w1_ref[1, t], ctx_ref[t].reshape(width, rows)) for t in range(tensors))
    return x_t, hat, rstd, normed_low, attn


def query_attn_kernel(
    x_ref, seg_ref, w1_ref, vec_ref,
    res_ref, hat_ref, rstd_ref, normed_ref, q_ref, k_ref, v_ref, pb_ref, inv_ref, ctx_ref, cols_ref,
    bias_ref, vec_pad,
):
    cols = columns_of(vec_ref, vec_pad)
    cols_ref[...] = cols
    x_t, hat, rstd, normed, attn = attend(
        x_ref, seg_ref, w1_ref, cols, q_ref, k_ref, v_ref, bias_ref, ctx_ref, pb_ref, inv_ref
    )
    hat_ref[...] = hat
    rstd_ref[...] = jnp.broadcast_to(rstd, rstd_ref.shape)
    normed_ref[...] = normed
    res_ref[...] = x_t + attn + cols[:, 3:4]


def momentum_kernel(
    x_ref, seg_ref, w1_ref, w2_ref, vec_ref, out_ref, q_ref, k_ref, v_ref, ctx_ref, bias_ref, vec_pad, acc_ref
):
    cols = columns_of(vec_ref, vec_pad)
    x_t, _, _, _, attn = attend(x_ref, seg_ref, w1_ref, cols, q_ref, k_ref, v_ref, bias_ref, ctx_ref, None, None)
    res = x_t + attn + cols[:, 3:4]
    _, _, normed = norm_cols(res, cols[:, 1:2], cols[:, 4:5])
    rows_low = normed.T.astype(BF16)
    acc_ref[...] = res + cols[:, 5:6]
    tensors, units = w2_ref.shape[1], w2_ref.shape[3]
    chunk = 256
    parts = units // chunk

    def step(i, carry):
        t, c = i // parts, pl.ds(pl.multiple_of((i % parts) * chunk, chunk), chunk)
        pre = nn(rows_low, w2_ref[0, t, :, c])
        half, _ = gelu_parts(pre)
        acc_ref[...] += nt(w2_ref[1, t, :, c], (pre * half).astype(BF16))
        return carry

    lax.fori_loop(0, tensors * parts, step, 0)
    out_ref[...] = acc_ref[...].T.astype(BF16)


def query_mlp_kernel(
    b_ref, res_ref, cot_ref, w2_ref, cols_ref,
    out_ref, keep_ref, send_ref, dres_ref, vgrad_ref,
    acc_ref, dn_ref, n2t_ref, gt_ref,
):
    b = b_ref[0]
    cols = cols_ref[...]
    res = res_ref[...]
    hat, rstd, normed = norm_cols(res, cols[:, 1:2], cols[:, 4:5])
    n2t_ref[...] = normed.astype(BF16)
    rows_low = normed.T.astype(BF16)
    cot = cot_ref[...]
    cot_t = cot.astype(F32).T
    gt_ref[...] = cot_t.astype(BF16)
    acc_ref[...] = res + cols[:, 5:6]
    dn_ref[...] = jnp.zeros_like(dn_ref)
    tensors, width, units = w2_ref.shape[1], w2_ref.shape[2], w2_ref.shape[3]
    chunk = 256
    parts = units // chunk
    half_rows = width // 2

    def step(i, carry):
        t, off = i // parts, pl.multiple_of((i % parts) * chunk, chunk)
        c = pl.ds(off, chunk)
        up, down = w2_ref[0, t, :, c], w2_ref[1, t, :, c]
        pre = nn(rows_low, up)
        d_hidden = nn(cot, down)
        half, bell = gelu_parts(pre)
        hidden = (pre * half).astype(BF16)
        d_pre = (d_hidden * (half + pre * bell * (1.0 / math.sqrt(2.0 * math.pi)))).astype(BF16)
        acc_ref[...] += nt(down, hidden)
        dn_ref[...] += nt(up, d_pre)
        for ref, which in ((keep_ref, b), (send_ref, 1 - b)):
            rows = pl.ds(pl.multiple_of(which * half_rows, 16), half_rows)
            ref[t, :, c] = nn(n2t_ref[rows, :], d_pre).astype(BF16)
            ref[t, :, pl.ds(pl.multiple_of(units + off, chunk), chunk)] = nn(gt_ref[rows, :], hidden).astype(BF16)
        return carry

    lax.fori_loop(0, tensors * parts, step, 0)
    out_ref[...] = acc_ref[...].T.astype(BF16)
    d_n2 = dn_ref[...]
    d_res = cot_t + norm_cols_back(d_n2, hat, rstd, cols[:, 1:2])
    dres_ref[...] = d_res
    lane = lax.broadcasted_iota(jnp.int32, vgrad_ref.shape, 1)
    total = jnp.zeros(vgrad_ref.shape, F32)
    for j, term in ((1, d_n2 * hat), (3, d_res), (4, d_n2), (5, cot_t)):
        total = total + jnp.where(lane == 64 + j, jnp.sum(term, axis=1, keepdims=True), 0.0)
    vgrad_ref[...] = total


def query_back_kernel(
    b_ref, dres_ref, hat_ref, rstd_ref, normed_ref, q_ref, k_ref, v_ref, pb_ref, inv_ref, ctx_ref, cols_ref, w1_ref,
    vgrad_ref,
    crop_keep_ref, crop_send_ref, keep_ref, send_ref,
    dctx_ref, dproj_ref, dattn_ref, vg_ref, crop_ref,
):
    b = b_ref[0]
    tensors, width = w1_ref.shape[1], w1_ref.shape[2]
    group = width // tensors
    heads_g = group // HD
    heads, nseq, slots = pb_ref.shape[0], pb_ref.shape[1], pb_ref.shape[2]
    rows = nseq * slots
    d_attn = dres_ref[...].astype(BF16)
    dattn_ref[...] = d_attn
    for t in range(tensors):
        vo = tn(w1_ref[1, t], d_attn).astype(BF16)
        dctx_ref[t * heads_g : (t + 1) * heads_g] = vo[group:].reshape(heads_g, HD, rows)
    dproj_ref[:, 3 * heads_g :] = jnp.zeros((tensors, heads_g, HD, rows), BF16)

    def one_head(h, carry):
        t, hh = h // heads_g, h % heads_g
        for s in range(nseq):
            part = slice(s * slots, (s + 1) * slots)
            low_ctx = dctx_ref[h, :, part].astype(F32) * inv_ref[h, 0:1, part]
            delta = jnp.sum(low_ctx * ctx_ref[t, heads_g + hh, :, part].astype(F32), axis=0, keepdims=True)
            low_ctx = low_ctx.astype(BF16)
            weights = pb_ref[h, s]
            d_probs = tn(v_ref[h, 0:HD, part], low_ctx)
            d_scores = (weights.astype(F32) * (d_probs - delta)).astype(BF16)
            scale = HD**-0.5
            dproj_ref[t, hh, :, part] = (nn(k_ref[h, :, part], d_scores) * scale).astype(BF16)
            dproj_ref[t, heads_g + hh, :, part] = (nt(q_ref[h, :, part], d_scores) * scale).astype(BF16)
            dproj_ref[t, 2 * heads_g + hh, :, part] = nt(low_ctx, weights).astype(BF16)
        return carry

    lax.fori_loop(0, heads, one_head, 0)
    d_normed = jnp.zeros((width, rows), F32)
    for t in range(tensors):
        d_t = dproj_ref[t].reshape(4 * group, rows)
        d_normed += nn(w1_ref[0, t], d_t[: 2 * group]) + nn(w1_ref[1, t], d_t[2 * group :])
    hat = hat_ref[...]
    cols = cols_ref[...]
    crop_ref[...] = dres_ref[...] + norm_cols_back(d_normed, hat, rstd_ref[0:1, :], cols[:, 0:1])
    lane = lax.broadcasted_iota(jnp.int32, vgrad_ref.shape, 1)
    total = vgrad_ref[...]
    for j, term in ((0, d_normed * hat), (2, d_normed)):
        total = total + jnp.where(lane == 64 + j, jnp.sum(term, axis=1, keepdims=True), 0.0)
    vg_ref[...] = total
    half_rows = width // 2
    for ref, which in ((keep_ref, b), (send_ref, 1 - b)):
        part = pl.ds(pl.multiple_of(which * half_rows, 16), half_rows)
        left, right = normed_ref[part, :], dattn_ref[part, :]
        for t in range(tensors):
            d_t = dproj_ref[t].reshape(4 * group, rows)
            grads = nt(left, d_t[: 3 * group + 64])
            tile = (3 * group) // 128 * 128
            ref[t, :, 0:tile] = grads[:, :tile].astype(BF16)
            ref[t, :, tile : tile + 128] = (grads[:, tile : tile + 128] + vg_ref[part, :]).astype(BF16)
            ref[t, :, tile + 128 : tile + 128 + group] = nt(
                right, ctx_ref[t, heads_g:].reshape(group, rows)
            ).astype(BF16)
            ref[t, :, tile + 128 + group :] = jnp.zeros((half_rows, 64), BF16)
    mine = crop_ref[pl.ds(pl.multiple_of(b * half_rows, 16), half_rows), :]
    other = crop_ref[pl.ds(pl.multiple_of((1 - b) * half_rows, 16), half_rows), :]
    crop_keep_ref[...] = mine.T
    crop_send_ref[...] = other.T.astype(BF16)


def call(kernel, out_shapes, scratch, args, smem=0, flops=0, nbytes=0, trans=0):
    vmem = pl.BlockSpec(memory_space=pltpu.VMEM)
    return pl.pallas_call(
        kernel,
        out_shape=[jax.ShapeDtypeStruct(s, d) for s, d in out_shapes],
        in_specs=[pl.BlockSpec(memory_space=pltpu.SMEM)] * smem + [vmem] * (len(args) - smem),
        out_specs=[vmem] * len(out_shapes),
        scratch_shapes=[pltpu.VMEM(s, d) for s, d in scratch],
        compiler_params=pltpu.CompilerParams(vmem_limit_bytes=VMEM_LIMIT),
        cost_estimate=pl.CostEstimate(flops=flops, bytes_accessed=nbytes, transcendentals=trans),
    )(*args)


SPAN = ("dp", "tensor")


def swap_cores(block):
    return lax.ppermute(block, "branch", [(0, 1), (1, 0)])


def exchange(block, dp_mask, t_mask):
    dp, tensors = lax.axis_size("dp"), lax.axis_size("tensor")
    pairs = [
        (i * tensors + t, (i ^ dp_mask) * tensors + (t ^ t_mask)) for i in range(dp) for t in range(tensors)
    ]
    return lax.ppermute(block, SPAN, pairs)


def after(value, *deps):
    return lax.optimization_barrier((value, *deps))[0]


def dp_groups():
    bits = lax.axis_size("dp").bit_length() - 1
    groups, high = [], bits
    while high >= 2:
        high -= 2
        groups.append((high, 4))
    last = (0, 2) if high == 1 else None
    return groups, last


def put(whole, block, index):
    return lax.dynamic_update_slice(whole, block, index)


def gather(block):
    groups, last = dp_groups()
    me, t = lax.axis_index("dp"), lax.axis_index("tensor")
    tensors = lax.axis_size("tensor")
    for number, (shift, size) in enumerate(groups):
        lead, tail = block.shape[:number], block.shape[number:]
        whole = jnp.zeros(lead + (size,) + tail, block.dtype)
        mine = (me >> shift) & (size - 1)
        pieces = [(0, block)] + [(k, exchange(block, k << shift, 0)) for k in range(1, size)]
        for k, piece in pieces:
            whole = put(whole, jnp.expand_dims(piece, number), (0,) * number + (mine ^ k,) + (0,) * len(tail))
        block = whole
    lead, tail = block.shape[: len(groups)], block.shape[len(groups) :]
    size = last[1] if last else 1
    mine = me & (size - 1)
    whole = jnp.zeros((tensors,) + lead + (size,) + tail, block.dtype)
    for k in range(size):
        for u in range(tensors):
            piece = block if k == u == 0 else exchange(block, k, u)
            piece = jnp.expand_dims(jnp.expand_dims(piece, len(lead)), 0)
            whole = put(whole, piece, (t ^ u,) + (0,) * len(lead) + (mine ^ k,) + (0,) * len(tail))
    return whole.reshape((tensors, lax.axis_size("dp")) + tail)


def scatter_sum(block):
    groups, last = dp_groups()
    me, t = lax.axis_index("dp"), lax.axis_index("tensor")
    tensors = lax.axis_size("tensor")
    tail = block.shape[2:]
    size = last[1] if last else 1
    lead = tuple(g[1] for g in groups)
    block = block.reshape((tensors,) + lead + (size,) + tail)
    mine = me & (size - 1)

    def take(k, u):
        start = (t ^ u,) + (0,) * len(lead) + (mine ^ k,) + (0,) * len(tail)
        piece = lax.dynamic_slice(block, start, (1,) + lead + (1,) + tail)
        return piece.reshape(lead + tail)

    total = take(0, 0).astype(F32)
    for k in range(size):
        for u in range(tensors):
            if k or u:
                total = total + exchange(take(k, u), k, u).astype(F32)
    for number in reversed(range(len(groups))):
        shift, size = groups[number]
        mine = (me >> shift) & (size - 1)
        low = total.astype(BF16)

        def part(k, whole=low, number=number, mine=mine):
            return lax.dynamic_index_in_dim(whole, mine ^ k, number, keepdims=False)

        total = part(0, total).astype(F32)
        for k in range(1, size):
            total = total + exchange(part(k), k << shift, 0).astype(F32)
    return total


def on_device(
    crops, segment_ids, cotangent, qkv_weight, out_weight, up_weight, down_weight, gain_rows, biases
):
    branch, me, t = lax.axis_index("branch"), lax.axis_index("dp"), lax.axis_index("tensor")
    dp, tensors = lax.axis_size("dp"), lax.axis_size("tensor")
    on_query = branch == 0
    _, sequences, slots, width = crops.shape
    nseq = sequences // (2 * tensors)
    rows = nseq * slots
    shard = qkv_weight.shape[1]
    group = out_weight.shape[1]
    units = up_weight.shape[2]
    heads = tensors * group // HD
    heads_g = group // HD

    qkv = qkv_weight[0].astype(BF16)
    small = jnp.concatenate([gain_rows[0], biases[0]], axis=0).astype(BF16)
    vec_rows = put(jnp.zeros((8, width), BF16), small, (0, me * shard))
    half_0 = jnp.concatenate([jnp.concatenate([qkv[:, 0], qkv[:, 1]], axis=1), vec_rows], axis=0)
    half_1 = jnp.concatenate(
        [jnp.concatenate([qkv[:, 2], out_weight[0].T.astype(BF16)], axis=1), vec_rows], axis=0
    )
    mlp_0, mlp_1 = up_weight[0].astype(BF16), down_weight[0].T.astype(BF16)
    keep_1, send_1 = jnp.where(on_query, half_0, half_1), jnp.where(on_query, half_1, half_0)
    keep_2, send_2 = jnp.where(on_query, mlp_0, mlp_1), jnp.where(on_query, mlp_1, mlp_0)
    got_1 = swap_cores(send_1)
    got_2 = swap_cores(send_2)
    q_1, m_1 = jnp.where(on_query, keep_1, got_1), jnp.where(on_query, got_1, keep_1)
    q_2, m_2 = jnp.where(on_query, keep_2, got_2), jnp.where(on_query, got_2, keep_2)

    first = nseq * (2 * t + branch)
    other = nseq * (2 * t + 1 - branch)
    own_crops = lax.dynamic_slice(crops[0], (first, 0, 0), (nseq, slots, width)).reshape(rows, width)
    got_crops = swap_cores(
        lax.dynamic_slice(crops[0], (other, 0, 0), (nseq, slots, width)).reshape(rows, width)
    )
    x_query = jnp.where(on_query, got_crops, own_crops)
    x_momentum = jnp.where(on_query, own_crops, got_crops)
    seg = lax.dynamic_slice(segment_ids, (0, first, 0), (2, nseq, slots))
    cot = lax.dynamic_slice(cotangent, (first, 0, 0), (nseq, slots, width)).reshape(rows, width)

    def finish_1(block):
        whole = gather(block)
        vec = jnp.sum(whole[0, :, shard:].astype(F32), axis=0)
        own = whole[:, :, :shard].reshape(tensors, width, width)
        got = swap_cores(own)
        return jnp.stack([jnp.where(on_query, own, got), jnp.where(on_query, got, own)]), vec

    def finish_2(block):
        own = gather(block).reshape(tensors, width, units)
        got = swap_cores(own)
        return jnp.stack([jnp.where(on_query, own, got), jnp.where(on_query, got, own)])

    wq_1, vec_q = finish_1(q_1)
    wq_2 = finish_2(q_2)
    m_1, m_2 = after((m_1, m_2), wq_2)
    wm_1, vec_m = finish_1(m_1)
    wm_2 = finish_2(m_2)

    flop = 2 * rows * width
    (res, hat, rstd, normed, q_t, k_t, v_t, pb, inv, ctx, cols) = call(
        query_attn_kernel,
        [
            ((width, rows), F32),
            ((width, rows), F32),
            ((8, rows), F32),
            ((width, rows), BF16),
            ((heads, HD, rows), BF16),
            ((heads, HD, rows), BF16),
            ((heads, HD + 16, rows), BF16),
            ((heads, nseq, slots, slots), BF16),
            ((heads, 8, rows), F32),
            ((tensors, 2 * heads_g, HD, rows), BF16),
            ((width, 128), F32),
        ],
        [((nseq, slots, slots), F32), ((128, width), F32)],
        (x_query, seg[1], wq_1, vec_q),
        flops=flop * (4 * width + 4 * slots * 8),
        nbytes=20_000_000,
    )
    b_arr = branch.astype(jnp.int32).reshape(1)
    out_q, keep_g2, send_g2, d_res, vgrad = call(
        query_mlp_kernel,
        [
            ((rows, width), BF16),
            ((tensors, width // 2, 2 * units), BF16),
            ((tensors, width // 2, 2 * units), BF16),
            ((width, rows), F32),
            ((width, 128), F32),
        ],
        [((width, rows), F32), ((width, rows), F32), ((width, rows), BF16), ((width, rows), BF16)],
        (b_arr, res, cot, wq_2, cols),
        smem=1,
        flops=flop * 6 * units * tensors,
        nbytes=20_000_000,
    )
    crop_keep, crop_send, keep_g1, send_g1 = call(
        query_back_kernel,
        [
            ((rows, width // 2), F32),
            ((rows, width // 2), BF16),
            ((tensors, width // 2, 4 * group + 128), BF16),
            ((tensors, width // 2, 4 * group + 128), BF16),
        ],
        [
            ((heads, HD, rows), BF16),
            ((tensors, 4 * heads_g, HD, rows), BF16),
            ((width, rows), BF16),
            ((width, 128), F32),
            ((width, rows), F32),
        ],
        (b_arr, d_res, hat, rstd, normed, q_t, k_t, v_t, pb, inv, ctx, cols, wq_1, vgrad),
        smem=1,
        flops=flop * (8 * width + 10 * slots * 8),
        nbytes=20_000_000,
    )
    (out_m,) = call(
        momentum_kernel,
        [((rows, width), BF16)],
        [
            ((heads, HD, rows), BF16),
            ((heads, HD, rows), BF16),
            ((heads, HD + 16, rows), BF16),
            ((tensors, 2 * heads_g, HD, rows), BF16),
            ((nseq, slots, slots), F32),
            ((128, width), F32),
            ((width, rows), F32),
        ],
        (x_momentum, seg[0], wm_1, wm_2, vec_m),
        flops=flop * (4 * width + 2 * units * tensors + 4 * slots * 8),
        nbytes=20_000_000,
    )

    def shares(keep, send):
        both = (keep.astype(F32) + swap_cores(send).astype(F32)).astype(BF16)
        return scatter_sum(both.reshape(tensors, dp, width // (2 * dp), both.shape[-1]))

    mlp_share = shares(keep_g2, send_g2)
    attn_share = shares(keep_g1, send_g1)
    out_rows = width // (2 * dp)
    qkv_grad = attn_share[:, : 3 * group].reshape(out_rows, 3, group)
    vec_grad = attn_share[:, 3 * group : 3 * group + 6].T
    out_grad = attn_share[:, 3 * group + 64 : 4 * group + 64].T
    up_grad = mlp_share[:, :units]
    down_grad = mlp_share[:, units:].T

    got_half = swap_cores(crop_send)
    mine = (2, nseq, slots, width // 2)
    pair = jnp.zeros(mine, F32)
    pair = put(pair, crop_keep.reshape((1,) + mine[1:]), (branch, 0, 0, 0))
    pair = put(pair, got_half.astype(F32).reshape((1,) + mine[1:]), (1 - branch, 0, 0, 0))
    far = exchange(pair.astype(BF16), 0, 1)
    crop_grad = jnp.zeros((tensors,) + mine, F32)
    crop_grad = put(crop_grad, pair[None], (t, 0, 0, 0, 0))
    crop_grad = put(crop_grad, far.astype(F32)[None], (1 - t, 0, 0, 0, 0))
    crop_grad = crop_grad.reshape(sequences, slots, width // 2)

    def over_tensor(out):
        whole = jnp.zeros((tensors, rows, width), BF16)
        whole = put(whole, out[None], (t, 0, 0))
        return put(whole, exchange(out, 0, 1)[None], (1 - t, 0, 0))

    all_q, all_m = over_tensor(out_q), over_tensor(out_m)
    own = jnp.where(on_query, all_m, all_q)
    got = swap_cores(jnp.where(on_query, all_q, all_m))
    encoded = jnp.zeros((tensors, 2, rows, width), BF16)
    encoded = put(encoded, own[:, None], (0, branch, 0, 0))
    encoded = put(encoded, got[:, None], (0, 1 - branch, 0, 0))
    encoded = encoded.reshape(1, sequences, slots, width)

    return (encoded, crop_grad, qkv_grad, out_grad, up_grad, down_grad, vec_grad[:2], vec_grad[2:])


def solution(mesh):
    placed = (
        P("branch", "dp", None, None),
        P(None, "dp", None),
        P("dp", None, None),
        P("branch", "dp", None, "tensor"),
        P("branch", "tensor", "dp"),
        P("branch", "dp", "tensor"),
        P("branch", "tensor", "dp"),
        P("branch", None, "dp"),
        P("branch", None, "dp"),
    )
    return jax.shard_map(
        on_device,
        mesh=mesh,
        in_specs=placed,
        out_specs=(
            P("branch", "dp", None, None),
            P("dp", None, "branch"),
            P(("branch", "dp"), None, "tensor"),
            P("tensor", ("branch", "dp")),
            P(("branch", "dp"), "tensor"),
            P("tensor", ("branch", "dp")),
            P(None, ("branch", "dp")),
            P(None, ("branch", "dp")),
        ),
        check_vma=False,
    )
```

time: 754 us -> 244 us (0.32)
  waiting for transfers between devices: 307 us -> 66.2 us
  blocking collectives: 226 us -> 0 us
  matrix products: 84.8 us -> 0 us
  starting transfers between devices: 3.26 us -> 65.4 us
  Pallas kernels: 0 us -> 53.4 us
  local copies, waits for them, and re-layouts: 73.1 us -> 38.3 us
  other arithmetic: 36.4 us -> 18 us
  between operations: 15.9 us -> 1.34 us
    all_gather x6 -> x0, blocking collectives: 192 us -> none  [the longest x1 33.5 us: on_device(): lax.all_gather(own_shards[2], 'dp', axis=0, tiled=True)]
    reduce_scatter x4 -> x0, waiting for transfers between devices: 187 us -> none  [the longest x1 61.5 us: on_device(): lax.psum_scatter(down_weight_grad * query_only, ('branch', 'dp'), scatter...]
    psum x3 -> x0, waiting for transfers between devices: 120 us -> none  [the longest x2 71.6 us: head_sum(): lax.psum(partial_rows.astype(jnp.bfloat16), 'tensor').astype(jnp.float32)]
    dot_general x39 -> x0, matrix products: 83.4 us -> none  [the longest x1 16.7 us: on_device(): pre_act = jnp.dot(normed_two, up_full, preferred_element_type=jnp.float32)]
    ppermute x3 -> x50, waiting for transfers between devices: 0.01 us -> 66.2 us  [the longest x39 66.2 us: exchange(): return lax.ppermute(block, SPAN, pairs)]
    ppermute x3 -> x50, starting transfers between devices: 2.97 us -> 65.4 us  [the longest x39 62.9 us: exchange(): return lax.ppermute(block, SPAN, pairs)]
    pallas_call x0 -> x4, Pallas kernels: none -> 53.4 us  [call(): pl.pallas_call(kernel, out_shape=[jax.ShapeDtypeStruct(s, d) for s, d in...]
    unnamed x1 -> x0, blocking collectives: 34.1 us -> none
  transfers between devices with their start and end apart: 10 -> 50, of which waited for: 6 -> 23; matrix products, arithmetic and copies ran while one was open for 7% -> 18% of each run, Pallas kernels for 0% -> 15%
where the time goes in v1:
time: 244 us; the launch traced here: 243 us
  waiting for transfers between devices  66.2 us (27%)
  starting transfers between devices  65.4 us (27%)
  Pallas kernels  53.4 us (22%)
  local copies, waits for them, and re-layouts  38.3 us (16%)
  other arithmetic  18 us (7%)
    ppermute x39, waiting for transfers between devices, exchange(): return lax.ppermute(block, SPAN, pairs)  66.2 us
    ppermute x39, starting transfers between devices, exchange(): return lax.ppermute(block, SPAN, pairs)  62.9 us
    pallas_call x4, Pallas kernels, call(): pl.pallas_call(kernel, out_shape=[jax.ShapeDtypeStruct(s, d) for s, d in...  53.4 us
    dynamic_update_slice x39, local copies, waits for them, and re-layouts, put(): return lax.dynamic_update_slice(whole, block, index)  16.3 us
    unnamed x38, local copies, waits for them, and re-layouts  5.46 us
  transfers between devices with their start and end apart: 50, of which 23 were waited for; matrix products, arithmetic and copies ran while one was open for 18% of the time, Pallas kernels for 15%

profile of v1, /device:TPU:0, one launch (start us, length us, event | category | flops | bytes accessed | tf_op | source)
XLA Modules:
  0.0 242.7 jit_solution(14310985048474893198)
XLA Ops:
  4.9 2.1 constant_dynamic-slice_fusion.8
  8.4 2.9 %collective-permute-start.25 = (bf16[56,384]{1,0:T(8,128)(2,1)S(1)}, bf16[56,384]{1,0:T(8,128)(2,1)S(1)}, u32[]{:S(2)}, u32[]{:S(2)}) collective-permute-start(bf16[56,384]{1,0:T(8,128)(2,1)S(1)} %get-tuple-element.73), channel_id=1, source_target_pairs={{0,4},{1,5},{2,6},{3,7},{4,0},{5,1},{6,2},{7,3},{8,12},{9,13},{10,... | collective-permute-start | bytes 129032 | tf_op jit(solution)/shard_map/ppermute | solution.py:288
  11.3 2.6 %collective-permute-start.26 = (bf16[56,384]{1,0:T(8,128)(2,1)S(1)}, bf16[56,384]{1,0:T(8,128)(2,1)S(1)}, u32[]{:S(2)}, u32[]{:S(2)}) collective-permute-start(bf16[56,384]{1,0:T(8,128)(2,1)S(1)} %get-tuple-element.73), channel_id=1, source_target_pairs={{0,8},{1,9},{2,10},{3,11},{4,12},{5,13},{6,14},{7,15},{8,0},{9,1},... | collective-permute-start | bytes 129032 | tf_op jit(solution)/shard_map/ppermute | solution.py:288
  15.7 3.5 %collective-permute-start.4 = (bf16[48,768]{1,0:T(8,128)(2,1)S(1)}, bf16[48,768]{1,0:T(8,128)(2,1)S(1)}, u32[]{:S(2)}, u32[]{:S(2)}) collective-permute-start(bf16[48,768]{1,0:T(8,128)(2,1)S(1)} %get-tuple-element.75), channel_id=1, source_target_pairs={{0,8},{1,9},{2,10},{3,11},{4,12},{5,13},{6,14},{7,15},{8,0},{9,1},... | collective-permute-start | bytes 221192 | tf_op jit(solution)/shard_map/ppermute | solution.py:288
  24.5 2.4 %collective-permute-start.30 = (bf16[4,56,384]{2,1,0:T(8,128)(2,1)S(1)}, bf16[4,56,384]{2,1,0:T(8,128)(2,1)S(1)}, u32[]{:S(2)}, u32[]{:S(2)}) collective-permute-start(bf16[4,56,384]{2,1,0:T(8,128)(2,1)S(1)} %bitcast_dynamic-update-slice_fusion.31), channel_id=1, source_target_pairs={{0,3},{1,2},{2,1},{3,0},{4,7},{5,6},{6,5},{7,4},{8,11},{9,10},{10,... | collective-permute-start | bytes 516104 | tf_op jit(solution)/shard_map/ppermute | solution.py:288
  28.6 1.9 collective-permute-start.7
  33.3 5.2 %collective-permute-done.6 = bf16[4,48,768]{2,1,0:T(8,128)(2,1)S(1)} collective-permute-done((bf16[4,48,768]{2,1,0:T(8,128)(2,1)S(1)}, bf16[4,48,768]{2,1,0:T(8,128)(2,1)S(1)}, u32[]{:S(2)}, u32[]{:S(2)}) %collective-permute-start.6) | collective-permute-done | bytes 294944 | tf_op jit(solution)/shard_map/ppermute | solution.py:288
  39.2 3.8 %collective-permute-done.8 = bf16[4,48,768]{2,1,0:T(8,128)(2,1)S(1)} collective-permute-done((bf16[4,48,768]{2,1,0:T(8,128)(2,1)S(1)}, bf16[4,48,768]{2,1,0:T(8,128)(2,1)S(1)}, u32[]{:S(2)}, u32[]{:S(2)}) %collective-permute-start.8) | collective-permute-done | bytes 294944 | tf_op jit(solution)/shard_map/ppermute | solution.py:288
  44.6 11.3 %shard_map.153 = (f32[384,512]{1,0:T(8,128)S(1)}, f32[384,512]{1,0:T(8,128)S(1)}, f32[8,512]{1,0:T(8,128)S(1)}, bf16[384,512]{1,0:T(8,128)(2,1)S(1)}, bf16[12,32...) custom-call(bf16[512,384]{1,0:T(8,128)(2,1)S(1)} %get-tuple-element., ...), custom_call_target="tpu_custom_call" | custom-call | flops 3825205248 | bytes 20000000 | tf_op jit(solution)/shard_map/pallas_call | solution.py:265
  58.9 3.5 %collective-permute-start.18 = (bf16[48,768]{1,0:T(8,128)(2,1)S(1)}, bf16[48,768]{1,0:T(8,128)(2,1)}, u32[]{:S(2)}, u32[]{:S(2)}) collective-permute-start(bf16[48,768]{1,0:T(8,128)(2,1)S(1)} %broadcast_select_fusion.2), channel_id=1, source_target_pairs={{0,8},{1,9},{2,10},{3,11},{4,12},{5,13},{6,14},{7,15},{8,0},{9,1},... | collective-permute-start | bytes 221192 | tf_op jit(solution)/shard_map/ppermute | solution.py:288
  62.8 11.7 %shard_map.154 = (bf16[512,384]{1,0:T(8,128)(2,1)S(1)}, bf16[2,192,1536]{2,1,0:T(8,128)(2,1)S(1)}, bf16[2,192,1536]{2,1,0:T(8,128)(2,1)}, f32[384,512]{1,0:T(8,128)S(1)}, f32[384,128]{1,0:T(8,128)S(1)}) custom-call(s32[1]{0:T(128)} %bitcast.62.b_ref, f32[384,512]{1,0:T(8,128)S(1)} %get-tuple-element.32.res_ref, bf16[512,384]{1,0:T(8,128)(2,1)S(1)} %bitcast.225, ...), custom_call_target="tpu_custom_call" | custom-call | flops 3623878656 | bytes 20000000 | tf_op jit(solution)/shard_map/pallas_call | solution.py:265
  74.5 14.0 %shard_map.155 = (f32[512,192]{1,0:T(8,128)S(1)}, bf16[512,192]{1,0:T(8,128)(2,1)S(1)}, bf16[2,192,896]{2,1,0:T(8,128)(2,1)S(1)}, bf16[2,192,896]{2,1,0:T(8,128)(2,1)}) custom-call(s32[1]{0:T(128)} %bitcast.62.b_ref, f32[384,512]{1,0:T(8,128)S(1)} %get-tuple-element.35.dres_ref, f32[384,512]{1,0:T(8,128)S(1)} %get-tuple-element.36.hat_ref, ...), custom_call_target="tpu_custom_call" | custom-call | flops 9261023232 | bytes 20000000 | tf_op jit(solution)/shard_map/pallas_call | solution.py:265
  96.5 2.9 %collective-permute-start.11 = (bf16[56,384]{1,0:T(8,128)(2,1)S(1)}, bf16[56,384]{1,0:T(8,128)(2,1)S(1)}, u32[]{:S(2)}, u32[]{:S(2)}) collective-permute-start(bf16[56,384]{1,0:T(8,128)(2,1)S(1)} %copy-done.17), channel_id=1, source_target_pairs={{0,8},{1,9},{2,10},{3,11},{4,12},{5,13},{6,14},{7,15},{8,0},{9,1},... | collective-permute-start | bytes 129032 | tf_op jit(solution)/shard_map/ppermute | solution.py:288
  101.4 3.3 %collective-permute-start.12 = (bf16[56,384]{1,0:T(8,128)(2,1)S(1)}, bf16[56,384]{1,0:T(8,128)(2,1)S(1)}, u32[]{:S(2)}, u32[]{:S(2)}) collective-permute-start(bf16[56,384]{1,0:T(8,128)(2,1)S(1)} %copy-done.17), channel_id=1, source_target_pairs={{0,12},{1,13},{2,14},{3,15},{4,8},{5,9},{6,10},{7,11},{8,4},{9,5},... | collective-permute-start | bytes 129032 | tf_op jit(solution)/shard_map/ppermute | solution.py:288
  105.4 1.9 collective-permute-done.12
  124.3 3.9 %collective-permute-done.15 = bf16[4,56,384]{2,1,0:T(8,128)(2,1)S(1)} collective-permute-done((bf16[4,56,384]{2,1,0:T(8,128)(2,1)}, bf16[4,56,384]{2,1,0:T(8,128)(2,1)S(1)}, u32[]{:S(2)}, u32[]{:S(2)}) %collective-permute-start.15) | collective-permute-done | bytes 172064 | tf_op jit(solution)/shard_map/ppermute | solution.py:288
  129.3 5.1 %collective-permute-done.20 = bf16[4,48,768]{2,1,0:T(8,128)(2,1)S(1)} collective-permute-done((bf16[4,48,768]{2,1,0:T(8,128)(2,1)S(1)}, bf16[4,48,768]{2,1,0:T(8,128)(2,1)S(1)}, u32[]{:S(2)}, u32[]{:S(2)}) %collective-permute-start.20) | collective-permute-done | bytes 294944 | tf_op jit(solution)/shard_map/ppermute | solution.py:288
  134.4 2.0 collective-permute-start.22
  138.3 6.0 %collective-permute-done.22 = bf16[4,48,768]{2,1,0:T(8,128)(2,1)S(1)} collective-permute-done((bf16[4,48,768]{2,1,0:T(8,128)(2,1)S(1)}, bf16[4,48,768]{2,1,0:T(8,128)(2,1)S(1)}, u32[]{:S(2)}, u32[]{:S(2)}) %collective-permute-start.22) | collective-permute-done | bytes 294944 | tf_op jit(solution)/shard_map/ppermute | solution.py:288
  145.6 1.8 bitcast_dynamic-update-slice_fusion.3
  147.3 5.3 %collective-permute-done.35 = bf16[2,2,256,192]{2,3,1,0:T(8,128)(2,1)S(1)} collective-permute-done((bf16[2,2,256,192]{2,3,1,0:T(8,128)(2,1)S(1)}, bf16[2,2,256,192]{2,3,1,0:T(8,128)(2,1)S(1)}, u32[]{:S(2)}, u32[]{:S(2)}) %collective-permute-start.35) | collective-permute-done | bytes 393248 | tf_op jit(solution)/shard_map/ppermute | solution.py:288
  159.0 2.6 %collective-permute-done.37 = bf16[4,24,896]{2,1,0:T(8,128)(2,1)S(1)} collective-permute-done((bf16[4,24,896]{2,1,0:T(8,128)(2,1)S(1)}, bf16[4,24,896]{2,1,0:T(8,128)(2,1)S(1)}, u32[]{:S(2)}, u32[]{:S(2)}) %collective-permute-start.37) | collective-permute-done | bytes 172064 | tf_op jit(solution)/shard_map/ppermute | solution.py:288
  161.6 2.5 %collective-permute-done.38 = bf16[4,24,896]{2,1,0:T(8,128)(2,1)S(1)} collective-permute-done((bf16[4,24,896]{2,1,0:T(8,128)(2,1)S(1)}, bf16[4,24,896]{2,1,0:T(8,128)(2,1)S(1)}, u32[]{:S(2)}, u32[]{:S(2)}) %collective-permute-start.38) | collective-permute-done | bytes 172064 | tf_op jit(solution)/shard_map/ppermute | solution.py:288
  164.1 2.3 collective-permute-done.39
  168.2 3.9 %collective-permute-start.41 = (bf16[24,896]{0,1:T(8,128)(2,1)}, bf16[24,896]{0,1:T(8,128)(2,1)}, u32[]{:S(2)}, u32[]{:S(2)}) collective-permute-start(bf16[24,896]{0,1:T(8,128)(2,1)} %bitcast.242), channel_id=1, source_target_pairs={{0,8},{1,9},{2,10},{3,11},{4,12},{5,13},{6,14},{7,15},{8,0},{9,1},... | collective-permute-start | bytes 129032 | tf_op jit(solution)/shard_map/ppermute | solution.py:288
  174.5 2.7 %collective-permute-done.40 = bf16[24,896]{0,1:T(8,128)(2,1)S(1)} collective-permute-done((bf16[24,896]{0,1:T(8,128)(2,1)}, bf16[24,896]{0,1:T(8,128)(2,1)S(1)}, u32[]{:S(2)}, u32[]{:S(2)}) %collective-permute-start.40) | collective-permute-done | bytes 43040 | tf_op jit(solution)/shard_map/ppermute | solution.py:288
  177.2 11.4 %collective-permute-done.41 = bf16[24,896]{0,1:T(8,128)(2,1)} collective-permute-done((bf16[24,896]{0,1:T(8,128)(2,1)}, bf16[24,896]{0,1:T(8,128)(2,1)}, u32[]{:S(2)}, u32[]{:S(2)}) %collective-permute-start.41) | collective-permute-done | bytes 43040 | tf_op jit(solution)/shard_map/ppermute | solution.py:288
  201.9 3.1 %collective-permute-done.46 = bf16[4,24,1536]{2,1,0:T(8,128)(2,1)S(1)} collective-permute-done((bf16[4,24,1536]{2,1,0:T(8,128)(2,1)S(1)}, bf16[4,24,1536]{2,1,0:T(8,128)(2,1)S(1)}, u32[]{:S(2)}, u32[]{:S(2)}) %collective-permute-start.46) | collective-permute-done | bytes 294944 | tf_op jit(solution)/shard_map/ppermute | solution.py:288
  206.1 1.8 select_bitcast_fusion.1
  208.1 16.4 %shard_map.152 = bf16[512,384]{1,0:T(8,128)(2,1)S(1)} custom-call(bf16[512,384]{1,0:T(8,128)(2,1)S(1)} %get-tuple-element.91.x_ref, s32[2,256]{1,0:T(2,128)S(1)} %get-tuple-element.107.seg_ref, bf16[2,2,384,384]{3,2,1,0:T(8,128)(2,1)S(1)} %pad_maximum_fusion.2.w1_ref, bf16[2,2,384,768]{3,2,1,0:T(8,128)(2,1)S(1)} %pad_maximum_fusion.1.w2_ref, ...), custom_call_target="tpu_custom_call" | custom-call | flops 5033164800 | bytes 20000000 | tf_op jit(solution)/shard_map/pallas_call | solution.py:265
  226.2 6.6 %collective-permute-start.47 = (bf16[24,1536]{1,0:T(8,128)(2,1)S(1)}, bf16[24,1536]{1,0:T(8,128)(2,1)S(1)}, u32[]{:S(2)}, u32[]{:S(2)}) collective-permute-start(bf16[24,1536]{1,0:T(8,128)(2,1)S(1)} %get-tuple-element.95), channel_id=1, source_target_pairs={{0,4},{1,5},{2,6},{3,7},{4,0},{5,1},{6,2},{7,3},{8,12},{9,13},{10,... | collective-permute-start | bytes 221192 | tf_op jit(solution)/shard_map/ppermute | solution.py:288
  237.0 1.8 collective-permute-done.48
  (218 shorter events, 89.4 us)
Async XLA Ops:
  6.9 36.2 %collective-permute-start = (bf16[512,384]{1,0:T(8,128)(2,1)}, bf16[512,384]{1,0:T(8,128)(2,1)}, u32[]{:S(2)}, u32[]{:S(2)}) collective-permute-start(bf16[512,384]{1,0:T(8,128)(2,1)} %bitcast.1), channel_id=1, source_target_pairs={{0,16},{16,0},{1,17},{17,1},{2,18},{18,2},{3,19},{19,3},{4,20},{20... | collective-permute-start | bytes 1179656 | tf_op jit(solution)/shard_map/ppermute | solution.py:280
  15.7 8.9 %collective-permute-start.4 = (bf16[48,768]{1,0:T(8,128)(2,1)S(1)}, bf16[48,768]{1,0:T(8,128)(2,1)S(1)}, u32[]{:S(2)}, u32[]{:S(2)}) collective-permute-start(bf16[48,768]{1,0:T(8,128)(2,1)S(1)} %get-tuple-element.75), channel_id=1, source_target_pairs={{0,8},{1,9},{2,10},{3,11},{4,12},{5,13},{6,14},{7,15},{8,0},{9,1},... | collective-permute-start | bytes 221192 | tf_op jit(solution)/shard_map/ppermute | solution.py:288
  20.4 8.2 %collective-permute-start.28 = (bf16[4,56,384]{2,1,0:T(8,128)(2,1)S(1)}, bf16[4,56,384]{2,1,0:T(8,128)(2,1)S(1)}, u32[]{:S(2)}, u32[]{:S(2)}) collective-permute-start(bf16[4,56,384]{2,1,0:T(8,128)(2,1)S(1)} %bitcast_dynamic-update-slice_fusion.31), channel_id=1, source_target_pairs={{0,1},{1,0},{2,3},{3,2},{4,5},{5,4},{6,7},{7,6},{8,9},{9,8},{10,11... | collective-permute-start | bytes 516104 | tf_op jit(solution)/shard_map/ppermute | solution.py:288
  22.1 8.4 %collective-permute-start.29 = (bf16[4,56,384]{2,1,0:T(8,128)(2,1)S(1)}, bf16[4,56,384]{2,1,0:T(8,128)(2,1)S(1)}, u32[]{:S(2)}, u32[]{:S(2)}) collective-permute-start(bf16[4,56,384]{2,1,0:T(8,128)(2,1)S(1)} %bitcast_dynamic-update-slice_fusion.31), channel_id=1, source_target_pairs={{0,2},{1,3},{2,0},{3,1},{4,6},{5,7},{6,4},{7,5},{8,10},{9,11},{10,... | collective-permute-start | bytes 516104 | tf_op jit(solution)/shard_map/ppermute | solution.py:288
  24.5 8.5 %collective-permute-start.30 = (bf16[4,56,384]{2,1,0:T(8,128)(2,1)S(1)}, bf16[4,56,384]{2,1,0:T(8,128)(2,1)S(1)}, u32[]{:S(2)}, u32[]{:S(2)}) collective-permute-start(bf16[4,56,384]{2,1,0:T(8,128)(2,1)S(1)} %bitcast_dynamic-update-slice_fusion.31), channel_id=1, source_target_pairs={{0,3},{1,2},{2,1},{3,0},{4,7},{5,6},{6,5},{7,4},{8,11},{9,10},{10,... | collective-permute-start | bytes 516104 | tf_op jit(solution)/shard_map/ppermute | solution.py:288
  27.0 11.4 %collective-permute-start.6 = (bf16[4,48,768]{2,1,0:T(8,128)(2,1)S(1)}, bf16[4,48,768]{2,1,0:T(8,128)(2,1)S(1)}, u32[]{:S(2)}, u32[]{:S(2)}) collective-permute-start(bf16[4,48,768]{2,1,0:T(8,128)(2,1)S(1)} %bitcast_dynamic-update-slice_fusion.27), channel_id=1, source_target_pairs={{0,1},{1,0},{2,3},{3,2},{4,5},{5,4},{6,7},{7,6},{8,9},{9,8},{10,11... | collective-permute-start | bytes 884744 | tf_op jit(solution)/shard_map/ppermute | solution.py:288
  28.6 10.5 %collective-permute-start.7 = (bf16[4,48,768]{2,1,0:T(8,128)(2,1)S(1)}, bf16[4,48,768]{2,1,0:T(8,128)(2,1)S(1)}, u32[]{:S(2)}, u32[]{:S(2)}) collective-permute-start(bf16[4,48,768]{2,1,0:T(8,128)(2,1)S(1)} %bitcast_dynamic-update-slice_fusion.27), channel_id=1, source_target_pairs={{0,2},{1,3},{2,0},{3,1},{4,6},{5,7},{6,4},{7,5},{8,10},{9,11},{10,... | collective-permute-start | bytes 884744 | tf_op jit(solution)/shard_map/ppermute | solution.py:288
  30.6 12.4 %collective-permute-start.8 = (bf16[4,48,768]{2,1,0:T(8,128)(2,1)S(1)}, bf16[4,48,768]{2,1,0:T(8,128)(2,1)S(1)}, u32[]{:S(2)}, u32[]{:S(2)}) collective-permute-start(bf16[4,48,768]{2,1,0:T(8,128)(2,1)S(1)} %bitcast_dynamic-update-slice_fusion.27), channel_id=1, source_target_pairs={{0,3},{1,2},{2,1},{3,0},{4,7},{5,6},{6,5},{7,4},{8,11},{9,10},{10,... | collective-permute-start | bytes 884744 | tf_op jit(solution)/shard_map/ppermute | solution.py:288
  33.2 11.0 %collective-permute-start.31 = (bf16[2,384,384]{2,1,0:T(8,128)(2,1)S(1)}, bf16[2,384,384]{2,1,0:T(8,128)(2,1)S(1)}, u32[]{:S(2)}, u32[]{:S(2)}) collective-permute-start(bf16[2,384,384]{2,1,0:T(8,128)(2,1)S(1)} %bitcast.236), channel_id=1, source_target_pairs={{0,16},{16,0},{1,17},{17,1},{2,18},{18,2},{3,19},{19,3},{4,20},{20... | collective-permute-start | bytes 1769480 | tf_op jit(solution)/shard_map/ppermute | solution.py:280
  43.0 12.9 %collective-permute-start.9 = (bf16[2,384,768]{2,1,0:T(8,128)(2,1)S(1)}, bf16[2,384,768]{2,1,0:T(8,128)(2,1)S(1)}, u32[]{:S(2)}, u32[]{:S(2)}) collective-permute-start(bf16[2,384,768]{2,1,0:T(8,128)(2,1)S(1)} %bitcast.228), channel_id=1, source_target_pairs={{0,16},{16,0},{1,17},{17,1},{2,18},{18,2},{3,19},{19,3},{4,20},{20... | collective-permute-start | bytes 3538952 | tf_op jit(solution)/shard_map/ppermute | solution.py:280
  58.4 50.5 %collective-permute-start.17 = (bf16[48,768]{1,0:T(8,128)(2,1)S(1)}, bf16[48,768]{1,0:T(8,128)(2,1)}, u32[]{:S(2)}, u32[]{:S(2)}) collective-permute-start(bf16[48,768]{1,0:T(8,128)(2,1)S(1)} %broadcast_select_fusion.2), channel_id=1, source_target_pairs={{0,4},{1,5},{2,6},{3,7},{4,0},{5,1},{6,2},{7,3},{8,12},{9,13},{10,... | collective-permute-start | bytes 221192 | tf_op jit(solution)/shard_map/ppermute | solution.py:288
  58.9 51.5 %collective-permute-start.18 = (bf16[48,768]{1,0:T(8,128)(2,1)S(1)}, bf16[48,768]{1,0:T(8,128)(2,1)}, u32[]{:S(2)}, u32[]{:S(2)}) collective-permute-start(bf16[48,768]{1,0:T(8,128)(2,1)S(1)} %broadcast_select_fusion.2), channel_id=1, source_target_pairs={{0,8},{1,9},{2,10},{3,11},{4,12},{5,13},{6,14},{7,15},{8,0},{9,1},... | collective-permute-start | bytes 221192 | tf_op jit(solution)/shard_map/ppermute | solution.py:288
  62.4 49.1 %collective-permute-start.19 = (bf16[48,768]{1,0:T(8,128)(2,1)S(1)}, bf16[48,768]{1,0:T(8,128)(2,1)}, u32[]{:S(2)}, u32[]{:S(2)}) collective-permute-start(bf16[48,768]{1,0:T(8,128)(2,1)S(1)} %broadcast_select_fusion.2), channel_id=1, source_target_pairs={{0,12},{1,13},{2,14},{3,15},{4,8},{5,9},{6,10},{7,11},{8,4},{9,5},... | collective-permute-start | bytes 221192 | tf_op jit(solution)/shard_map/ppermute | solution.py:288
  89.4 55.6 %collective-permute-start.32 = (bf16[512,384]{1,0:T(8,128)(2,1)S(1)}, bf16[512,384]{1,0:T(8,128)(2,1)}, u32[]{:S(2)}, u32[]{:S(2)}) collective-permute-start(bf16[512,384]{1,0:T(8,128)(2,1)S(1)} %get-tuple-element.34), channel_id=1, source_target_pairs={{0,1},{1,0},{2,3},{3,2},{4,5},{5,4},{6,7},{7,6},{8,9},{9,8},{10,11... | collective-permute-start | bytes 1179656 | tf_op jit(solution)/shard_map/ppermute | solution.py:288
  107.3 82.7 %collective-permute-start.43 = (bf16[2,192,1536]{2,1,0:T(8,128)(2,1)}, bf16[2,192,1536]{2,1,0:T(8,128)(2,1)}, u32[]{:S(2)}, u32[]{:S(2)}) collective-permute-start(bf16[2,192,1536]{2,1,0:T(8,128)(2,1)} %get-tuple-element.51), channel_id=1, source_target_pairs={{0,16},{16,0},{1,17},{17,1},{2,18},{18,2},{3,19},{19,3},{4,20},{20... | collective-permute-start | bytes 3538952 | tf_op jit(solution)/shard_map/ppermute | solution.py:280
  108.9 43.8 %collective-permute-start.36 = (bf16[2,192,896]{2,1,0:T(8,128)(2,1)}, bf16[2,192,896]{2,1,0:T(8,128)(2,1)}, u32[]{:S(2)}, u32[]{:S(2)}) collective-permute-start(bf16[2,192,896]{2,1,0:T(8,128)(2,1)} %get-tuple-element.49), channel_id=1, source_target_pairs={{0,16},{16,0},{1,17},{17,1},{2,18},{18,2},{3,19},{19,3},{4,20},{20... | collective-permute-start | bytes 2064392 | tf_op jit(solution)/shard_map/ppermute | solution.py:280
  111.5 9.3 %collective-permute-start.13 = (bf16[4,56,384]{2,1,0:T(8,128)(2,1)}, bf16[4,56,384]{2,1,0:T(8,128)(2,1)}, u32[]{:S(2)}, u32[]{:S(2)}) collective-permute-start(bf16[4,56,384]{2,1,0:T(8,128)(2,1)} %bitcast_dynamic-update-slice_fusion.35), channel_id=1, source_target_pairs={{0,1},{1,0},{2,3},{3,2},{4,5},{5,4},{6,7},{7,6},{8,9},{9,8},{10,11... | collective-permute-start | bytes 516104 | tf_op jit(solution)/shard_map/ppermute | solution.py:288
  115.2 8.3 %collective-permute-start.14 = (bf16[4,56,384]{2,1,0:T(8,128)(2,1)}, bf16[4,56,384]{2,1,0:T(8,128)(2,1)S(1)}, u32[]{:S(2)}, u32[]{:S(2)}) collective-permute-start(bf16[4,56,384]{2,1,0:T(8,128)(2,1)} %bitcast_dynamic-update-slice_fusion.35), channel_id=1, source_target_pairs={{0,2},{1,3},{2,0},{3,1},{4,6},{5,7},{6,4},{7,5},{8,10},{9,11},{10,... | collective-permute-start | bytes 516104 | tf_op jit(solution)/shard_map/ppermute | solution.py:288
  123.5 10.9 %collective-permute-start.20 = (bf16[4,48,768]{2,1,0:T(8,128)(2,1)S(1)}, bf16[4,48,768]{2,1,0:T(8,128)(2,1)S(1)}, u32[]{:S(2)}, u32[]{:S(2)}) collective-permute-start(bf16[4,48,768]{2,1,0:T(8,128)(2,1)S(1)} %copy-done.13), channel_id=1, source_target_pairs={{0,1},{1,0},{2,3},{3,2},{4,5},{5,4},{6,7},{7,6},{8,9},{9,8},{10,11... | collective-permute-start | bytes 884744 | tf_op jit(solution)/shard_map/ppermute | solution.py:288
  128.2 8.9 %collective-permute-start.21 = (bf16[4,48,768]{2,1,0:T(8,128)(2,1)S(1)}, bf16[4,48,768]{2,1,0:T(8,128)(2,1)S(1)}, u32[]{:S(2)}, u32[]{:S(2)}) collective-permute-start(bf16[4,48,768]{2,1,0:T(8,128)(2,1)S(1)} %copy-done.13), channel_id=1, source_target_pairs={{0,2},{1,3},{2,0},{3,1},{4,6},{5,7},{6,4},{7,5},{8,10},{9,11},{10,... | collective-permute-start | bytes 884744 | tf_op jit(solution)/shard_map/ppermute | solution.py:288
  134.4 9.9 %collective-permute-start.22 = (bf16[4,48,768]{2,1,0:T(8,128)(2,1)S(1)}, bf16[4,48,768]{2,1,0:T(8,128)(2,1)S(1)}, u32[]{:S(2)}, u32[]{:S(2)}) collective-permute-start(bf16[4,48,768]{2,1,0:T(8,128)(2,1)S(1)} %copy-done.13), channel_id=1, source_target_pairs={{0,3},{1,2},{2,1},{3,0},{4,7},{5,6},{6,5},{7,4},{8,11},{9,10},{10,... | collective-permute-start | bytes 884744 | tf_op jit(solution)/shard_map/ppermute | solution.py:288
  137.1 15.6 %collective-permute-start.35 = (bf16[2,2,256,192]{2,3,1,0:T(8,128)(2,1)S(1)}, bf16[2,2,256,192]{2,3,1,0:T(8,128)(2,1)S(1)}, u32[]{:S(2)}, u32[]{:S(2)}) collective-permute-start(bf16[2,2,256,192]{2,3,1,0:T(8,128)(2,1)S(1)} %convert_element_type.128), channel_id=1, source_target_pairs={{0,1},{1,0},{2,3},{3,2},{4,5},{5,4},{6,7},{7,6},{8,9},{9,8},{10,11... | collective-permute-start | bytes 1179656 | tf_op jit(solution)/shard_map/ppermute | solution.py:288
  144.3 13.5 %collective-permute-start.16 = (bf16[2,384,384]{2,1,0:T(8,128)(2,1)S(1)}, bf16[2,384,384]{2,1,0:T(8,128)(2,1)S(1)}, u32[]{:S(2)}, u32[]{:S(2)}) collective-permute-start(bf16[2,384,384]{2,1,0:T(8,128)(2,1)S(1)} %bitcast.235), channel_id=1, source_target_pairs={{0,16},{16,0},{1,17},{17,1},{2,18},{18,2},{3,19},{19,3},{4,20},{20... | collective-permute-start | bytes 1769480 | tf_op jit(solution)/shard_map/ppermute | solution.py:280
  145.1 61.0 %collective-permute-start.23 = (bf16[2,384,768]{2,1,0:T(8,128)(2,1)}, bf16[2,384,768]{2,1,0:T(8,128)(2,1)}, u32[]{:S(2)}, u32[]{:S(2)}) collective-permute-start(bf16[2,384,768]{2,1,0:T(8,128)(2,1)} %bitcast.57), channel_id=1, source_target_pairs={{0,16},{16,0},{1,17},{17,1},{2,18},{18,2},{3,19},{19,3},{4,20},{20... | collective-permute-start | bytes 3538952 | tf_op jit(solution)/shard_map/ppermute | solution.py:280
  157.8 8.6 %collective-permute-start.39 = (bf16[4,24,896]{2,1,0:T(8,128)(2,1)S(1)}, bf16[4,24,896]{2,1,0:T(8,128)(2,1)S(1)}, u32[]{:S(2)}, u32[]{:S(2)}) collective-permute-start(bf16[4,24,896]{2,1,0:T(8,128)(2,1)S(1)} %get-tuple-element.93), channel_id=1, source_target_pairs={{0,3},{1,2},{2,1},{3,0},{4,7},{5,6},{6,5},{7,4},{8,11},{9,10},{10,... | collective-permute-start | bytes 516104 | tf_op jit(solution)/shard_map/ppermute | solution.py:288
  167.4 9.8 %collective-permute-start.40 = (bf16[24,896]{0,1:T(8,128)(2,1)}, bf16[24,896]{0,1:T(8,128)(2,1)S(1)}, u32[]{:S(2)}, u32[]{:S(2)}) collective-permute-start(bf16[24,896]{0,1:T(8,128)(2,1)} %bitcast.241), channel_id=1, source_target_pairs={{0,4},{1,5},{2,6},{3,7},{4,0},{5,1},{6,2},{7,3},{8,12},{9,13},{10,... | collective-permute-start | bytes 129032 | tf_op jit(solution)/shard_map/ppermute | solution.py:288
  168.2 20.4 %collective-permute-start.41 = (bf16[24,896]{0,1:T(8,128)(2,1)}, bf16[24,896]{0,1:T(8,128)(2,1)}, u32[]{:S(2)}, u32[]{:S(2)}) collective-permute-start(bf16[24,896]{0,1:T(8,128)(2,1)} %bitcast.242), channel_id=1, source_target_pairs={{0,8},{1,9},{2,10},{3,11},{4,12},{5,13},{6,14},{7,15},{8,0},{9,1},... | collective-permute-start | bytes 129032 | tf_op jit(solution)/shard_map/ppermute | solution.py:288
  173.0 15.7 %collective-permute-start.42 = (bf16[24,896]{0,1:T(8,128)(2,1)}, bf16[24,896]{0,1:T(8,128)(2,1)}, u32[]{:S(2)}, u32[]{:S(2)}) collective-permute-start(bf16[24,896]{0,1:T(8,128)(2,1)} %bitcast.243), channel_id=1, source_target_pairs={{0,12},{1,13},{2,14},{3,15},{4,8},{5,9},{6,10},{7,11},{8,4},{9,5},... | collective-permute-start | bytes 129032 | tf_op jit(solution)/shard_map/ppermute | solution.py:288
  193.5 8.3 %collective-permute-start.44 = (bf16[4,24,1536]{2,1,0:T(8,128)(2,1)}, bf16[4,24,1536]{2,1,0:T(8,128)(2,1)S(1)}, u32[]{:S(2)}, u32[]{:S(2)}) collective-permute-start(bf16[4,24,1536]{2,1,0:T(8,128)(2,1)} %get-tuple-element.83), channel_id=1, source_target_pairs={{0,1},{1,0},{2,3},{3,2},{4,5},{5,4},{6,7},{7,6},{8,9},{9,8},{10,11... | collective-permute-start | bytes 884744 | tf_op jit(solution)/shard_map/ppermute | solution.py:288
  196.0 8.9 %collective-permute-start.46 = (bf16[4,24,1536]{2,1,0:T(8,128)(2,1)S(1)}, bf16[4,24,1536]{2,1,0:T(8,128)(2,1)S(1)}, u32[]{:S(2)}, u32[]{:S(2)}) collective-permute-start(bf16[4,24,1536]{2,1,0:T(8,128)(2,1)S(1)} %get-tuple-element.84), channel_id=1, source_target_pairs={{0,3},{1,2},{2,1},{3,0},{4,7},{5,6},{6,5},{7,4},{8,11},{9,10},{10,... | collective-permute-start | bytes 884744 | tf_op jit(solution)/shard_map/ppermute | solution.py:288
  224.5 11.0 %collective-permute-start.24 = (bf16[512,384]{1,0:T(8,128)(2,1)S(1)}, bf16[512,384]{1,0:T(8,128)(2,1)S(1)}, u32[]{:S(2)}, u32[]{:S(2)}) collective-permute-start(bf16[512,384]{1,0:T(8,128)(2,1)S(1)} %shard_map.152), channel_id=1, source_target_pairs={{0,1},{1,0},{2,3},{3,2},{4,5},{5,4},{6,7},{7,6},{8,9},{9,8},{10,11... | collective-permute-start | bytes 1179656 | tf_op jit(solution)/shard_map/ppermute | solution.py:288
  226.2 10.8 %collective-permute-start.47 = (bf16[24,1536]{1,0:T(8,128)(2,1)S(1)}, bf16[24,1536]{1,0:T(8,128)(2,1)S(1)}, u32[]{:S(2)}, u32[]{:S(2)}) collective-permute-start(bf16[24,1536]{1,0:T(8,128)(2,1)S(1)} %get-tuple-element.95), channel_id=1, source_target_pairs={{0,4},{1,5},{2,6},{3,7},{4,0},{5,1},{6,2},{7,3},{8,12},{9,13},{10,... | collective-permute-start | bytes 221192 | tf_op jit(solution)/shard_map/ppermute | solution.py:288
  (36 other events, 185.5 us)

commit v2 on v1

v2 whole, which is shorter than its diff:
```python
import functools
import math

import jax
import jax.numpy as jnp
from jax import lax
from jax.experimental import pallas as pl
from jax.experimental.pallas import tpu as pltpu
from jax.sharding import PartitionSpec as P

HD = 32
EPSILON = 1e-06
MASKED_SCORE = -1e30
LOG2E = 1.4426950408889634
BF16 = jnp.bfloat16
F32 = jnp.float32
VMEM_LIMIT = 56 * 1024 * 1024
PACE = 3600000


def nn(left, right):
    return lax.dot_general(left, right, (((1,), (0,)), ((), ())), preferred_element_type=F32)


def nt(left, right):
    return lax.dot_general(left, right, (((1,), (1,)), ((), ())), preferred_element_type=F32)


def tn(left, right):
    return lax.dot_general(left, right, (((0,), (0,)), ((), ())), preferred_element_type=F32)


def gelu_parts(v):
    a = jnp.abs(v)
    t = 1.0 / (1.0 + (0.3275911 / math.sqrt(2.0)) * a)
    bell = jnp.exp2(v * v * (-0.5 * LOG2E))
    poly = t * (
        0.5 * 0.254829592
        + t * (0.5 * -0.284496736 + t * (0.5 * 1.421413741 + t * (0.5 * -1.453152027 + t * (0.5 * 1.061405429))))
    )
    tail = poly * bell
    return jnp.where(v < 0, tail, 1.0 - tail), bell


def norm_cols(values, gain, shift):
    centred = values - jnp.mean(values, axis=0, keepdims=True)
    spread = jnp.mean(centred * centred, axis=0, keepdims=True)
    rstd = lax.rsqrt(spread + EPSILON)
    hat = centred * rstd
    return hat, rstd, hat * gain + shift


def norm_cols_back(upstream, hat, rstd, gain):
    t = upstream * gain
    return rstd * (t - jnp.mean(t, axis=0, keepdims=True) - hat * jnp.mean(t * hat, axis=0, keepdims=True))


def columns_of(vec_ref, scratch):
    scratch[...] = jnp.zeros_like(scratch)
    scratch[0:8, :] = vec_ref[...]
    return scratch[...].T


def place_columns(plan, chunk_refs, shard, width, me, cols_ref):
    for ref, spots in zip(chunk_refs, plan):
        for index, (mask, u) in spots:
            if u == 0:
                rows = pl.ds(pl.multiple_of((me ^ mask) * shard, 16), shard)
                cols_ref[rows, :] = ref[index + (slice(None), slice(width, width + 128))].astype(F32)


def place_weights(plan, own_refs, got_refs, shard, ids, targets):
    b, me, t = ids
    for half, refs in ((b, own_refs), (1 - b, got_refs)):
        for ref, spots in zip(refs, plan):
            for index, (mask, u) in spots:
                rows = pl.ds(pl.multiple_of((me ^ mask) * shard, 16), shard)
                for target, start, wide in targets:
                    target[half, t ^ u, rows, :] = ref[index + (slice(0, shard), slice(start, start + wide))]


def attend(x_ref, seg_ref, w1_ref, cols, q_ref, k_ref, v_ref, bias_ref, ctx_ref, pb_refs, inv_ref, score_refs, ready):
    tensors, width = w1_ref.shape[1], w1_ref.shape[2]
    group = width // tensors
    heads_g = group // HD
    nseq, slots = seg_ref.shape
    x_t = x_ref[...].astype(F32).T
    hat, rstd, normed = norm_cols(x_t, cols[:, 0:1], cols[:, 2:3])
    normed_low = normed.astype(BF16)
    ready("normed", hat, rstd, normed_low)
    rows = x_t.shape[1]
    for t in range(tensors):
        qk = tn(w1_ref[0, t], normed_low).astype(BF16)
        q_ref[t * heads_g : (t + 1) * heads_g] = qk[:group].reshape(heads_g, HD, rows)
        k_ref[t * heads_g : (t + 1) * heads_g] = qk[group:].reshape(heads_g, HD, rows)
        vo = tn(w1_ref[1, t], normed_low).astype(BF16)
        v_ref[t * heads_g : (t + 1) * heads_g, 0:HD] = vo[:group].reshape(heads_g, HD, rows)
    v_ref[:, HD:, :] = jnp.ones((v_ref.shape[0], v_ref.shape[1] - HD, rows), BF16)
    ready("projected")
    for s in range(nseq):
        across = jnp.broadcast_to(seg_ref[s : s + 1, :].astype(F32), (slots, slots))
        bias_ref[s] = jnp.where(across == across.T, 0.0, MASKED_SCORE)
    heads = tensors * heads_g
    parts = [slice(s * slots, (s + 1) * slots) for s in range(nseq)]
    ctx_ref[:, :heads_g] = jnp.zeros((tensors, heads_g, HD, rows), BF16)

    def score(h, s):
        score_refs[s][...] = tn(k_ref[h, :, parts[s]], q_ref[h, :, parts[s]])

    def soften(h, s):
        scores = score_refs[s][...] + bias_ref[s]
        top = jnp.max(scores, axis=0, keepdims=True)
        pb_refs[s][h] = jnp.exp2((scores - top) * (HD**-0.5 * LOG2E)).astype(BF16)

    def blend(h, s):
        both = nn(v_ref[h, :, parts[s]], pb_refs[s][h])
        inv = 1.0 / both[HD : HD + 1]
        if inv_ref is not None:
            inv_ref[h, :, parts[s]] = jnp.broadcast_to(inv, (8, slots))
        ctx_ref[h // heads_g, heads_g + h % heads_g, :, parts[s]] = (both[:HD] * inv).astype(BF16)

    def one_head(h, carry):
        for s in range(nseq):
            if s + 1 < nseq:
                score(h, s + 1)
            else:
                score(jnp.minimum(h + 1, heads - 1), 0)
            if s:
                blend(h, s - 1)
            else:
                blend(jnp.maximum(h - 1, 0), nseq - 1)
            soften(h, s)
        return carry

    score(0, 0)
    lax.fori_loop(0, heads, one_head, 0, unroll=4)
    ready("weights")
    blend(heads - 1, nseq - 1)
    ready("context")
    attn = sum(nn(w1_ref[1, t], ctx_ref[t].reshape(width, rows)) for t in range(tensors))
    return x_t, attn


def pack_kernel(b_ref, qkv_ref, out_ref, up_ref, down_ref, gain_ref, bias_ref, keep_ref, send_ref):
    first = b_ref[0] == 0
    shard, width = up_ref.shape[0], 2 * out_ref.shape[1]
    vec = jnp.concatenate([gain_ref[...], bias_ref[...], jnp.zeros((2, shard), F32)], axis=0)
    vec = jnp.concatenate([vec, jnp.zeros((8, 128 - shard), F32)], axis=1)
    none = jnp.zeros((8, 128), F32)
    vec = jnp.concatenate([jnp.where(first, vec, none), jnp.where(first, none, vec), jnp.zeros((112, 128), F32)], axis=0)
    vec = vec.T[:shard, :].astype(BF16)
    half_0 = jnp.concatenate([qkv_ref[0], qkv_ref[1]], axis=1).astype(BF16)
    half_1 = jnp.concatenate([qkv_ref[2], out_ref[...]], axis=1).astype(BF16)
    up, down = up_ref[...].astype(BF16), down_ref[...].astype(BF16)
    for ref, is_first in ((keep_ref, first), (send_ref, jnp.logical_not(first))):
        ref[:, :width] = jnp.where(is_first, half_0, half_1)
        ref[:, width : width + 128] = vec
        ref[:, width + 128 :] = jnp.where(is_first, up, down)


def split_kernel(width, b_ref, keep_ref, got_ref, q_ref, m_ref):
    first = b_ref[0] == 0
    keep, got = keep_ref[...], got_ref[...]
    q_ref[...] = jnp.where(first, keep, got)
    q_ref[:, width : width + 128] = keep[:, width : width + 128] + got[:, width : width + 128]
    m_ref[:, :width] = jnp.where(first, got[:, :width], keep[:, :width])
    m_ref[:, width:] = jnp.where(first, got[:, width + 128 :], keep[:, width + 128 :])


def query_attn_kernel(plan, shard, *refs):
    ids_ref, x_ref, seg_ref = refs[:3]
    nseq, refs = seg_ref.shape[0], refs[3:]
    if plan is None:
        given_ref, vec_ref = refs[:2]
        refs = refs[2:]
    else:
        own, got = refs[: len(plan)], refs[len(plan) : 2 * len(plan)]
        refs = refs[2 * len(plan) :]
    res_ref, cols_ref, refs = refs[0], refs[1], refs[2:]
    count = 9 + nseq
    far, kept, refs = refs[:count], refs[count : 2 * count], refs[2 * count :]
    w1_ref, hat_ref, rstd_ref, normed_ref, q_ref, k_ref, v_ref, inv_ref, ctx_ref, *pb_refs = kept
    score_refs, bias_ref, sems = refs[:nseq], refs[nseq], refs[-1]
    copies = [pltpu.make_async_copy(here, there, sems.at[i]) for i, (here, there) in enumerate(zip(kept, far))]
    if plan is None:
        w1_ref[...] = given_ref[...]
        cols_ref[...] = columns_of(vec_ref, refs[nseq + 1])
    else:
        ids = ids_ref[0], ids_ref[1], ids_ref[2]
        place_columns(plan, own, shard, w1_ref.shape[3], ids[1], cols_ref)
        place_weights(plan, own, got, shard, ids, [(w1_ref, 0, w1_ref.shape[3])])
    copies[0].start()
    cols = cols_ref[...]

    def ready(what, *values):
        if what == "normed":
            hat, rstd, normed = values
            hat_ref[...] = hat
            rstd_ref[...] = jnp.broadcast_to(rstd, rstd_ref.shape)
            normed_ref[...] = normed
        spots = {"normed": (1, 2, 3), "projected": (4, 5, 6), "weights": range(9, count), "context": (7, 8)}
        for i in spots[what]:
            copies[i].start()

    x_t, attn = attend(
        x_ref, seg_ref, w1_ref, cols, q_ref, k_ref, v_ref, bias_ref, ctx_ref, pb_refs, inv_ref, score_refs, ready
    )
    res_ref[...] = x_t + attn + cols[:, 3:4]
    for copy in copies:
        copy.wait()


def momentum_kernel(plan, shard, *refs):
    ids_ref, x_ref, seg_ref = refs[:3]
    nseq = seg_ref.shape[0]
    pb_refs, score_refs, refs = refs[-2 * nseq : -nseq], refs[-nseq:], refs[3 : -2 * nseq]
    if plan is None:
        w1_ref, w2_ref, vec_ref, out_ref = refs[:4]
        q_ref, k_ref, v_ref, ctx_ref, bias_ref, acc_ref, vec_pad = refs[4:]
        cols = columns_of(vec_ref, vec_pad)
    else:
        cols_ref, refs = refs[0], refs[1:]
        own, got = refs[: len(plan)], refs[len(plan) : 2 * len(plan)]
        out_ref, q_ref, k_ref, v_ref, ctx_ref, bias_ref, acc_ref, w1_ref, w2_ref = refs[2 * len(plan) :]
        cols = cols_ref[...][:, 8:]
        ids = ids_ref[0], ids_ref[1], ids_ref[2]
        wide = w1_ref.shape[3]
        place_weights(plan, own, got, shard, ids, [(w1_ref, 0, wide), (w2_ref, wide, w2_ref.shape[3])])
    x_t, attn = attend(
        x_ref, seg_ref, w1_ref, cols, q_ref, k_ref, v_ref, bias_ref, ctx_ref, pb_refs, None, score_refs, lambda *what: None
    )
    res = x_t + attn + cols[:, 3:4]
    _, _, normed = norm_cols(res, cols[:, 1:2], cols[:, 4:5])
    rows_low = normed.T.astype(BF16)
    acc_ref[...] = res + cols[:, 5:6]
    tensors, units = w2_ref.shape[1], w2_ref.shape[3]
    chunk = 256
    parts = units // chunk

    def step(i, carry):
        t, c = i // parts, pl.ds(pl.multiple_of((i % parts) * chunk, chunk), chunk)
        pre = nn(rows_low, w2_ref[0, t, :, c])
        half, _ = gelu_parts(pre)
        acc_ref[...] += nt(w2_ref[1, t, :, c], (pre * half).astype(BF16))
        return carry

    lax.fori_loop(0, tensors * parts, step, 0)
    out_ref[...] = acc_ref[...].T.astype(BF16)


def store_grads(plan, ids, ref, t, cols, values):
    if plan is None:
        ref[t, :, cols] = values
        return
    dp, final = plan
    me, mine = ids[1], ids[2]
    share = values.shape[0] // dp
    size = final.bit_length()
    for i in range(dp):
        mask = me ^ i
        ref[(mask & final) * 2 + (mine ^ t), mask >> (size), :, cols] = values[i * share : (i + 1) * share]


def query_mlp_kernel(plan, chunks, shard, *refs):
    ids_ref, res_ref, cot_ref, cols_ref = refs[:4]
    refs = refs[4:]
    ids = ids_ref[0], ids_ref[1], ids_ref[2]
    b = ids[0]
    if chunks is None:
        w2_ref, refs = refs[0], refs[1:]
    else:
        own, got = refs[: len(chunks)], refs[len(chunks) : 2 * len(chunks)]
        w2_ref, refs = refs[-1], refs[2 * len(chunks) : -1]
        place_weights(chunks, own, got, shard, ids, [(w2_ref, 0, w2_ref.shape[3])])
    out_ref, keep_ref, send_ref, dres_ref, vgrad_ref, acc_ref, dn_ref, n2t_ref, gt_ref = refs
    cols = cols_ref[...]
    res = res_ref[...]
    hat, rstd, normed = norm_cols(res, cols[:, 1:2], cols[:, 4:5])
    n2t_ref[...] = normed.astype(BF16)
    rows_low = normed.T.astype(BF16)
    cot = cot_ref[...]
    cot_t = cot.astype(F32).T
    gt_ref[...] = cot_t.astype(BF16)
    acc_ref[...] = res + cols[:, 5:6]
    dn_ref[...] = jnp.zeros_like(dn_ref)
    tensors, width, units = w2_ref.shape[1], w2_ref.shape[2], w2_ref.shape[3]
    chunk = 256
    parts = units // chunk
    half_rows = width // 2

    def step(i, carry):
        t, off = i // parts, pl.multiple_of((i % parts) * chunk, chunk)
        c = pl.ds(off, chunk)
        up, down = w2_ref[0, t, :, c], w2_ref[1, t, :, c]
        pre = nn(rows_low, up)
        d_hidden = nn(cot, down)
        half, bell = gelu_parts(pre)
        hidden = (pre * half).astype(BF16)
        d_pre = (d_hidden * (half + pre * bell * (1.0 / math.sqrt(2.0 * math.pi)))).astype(BF16)
        acc_ref[...] += nt(down, hidden)
        dn_ref[...] += nt(up, d_pre)
        for ref, which in ((keep_ref, b), (send_ref, 1 - b)):
            rows = pl.ds(pl.multiple_of(which * half_rows, 16), half_rows)
            store_grads(plan, ids, ref, t, c, nn(n2t_ref[rows, :], d_pre).astype(BF16))
            later = pl.ds(pl.multiple_of(units + off, chunk), chunk)
            store_grads(plan, ids, ref, t, later, nn(gt_ref[rows, :], hidden).astype(BF16))
        return carry

    lax.fori_loop(0, tensors * parts, step, 0)
    out_ref[...] = acc_ref[...].T.astype(BF16)
    d_n2 = dn_ref[...]
    d_res = cot_t + norm_cols_back(d_n2, hat, rstd, cols[:, 1:2])
    dres_ref[...] = d_res
    lane = lax.broadcasted_iota(jnp.int32, vgrad_ref.shape, 1)
    total = jnp.zeros(vgrad_ref.shape, F32)
    for j, term in ((1, d_n2 * hat), (3, d_res), (4, d_n2), (5, cot_t)):
        total = total + jnp.where(lane == 64 + j, jnp.sum(term, axis=1, keepdims=True), 0.0)
    vgrad_ref[...] = total


def query_back_kernel(plan, nseq, *refs):
    ids_ref, dres_ref, vgrad_ref, cols_ref = refs[:4]
    count = 9 + nseq
    far, refs = refs[4 : 4 + count], refs[4 + count :]
    crop_keep_ref, crop_send_ref, keep_ref, send_ref, dctx_ref, dproj_ref, dattn_ref, vg_ref, crop_ref = refs[:9]
    dp_refs, ds_refs, delta_refs = (refs[9 + i * nseq : 9 + (i + 1) * nseq] for i in range(3))
    kept, sems = refs[9 + 3 * nseq : -1], refs[-1]
    w1_ref, hat_ref, rstd_ref, normed_ref, q_ref, k_ref, v_ref, inv_ref, ctx_ref, *pb_refs = kept
    copies = [pltpu.make_async_copy(there, here, sems.at[i]) for i, (here, there) in enumerate(zip(kept, far))]
    late = (1, 2, 3)
    for i in [i for i in range(count) if i not in late] + list(late):
        copies[i].start()
    ids = ids_ref[0], ids_ref[1], ids_ref[2]
    b = ids[0]
    tensors, width = w1_ref.shape[1], w1_ref.shape[2]
    group = width // tensors
    heads_g = group // HD
    heads, slots = pb_refs[0].shape[0], pb_refs[0].shape[1]
    rows = nseq * slots
    d_attn = dres_ref[...].astype(BF16)
    dattn_ref[...] = d_attn
    copies[0].wait()
    for t in range(tensors):
        vo = tn(w1_ref[1, t], d_attn).astype(BF16)
        dctx_ref[t * heads_g : (t + 1) * heads_g] = vo[group:].reshape(heads_g, HD, rows)
    dproj_ref[:, 3 * heads_g :] = jnp.zeros((tensors, heads_g, HD, rows), BF16)
    parts = [slice(s * slots, (s + 1) * slots) for s in range(nseq)]
    scale = HD**-0.5

    def d_weights(h, s):
        t, hh = h // heads_g, h % heads_g
        low_ctx = dctx_ref[h, :, parts[s]].astype(F32) * inv_ref[h, 0:1, parts[s]]
        delta = jnp.sum(low_ctx * ctx_ref[t, heads_g + hh, :, parts[s]].astype(F32), axis=0, keepdims=True)
        delta_refs[s][...] = jnp.broadcast_to(delta, (8, slots))
        low_ctx = low_ctx.astype(BF16)
        dp_refs[s][...] = tn(v_ref[h, 0:HD, parts[s]], low_ctx)
        dproj_ref[t, 2 * heads_g + hh, :, parts[s]] = nt(low_ctx, pb_refs[s][h]).astype(BF16)

    def harden(h, s):
        ds_refs[s][...] = (pb_refs[s][h].astype(F32) * (dp_refs[s][...] - delta_refs[s][0:1, :])).astype(BF16)

    def d_inputs(h, s):
        t, hh = h // heads_g, h % heads_g
        d_scores = ds_refs[s][...]
        dproj_ref[t, hh, :, parts[s]] = (nn(k_ref[h, :, parts[s]], d_scores) * scale).astype(BF16)
        dproj_ref[t, heads_g + hh, :, parts[s]] = (nt(q_ref[h, :, parts[s]], d_scores) * scale).astype(BF16)

    def one_head(h, carry):
        for s in range(nseq):
            if s + 1 < nseq:
                d_weights(h, s + 1)
            else:
                d_weights(jnp.minimum(h + 1, heads - 1), 0)
            if s:
                d_inputs(h, s - 1)
            else:
                d_inputs(jnp.maximum(h - 1, 0), nseq - 1)
            harden(h, s)
        return carry

    for i in range(1, count):
        if i not in late:
            copies[i].wait()
    d_weights(0, 0)
    lax.fori_loop(0, heads, one_head, 0, unroll=4)
    d_inputs(heads - 1, nseq - 1)
    d_normed = jnp.zeros((width, rows), F32)
    for t in range(tensors):
        d_t = dproj_ref[t].reshape(4 * group, rows)
        d_normed += nn(w1_ref[0, t], d_t[: 2 * group]) + nn(w1_ref[1, t], d_t[2 * group :])
    for i in late:
        copies[i].wait()
    hat = hat_ref[...]
    cols = cols_ref[...]
    crop_ref[...] = dres_ref[...] + norm_cols_back(d_normed, hat, rstd_ref[0:1, :], cols[:, 0:1])
    lane = lax.broadcasted_iota(jnp.int32, vgrad_ref.shape, 1)
    total = vgrad_ref[...]
    for j, term in ((0, d_normed * hat), (2, d_normed)):
        total = total + jnp.where(lane == 64 + j, jnp.sum(term, axis=1, keepdims=True), 0.0)
    vg_ref[...] = total
    half_rows = width // 2
    tile = (3 * group) // 128 * 128
    for ref, which in ((keep_ref, b), (send_ref, 1 - b)):
        part = pl.ds(pl.multiple_of(which * half_rows, 16), half_rows)
        left, right = normed_ref[part, :], dattn_ref[part, :]
        for t in range(tensors):
            d_t = dproj_ref[t].reshape(4 * group, rows)
            grads = nt(left, d_t[: 3 * group + 64])
            outs = nt(right, ctx_ref[t, heads_g:].reshape(group, rows))
            outs = jnp.concatenate([outs, jnp.zeros((half_rows, 64), F32)], axis=1)
            grads = jnp.concatenate([grads[:, :tile], grads[:, tile:] + vg_ref[part, :], outs], axis=1)
            store_grads(plan, ids, ref, t, slice(None), grads.astype(BF16))
    for s in range(nseq):
        part = slice(s * slots, (s + 1) * slots)
        crop_keep_ref[s] = crop_ref[pl.ds(pl.multiple_of(b * half_rows, 16), half_rows), part]
        crop_send_ref[s] = crop_ref[pl.ds(pl.multiple_of((1 - b) * half_rows, 16), half_rows), part].astype(BF16)


def encoded_kernel(ids_ref, q_ref, q_far, m_ref, m_far, got_ref, got_far, out_ref):
    b, t = ids_ref[0], ids_ref[2]
    first = b == 0
    out_ref[t, b] = jnp.where(first, m_ref[...], q_ref[...])
    out_ref[1 - t, b] = jnp.where(first, m_far[...], q_far[...])
    out_ref[t, 1 - b] = got_ref[...]
    out_ref[1 - t, 1 - b] = got_far[...]


def call(kernel, out_shapes, scratch, args, smem=0, hbm=0, hbm_outs=0, copies=0, stream=False):
    place, hold = pl.BlockSpec(memory_space=pltpu.VMEM), pl.BlockSpec(memory_space=pltpu.HBM)
    inner = args[smem : len(args) - hbm]
    if stream:
        specs = [pl.BlockSpec(x.shape, lambda i, n=x.ndim: (0,) * n) for x in inner]
    else:
        specs = [place] * len(inner)
    return pl.pallas_call(
        kernel,
        grid=(1,) if stream else (),
        out_shape=[jax.ShapeDtypeStruct(s, d) for s, d in out_shapes],
        in_specs=[pl.BlockSpec(memory_space=pltpu.SMEM)] * smem + specs + [hold] * hbm,
        out_specs=[place] * (len(out_shapes) - hbm_outs) + [hold] * hbm_outs,
        scratch_shapes=[pltpu.VMEM(s, d) for s, d in scratch]
        + ([pltpu.SemaphoreType.DMA((copies,))] if copies else []),
        compiler_params=pltpu.CompilerParams(vmem_limit_bytes=VMEM_LIMIT),
    )(*args)


SPAN = ("dp", "tensor")


def swap_cores(block):
    return lax.ppermute(block, "branch", [(0, 1), (1, 0)])


def exchange(block, dp_mask, t_mask):
    dp, tensors = lax.axis_size("dp"), lax.axis_size("tensor")
    pairs = [
        (i * tensors + t, (i ^ dp_mask) * tensors + (t ^ t_mask)) for i in range(dp) for t in range(tensors)
    ]
    return lax.ppermute(block, SPAN, pairs)


def after(value, *deps):
    return lax.optimization_barrier((value, *deps))[0]


def near_pieces(both):
    return [exchange(both[j], j // 2, j % 2) for j in range(1, both.shape[0])]


def far_pieces(low, final):
    return [exchange(low[k], k << final.bit_length(), 0) for k in range(1, low.shape[0])]


def add_all(total, pieces):
    for piece in pieces:
        total = total + piece.astype(F32)
    return total


def dp_groups():
    bits = lax.axis_size("dp").bit_length() - 1
    groups, high = [], bits
    while high >= 2:
        high -= 2
        groups.append((high, 4))
    last = (0, 2) if high == 1 else None
    return groups, last


def put(whole, block, index):
    return lax.dynamic_update_slice(whole, block, index)


def gather(block):
    groups, last = dp_groups()
    me, t = lax.axis_index("dp"), lax.axis_index("tensor")
    tensors = lax.axis_size("tensor")
    for number, (shift, size) in enumerate(groups):
        lead, tail = block.shape[:number], block.shape[number:]
        whole = jnp.zeros(lead + (size,) + tail, block.dtype)
        mine = (me >> shift) & (size - 1)
        pieces = [(0, block)] + [(k, exchange(block, k << shift, 0)) for k in range(1, size)]
        for k, piece in pieces:
            whole = put(whole, jnp.expand_dims(piece, number), (0,) * number + (mine ^ k,) + (0,) * len(tail))
        block = whole
    lead, tail = block.shape[: len(groups)], block.shape[len(groups) :]
    size = last[1] if last else 1
    mine = me & (size - 1)
    whole = jnp.zeros((tensors,) + lead + (size,) + tail, block.dtype)
    for k in range(size):
        for u in range(tensors):
            piece = block if k == u == 0 else exchange(block, k, u)
            piece = jnp.expand_dims(jnp.expand_dims(piece, len(lead)), 0)
            whole = put(whole, piece, (t ^ u,) + (0,) * len(lead) + (mine ^ k,) + (0,) * len(tail))
    return whole.reshape((tensors, lax.axis_size("dp")) + tail)


def scatter_sum(block):
    groups, last = dp_groups()
    me, t = lax.axis_index("dp"), lax.axis_index("tensor")
    tensors = lax.axis_size("tensor")
    tail = block.shape[2:]
    size = last[1] if last else 1
    lead = tuple(g[1] for g in groups)
    block = block.reshape((tensors,) + lead + (size,) + tail)
    mine = me & (size - 1)

    def take(k, u):
        start = (t ^ u,) + (0,) * len(lead) + (mine ^ k,) + (0,) * len(tail)
        piece = lax.dynamic_slice(block, start, (1,) + lead + (1,) + tail)
        return piece.reshape(lead + tail)

    total = take(0, 0).astype(F32)
    for k in range(size):
        for u in range(tensors):
            if k or u:
                total = total + exchange(take(k, u), k, u).astype(F32)
    for number in reversed(range(len(groups))):
        shift, size = groups[number]
        mine = (me >> shift) & (size - 1)
        low = total.astype(BF16)

        def part(k, whole=low, number=number, mine=mine):
            return lax.dynamic_index_in_dim(whole, mine ^ k, number, keepdims=False)

        total = part(0, total).astype(F32)
        for k in range(1, size):
            total = total + exchange(part(k), k << shift, 0).astype(F32)
    return total


def stack_peers(block, stage):
    return jnp.stack([block] + [exchange(block, *peer) for peer in stage]), [(0, 0)] + stage


def chunks_of(block, masks, stage):
    pieces = [((0, 0), block)] + [(peer, exchange(block, *peer)) for peer in stage]
    return [
        (piece, [((j,), (m ^ peer[0], u ^ peer[1])) for j, (m, u) in enumerate(masks)]) for peer, piece in pieces
    ]


def chip_sum(keep, send):
    return (keep.astype(F32) + swap_cores(send).astype(F32)).astype(BF16)


def on_device(
    crops, segment_ids, cotangent, qkv_weight, out_weight, up_weight, down_weight, gain_rows, biases
):
    branch, me, t = lax.axis_index("branch"), lax.axis_index("dp"), lax.axis_index("tensor")
    dp, tensors = lax.axis_size("dp"), lax.axis_size("tensor")
    on_query = branch == 0
    _, sequences, slots, width = crops.shape
    nseq = sequences // (2 * tensors)
    rows = nseq * slots
    shard = qkv_weight.shape[1]
    group = out_weight.shape[1]
    units = up_weight.shape[2]
    heads = tensors * group // HD
    heads_g = group // HD
    ids = jnp.stack([branch, me, t]).astype(jnp.int32)
    fine = tensors == 2 and dp == 8 and shard % 16 == 0
    near = [(k << 1, 0) for k in range(1, 4)]

    qkv, out_t = qkv_weight[0].transpose(1, 0, 2), out_weight[0].T
    up, down_t = up_weight[0], down_weight[0].T
    if fine:
        block = ((shard, width + 128 + units), BF16)
        keep, send = call(
            pack_kernel,
            [block] * 2,
            [],
            (ids, qkv, out_t, up, down_t, gain_rows[0], biases[0]),
            smem=1,
            stream=True,
        )
        got = swap_cores(send)
        q_all, m_all = call(
            functools.partial(split_kernel, width),
            [block, ((shard, width + units), BF16)],
            [],
            (ids, keep, got),
            smem=1,
        )
    else:
        small = jnp.concatenate([gain_rows[0], biases[0]], axis=0).astype(BF16)
        vec_rows = put(jnp.zeros((8, width), BF16), small, (0, me * shard))
        half_0 = jnp.concatenate([qkv[0], qkv[1]], axis=1).astype(BF16)
        half_1 = jnp.concatenate([qkv[2], out_t], axis=1).astype(BF16)
        half_0, half_1 = (jnp.concatenate([half, vec_rows], axis=0) for half in (half_0, half_1))
        mlp_0, mlp_1 = up.astype(BF16), down_t.astype(BF16)
        keep_1, send_1 = jnp.where(on_query, half_0, half_1), jnp.where(on_query, half_1, half_0)
        keep_2, send_2 = jnp.where(on_query, mlp_0, mlp_1), jnp.where(on_query, mlp_1, mlp_0)
        got_1, got_2 = swap_cores(send_1), swap_cores(send_2)
        q_2, m_2 = jnp.where(on_query, keep_2, got_2), jnp.where(on_query, got_2, keep_2)

    first = nseq * (2 * t + branch)
    other = nseq * (2 * t + 1 - branch)
    own_crops = lax.dynamic_slice(crops[0], (first, 0, 0), (nseq, slots, width)).reshape(rows, width)
    got_crops = swap_cores(
        lax.dynamic_slice(crops[0], (other, 0, 0), (nseq, slots, width)).reshape(rows, width)
    )
    x_query = jnp.where(on_query, got_crops, own_crops)
    x_momentum = jnp.where(on_query, own_crops, got_crops)
    seg = lax.dynamic_slice(segment_ids, (0, first, 0), (2, nseq, slots))
    cot = lax.dynamic_slice(cotangent, (first, 0, 0), (nseq, slots, width)).reshape(rows, width)

    w1_shape, w2_shape = (2, tensors, width, width), (2, tensors, width, units)
    share = width // (2 * dp)
    if fine:
        both_ways = [(1, 0), (0, 1), (1, 1)]
        stack_q, masks = stack_peers(q_all, near)
        stack_1, stack_2 = stack_q[..., : width + 128], stack_q[..., width + 128 :]
        chunks = chunks_of(stack_1, masks, both_ways)
        plan = [spots for _, spots in chunks]
        args_1 = [block for block, _ in chunks]
        args_1 = args_1 + [swap_cores(block) for block in args_1]
        stack_2 = after(stack_2, args_1[1])
        m_all = after(m_all, stack_1)
        stack_m, _ = stack_peers(m_all, near)
        x_query = after(x_query, stack_2)
        own_2 = [block for block, _ in chunks_of(stack_2, masks, both_ways)]
        plan_1 = plan_2 = plan_m = plan
        extra_1, extra_2, extra_m = [], [(w2_shape, BF16)], [(w1_shape, BF16), (w2_shape, BF16)]
        scatter = (dp, 1)
        grads_1, grads_2 = (4, dp // 2, share, 4 * group + 128), (4, dp // 2, share, 2 * units)
    else:

        def finish(block):
            own = gather(block)
            got = swap_cores(own)
            return jnp.stack([jnp.where(on_query, own, got), jnp.where(on_query, got, own)])

        def finish_1(block):
            whole = finish(block)
            vec = jnp.sum(whole[0, 0, :, shard:].astype(F32), axis=0)
            return whole[:, :, :, :shard].reshape(w1_shape), vec

        wq_1, vec_q = finish_1(jnp.where(on_query, keep_1, got_1))
        wm_1, vec_m = finish_1(jnp.where(on_query, got_1, keep_1))
        wq_2, wm_2 = (finish(block).reshape(w2_shape) for block in (q_2, m_2))
        plan_1 = plan_2 = plan_m = scatter = None
        args_1, args_2, args_m = [wq_1, vec_q], [wq_2], [wm_1, wm_2, vec_m]
        extra_1 = extra_m = [((128, width), F32)]
        extra_2 = []
        grads_1, grads_2 = (tensors, width // 2, 4 * group + 128), (tensors, width // 2, 2 * units)

    head_block = ((heads, HD, rows), BF16)
    v_block = ((heads, HD + 16, rows), BF16)
    ctx_block = ((tensors, 2 * heads_g, HD, rows), BF16)
    bias_block = ((nseq, slots, slots), F32)
    score_block, pb_block = ((slots, slots), F32), ((heads, slots, slots), BF16)
    col_block = ((width, 128), F32)
    wide_f, wide_b = ((width, rows), F32), ((width, rows), BF16)
    kept = [(w1_shape, BF16), wide_f, ((8, rows), F32), wide_b, head_block, head_block, v_block]
    kept = kept + [((heads, 8, rows), F32), ctx_block] + [pb_block] * nseq
    attn_outs = call(
        functools.partial(query_attn_kernel, plan_1, shard),
        [wide_f, col_block] + kept,
        kept + [score_block] * nseq + [bias_block] + extra_1,
        (ids, x_query, seg[1], *args_1),
        smem=1,
        hbm_outs=len(kept),
        copies=len(kept),
    )
    if fine:
        own_2, attn_outs = after((own_2, attn_outs))
        args_2 = own_2 + [swap_cores(block) for block in own_2]
        cot = after(cot, stack_m)
        own_m = [block for block, _ in chunks_of(stack_m, masks, both_ways)]
    res, cols, *saved = attn_outs
    out_q, keep_g2, send_g2, d_res, vgrad = call(
        functools.partial(query_mlp_kernel, scatter, plan_2, shard),
        [((rows, width), BF16), (grads_2, BF16), (grads_2, BF16), wide_f, col_block],
        [wide_f, wide_f, wide_b, wide_b] + extra_2,
        (ids, res, cot, cols, *args_2),
        smem=1,
    )
    if fine:
        own_m, (out_q, keep_g2, send_g2, d_res, vgrad) = after((own_m, (out_q, keep_g2, send_g2, d_res, vgrad)))
        args_m = own_m + [swap_cores(block) for block in own_m]
        mlp_chip = chip_sum(keep_g2, send_g2)
        d_res = after(d_res, mlp_chip)
        pieces_2 = near_pieces(mlp_chip)
    crop_keep, crop_send, keep_g1, send_g1 = call(
        functools.partial(query_back_kernel, scatter, nseq),
        [((nseq, width // 2, slots), F32), ((nseq, width // 2, slots), BF16), (grads_1, BF16), (grads_1, BF16)],
        [head_block, ((tensors, 4 * heads_g, HD, rows), BF16), wide_b, col_block, wide_f]
        + [score_block] * nseq
        + [((slots, slots), BF16)] * nseq
        + [((8, slots), F32)] * nseq
        + kept,
        (ids, d_res, vgrad, cols, *saved),
        smem=1,
        hbm=len(kept),
        copies=len(kept),
    )
    if fine:
        pieces_2, (crop_keep, crop_send, keep_g1, send_g1) = after((pieces_2, (crop_keep, crop_send, keep_g1, send_g1)))
        mlp_near = add_all(mlp_chip[0].astype(F32), pieces_2)
        mlp_low = mlp_near.astype(BF16)
    got_half = swap_cores(crop_send)
    mine = (2, nseq, width // 2, slots)
    pair = jnp.zeros(mine, F32)
    pair = put(pair, crop_keep[None], (branch, 0, 0, 0))
    pair = put(pair, got_half.astype(F32)[None], (1 - branch, 0, 0, 0))
    if fine:
        attn_chip = chip_sum(keep_g1, send_g1)
        x_momentum = after(x_momentum, attn_chip, pair, mlp_low)
        pieces_1, far_2, far = near_pieces(attn_chip), far_pieces(mlp_low, 1), exchange(pair.astype(BF16), 0, 1)
    (out_m,) = call(
        functools.partial(momentum_kernel, plan_m, shard),
        [((rows, width), BF16)],
        [head_block, head_block, v_block, ctx_block, bias_block, wide_f] + extra_m + [pb_block] * nseq + [score_block] * nseq,
        (ids, x_momentum, seg[0], *([cols] if fine else []), *args_m),
        smem=1,
    )

    if fine:
        pieces_1, far_2, far, out_m = after((pieces_1, far_2, far, out_m))
        mlp_share = add_all(mlp_near[0], far_2)
        attn_near = add_all(attn_chip[0].astype(F32), pieces_1)
        attn_share = add_all(attn_near[0], far_pieces(attn_near.astype(BF16), 1))
    else:

        def shares(keep, send):
            both = chip_sum(keep, send)
            return scatter_sum(both.reshape(tensors, dp, share, both.shape[-1]))

        mlp_share, attn_share = shares(keep_g2, send_g2), shares(keep_g1, send_g1)
    qkv_grad = attn_share[:, : 3 * group].reshape(share, 3, group)
    vec_grad = attn_share[:, 3 * group : 3 * group + 6].T
    out_grad = attn_share[:, 3 * group + 64 : 4 * group + 64].T
    up_grad = mlp_share[:, :units]
    down_grad = mlp_share[:, units:].T

    if not fine:
        far = exchange(pair.astype(BF16), 0, 1)
    crop_grad = jnp.zeros((tensors,) + mine, F32)
    crop_grad = put(crop_grad, pair[None], (t, 0, 0, 0, 0))
    crop_grad = put(crop_grad, far.astype(F32)[None], (1 - t, 0, 0, 0, 0))
    crop_grad = crop_grad.reshape(sequences, width // 2, slots).transpose(0, 2, 1)

    far_q, far_m = exchange(out_q, 0, 1), exchange(out_m, 0, 1)
    got = swap_cores(jnp.where(on_query, out_q, out_m))
    got_far = swap_cores(jnp.where(on_query, far_q, far_m))
    (encoded,) = call(
        encoded_kernel,
        [((tensors, 2, rows, width), BF16)],
        [],
        (ids, out_q, far_q, out_m, far_m, got, got_far),
        smem=1,
    )
    encoded = encoded.reshape(1, sequences, slots, width)

    return (encoded, crop_grad, qkv_grad, out_grad, up_grad, down_grad, vec_grad[:2], vec_grad[2:])


def solution(mesh):
    placed = (
        P("branch", "dp", None, None),
        P(None, "dp", None),
        P("dp", None, None),
        P("branch", "dp", None, "tensor"),
        P("branch", "tensor", "dp"),
        P("branch", "dp", "tensor"),
        P("branch", "tensor", "dp"),
        P("branch", None, "dp"),
        P("branch", None, "dp"),
    )
    return jax.shard_map(
        on_device,
        mesh=mesh,
        in_specs=placed,
        out_specs=(
            P("branch", "dp", None, None),
            P("dp", None, "branch"),
            P(("branch", "dp"), None, "tensor"),
            P("tensor", ("branch", "dp")),
            P(("branch", "dp"), "tensor"),
            P("tensor", ("branch", "dp")),
            P(None, ("branch", "dp")),
            P(None, ("branch", "dp")),
        ),
        check_vma=False,
    )
```

time: 244 us -> 157 us (0.64)
  waiting for transfers between devices: 66.2 us -> 31 us
  starting transfers between devices: 65.4 us -> 44 us
  local copies, waits for them, and re-layouts: 38.3 us -> 17.5 us
  other arithmetic: 18 us -> 8.4 us
    ppermute x39 -> x30, waiting for transfers between devices: 66.2 us -> 25.9 us  [exchange(): return lax.ppermute(block, SPAN, pairs)]
    ppermute x39 -> x30, starting transfers between devices: 62.9 us -> 40.5 us  [exchange(): return lax.ppermute(block, SPAN, pairs)]
    dynamic_update_slice x39 -> x2, local copies, waits for them, and re-layouts: 16.3 us -> 0.11 us  [put(): return lax.dynamic_update_slice(whole, block, index)]
    ppermute x11 -> x19, waiting for transfers between devices: 0.03 us -> 5.14 us  [swap_cores(): return lax.ppermute(block, 'branch', [(0, 1), (1, 0)])]
    another operation x8 -> x3, other arithmetic: 4.51 us -> 0.75 us  [the longest x1 0.66 us: on_device(): ids = jnp.stack([branch, me, t]).astype(jnp.int32)]
    dynamic_slice x6 -> x0, local copies, waits for them, and re-layouts: 3.55 us -> none  [part(): return lax.dynamic_index_in_dim(whole, mine ^ k, number, keepdims=False)]
    convert_element_type x7 -> x5, other arithmetic: 7.08 us -> 3.87 us  [the longest x2 1.71 us: chip_sum(): return (keep.astype(F32) + swap_cores(send).astype(F32)).astype(BF16)]
    another operation x10 -> x0, local copies, waits for them, and re-layouts: 3.1 us -> none
  transfers between devices with their start and end apart: 50 -> 49, of which waited for: 23 -> 14; matrix products, arithmetic and copies ran while one was open for 18% -> 13% of each run, Pallas kernels for 15% -> 30%
where the time goes in v2:
time: 157 us; the launch traced here: 156 us
  Pallas kernels  53.8 us (34%)
  starting transfers between devices  44 us (28%)
  waiting for transfers between devices  31 us (20%)
  local copies, waits for them, and re-layouts  17.5 us (11%)
  other arithmetic  8.4 us (5%)
    pallas_call x7, Pallas kernels, call(): pl.pallas_call(kernel, grid=(1,) if stream else (), out_shape=[jax.ShapeD...  53.8 us
    ppermute x30, starting transfers between devices, exchange(): return lax.ppermute(block, SPAN, pairs)  40.5 us
    ppermute x30, waiting for transfers between devices, exchange(): return lax.ppermute(block, SPAN, pairs)  25.9 us
    unnamed x65, local copies, waits for them, and re-layouts  6.43 us
    ppermute x19, waiting for transfers between devices, swap_cores(): return lax.ppermute(block, 'branch', [(0, 1), (1, 0)])  5.14 us
    ppermute x19, starting transfers between devices, swap_cores(): return lax.ppermute(block, 'branch', [(0, 1), (1, 0)])  3.44 us
  transfers between devices with their start and end apart: 49, of which 14 were waited for; matrix products, arithmetic and copies ran while one was open for 13% of the time, Pallas kernels for 30%

profile of v2, /device:TPU:0, one launch (start us, length us, event | category | flops | bytes accessed | tf_op | source)
XLA Modules:
  0.0 155.8 jit_solution(4852180958670097035)
XLA Ops:
  1.3 1.9 %shard_map.152 = (bf16[48,1280]{1,0:T(8,128)(2,1)}, bf16[48,1280]{1,0:T(8,128)(2,1)}) custom-call(s32[3]{0:T(128)} %pad_add_fusion.b_ref.refs_0_.ids_ref, f32[3,48,192]{2,1,0:T(8,128)} %bitcast.117, f32[48,192]{1,0:T(8,128)} %bitcast.125, f32[48,768]{1,0:T(8,128)} %bitcast.118, f32[48,768]{1,0:T(8,128)} %bitcast.119, f32[2,48]{1,0:T(2,128)} %bitcast.127, ...), custom_call_target="tpu_custom_call" | custom-call | tf_op jit(solution)/shard_map/pallas_call | solution.py:435
  5.5 1.7 %shard_map.153 = (bf16[48,1280]{1,0:T(8,128)(2,1)}, bf16[48,1152]{1,0:T(8,128)(2,1)}) custom-call(s32[3]{0:T(128)} %pad_add_fusion.b_ref.refs_0_.ids_ref, bf16[48,1280]{1,0:T(8,128)(2,1)} %get-tuple-element.81.keep_ref, bf16[48,1280]{1,0:T(8,128)(2,1)} %copy-done.25), custom_call_target="tpu_custom_call" | custom-call | tf_op jit(solution)/shard_map/pallas_call | solution.py:435
  7.2 2.9 %collective-permute-start.1 = (bf16[48,1280]{1,0:T(8,128)(2,1)}, bf16[48,1280]{1,0:T(8,128)(2,1)S(1)}, u32[]{:S(2)}, u32[]{:S(2)}) collective-permute-start(bf16[48,1280]{1,0:T(8,128)(2,1)} %get-tuple-element.84), channel_id=1, source_target_pairs={{0,4},{1,5},{2,6},{3,7},{4,0},{5,1},{6,2},{7,3},{8,12},{9,13},{10,... | collective-permute-start | bytes 368648 | tf_op jit(solution)/shard_map/ppermute | solution.py:459
  10.1 2.6 %collective-permute-start.2 = (bf16[48,1280]{1,0:T(8,128)(2,1)}, bf16[48,1280]{1,0:T(8,128)(2,1)S(1)}, u32[]{:S(2)}, u32[]{:S(2)}) collective-permute-start(bf16[48,1280]{1,0:T(8,128)(2,1)} %get-tuple-element.84), channel_id=1, source_target_pairs={{0,8},{1,9},{2,10},{3,11},{4,12},{5,13},{6,14},{7,15},{8,0},{9,1},... | collective-permute-start | bytes 368648 | tf_op jit(solution)/shard_map/ppermute | solution.py:459
  14.0 1.7 %collective-permute-done.1 = bf16[48,1280]{1,0:T(8,128)(2,1)S(1)} collective-permute-done((bf16[48,1280]{1,0:T(8,128)(2,1)}, bf16[48,1280]{1,0:T(8,128)(2,1)S(1)}, u32[]{:S(2)}, u32[]{:S(2)}) %collective-permute-start.1) | collective-permute-done | bytes 122912 | tf_op jit(solution)/shard_map/ppermute | solution.py:459
  15.7 7.0 %collective-permute-done.2 = bf16[48,1280]{1,0:T(8,128)(2,1)S(1)} collective-permute-done((bf16[48,1280]{1,0:T(8,128)(2,1)}, bf16[48,1280]{1,0:T(8,128)(2,1)S(1)}, u32[]{:S(2)}, u32[]{:S(2)}) %collective-permute-start.2) | collective-permute-done | bytes 122912 | tf_op jit(solution)/shard_map/ppermute | solution.py:459
  22.7 1.6 collective-permute-start.10
  24.3 1.5 collective-permute-start.15
  26.3 3.9 %collective-permute-done.10.refs_4_ = bf16[4,48,512]{2,1,0:T(8,128)(2,1)} collective-permute-done((bf16[4,48,512]{2,1,0:T(8,128)(2,1)S(1)}, bf16[4,48,512]{2,1,0:T(8,128)(2,1)}, u32[]{:S(2)}, u32[]{:S(2)}) %collective-permute-start.10) | collective-permute-done | bytes 196640 | tf_op jit(solution)/shard_map/ppermute | solution.py:459
  31.5 2.0 %collective-permute-done.15.refs_5_ = bf16[4,48,512]{2,1,0:T(8,128)(2,1)} collective-permute-done((bf16[4,48,512]{2,1,0:T(8,128)(2,1)S(1)}, bf16[4,48,512]{2,1,0:T(8,128)(2,1)}, u32[]{:S(2)}, u32[]{:S(2)}) %collective-permute-start.15) | collective-permute-done | bytes 196640 | tf_op jit(solution)/shard_map/ppermute | solution.py:459
  37.2 3.1 %collective-permute-start.4 = (bf16[48,1152]{1,0:T(8,128)(2,1)}, bf16[48,1152]{1,0:T(8,128)(2,1)S(1)}, u32[]{:S(2)}, u32[]{:S(2)}) collective-permute-start(bf16[48,1152]{1,0:T(8,128)(2,1)} %get-tuple-element.85), channel_id=1, source_target_pairs={{0,4},{1,5},{2,6},{3,7},{4,0},{5,1},{6,2},{7,3},{8,12},{9,13},{10,... | collective-permute-start | bytes 331784 | tf_op jit(solution)/shard_map/ppermute | solution.py:459
  41.4 1.5 collective-permute-start.6
  43.9 9.2 %shard_map.154 = (f32[384,512]{1,0:T(8,128)}, f32[384,128]{1,0:T(8,128)}, bf16[2,2,384,384]{3,2,1,0:T(8,128)(2,1)}, f32[384,512]{1,0:T(8,128)}, f32[8,512]{1,0:T...) custom-call(s32[3]{0:T(128)} %pad_add_fusion.b_ref.refs_0_.ids_ref, ...), custom_call_target="tpu_custom_call" | custom-call | tf_op jit(solution)/shard_map/pallas_call | solution.py:435
  55.2 1.5 collective-permute-start.8
  60.4 12.5 %shard_map.155 = (bf16[512,384]{1,0:T(8,128)(2,1)}, bf16[4,4,24,1536]{3,2,1,0:T(8,128)(2,1)}, bf16[4,4,24,1536]{3,2,1,0:T(8,128)(2,1)}, f32[384,512]{1,0:T(8,128)}, f32[384,128]{1,0:T(8,128)}) custom-call(s32[3]{0:T(128)} %pad_add_fusion.b_ref.refs_0_.ids_ref, f32[384,512]{1,0:T(8,128)} %get-tuple-element.101.refs_1_, bf16[512,384]{1,0:T(8,128)(2,1)} %bitcast.107, ...), custom_call_target="tpu_custom_call" | custom-call | tf_op jit(solution)/shard_map/pallas_call | solution.py:435
  72.9 3.7 %collective-permute-done.8.refs_6_ = bf16[4,48,1152]{2,1,0:T(8,128)(2,1)S(1)} collective-permute-done((bf16[4,48,1152]{2,1,0:T(8,128)(2,1)S(1)}, bf16[4,48,1152]{2,1,0:T(8,128)(2,1)S(1)}, u32[]{:S(2)}, u32[]{:S(2)}) %collective-permute-start.8) | collective-permute-done | bytes 442400 | tf_op jit(solution)/shard_map/ppermute | solution.py:459
  76.7 3.0 %collective-permute-done.26 = bf16[4,4,24,1536]{3,2,1,0:T(8,128)(2,1)S(1)} collective-permute-done((bf16[4,4,24,1536]{3,2,1,0:T(8,128)(2,1)}, bf16[4,4,24,1536]{3,2,1,0:T(8,128)(2,1)S(1)}, u32[]{:S(2)}, u32[]{:S(2)}) %collective-permute-start.26) | collective-permute-done | bytes 1179680 | tf_op jit(solution)/shard_map/ppermute | solution.py:451
  79.7 1.5 add_convert_fusion
  82.2 1.5 collective-permute-start.27
  84.2 1.5 collective-permute-start.29
  86.2 11.4 %shard_map.156 = (f32[2,192,256]{2,1,0:T(8,128)}, bf16[2,192,256]{2,1,0:T(8,128)(2,1)}, bf16[4,4,24,896]{3,2,1,0:T(8,128)(2,1)}, bf16[4,4,24,896]{3,2,1,0:T(8,128)(2,1)}) custom-call(s32[3]{0:T(128)} %pad_add_fusion.b_ref.refs_0_.ids_ref, f32[384,512]{1,0:T(8,128)} %get-tuple-element.117.refs_1_, f32[384,128]{1,0:T(8,128)} %get-tuple-element.118.refs_2_, ...), custom_call_target="tpu_custom_call" | custom-call | tf_op jit(solution)/shard_map/pallas_call | solution.py:435
  102.0 1.6 %collective-permute-start.34 = (bf16[24,1536]{1,0:T(8,128)(2,1)S(1)}, bf16[24,1536]{1,0:T(8,128)(2,1)S(1)}, u32[]{:S(2)}, u32[]{:S(2)}) collective-permute-start(bf16[24,1536]{1,0:T(8,128)(2,1)S(1)} %get-tuple-element.186), channel_id=1, source_target_pairs={{0,4},{1,5},{2,6},{3,7},{4,0},{5,1},{6,2},{7,3},{8,12},{9,13},{10,... | collective-permute-start | bytes 221192 | tf_op jit(solution)/shard_map/ppermute | solution.py:459
  105.2 1.5 collective-permute-start.38
  112.7 14.2 %shard_map.157.m_ref = bf16[512,384]{1,0:T(8,128)(2,1)} custom-call(s32[3]{0:T(128)} %pad_add_fusion.b_ref.refs_0_.ids_ref, bf16[512,384]{1,0:T(8,128)(2,1)} %get-tuple-element.141.refs_1_, s32[2,256]{1,0:T(2,128)} %get-tuple-element.192.refs_2_, f32[384,128]{1,0:T(8,128)} %get-tuple-element.103.refs_3_, bf16[4,48,1152]{2,1,0:T(8,128)(2,1)} %copy-done.1, ...), custom_call_target="tpu_custom_call" | custom-call | tf_op jit(solution)/shard_map/pallas_call | solution.py:435
  127.0 2.1 %collective-permute-start.25 = (bf16[512,384]{1,0:T(8,128)(2,1)S(1)}, bf16[512,384]{1,0:T(8,128)(2,1)}, u32[]{:S(2)}, u32[]{:S(2)}) collective-permute-start(bf16[512,384]{1,0:T(8,128)(2,1)S(1)} %copy-done.3), channel_id=1, source_target_pairs={{0,1},{1,0},{2,3},{3,2},{4,5},{5,4},{6,7},{7,6},{8,9},{9,8},{10,11... | collective-permute-start | bytes 1179656 | tf_op jit(solution)/shard_map/ppermute | solution.py:459
  130.9 2.6 %collective-permute-start.47 = (bf16[24,896]{1,0:T(8,128)(2,1)S(1)}, bf16[24,896]{1,0:T(8,128)(2,1)S(1)}, u32[]{:S(2)}, u32[]{:S(2)}) collective-permute-start(bf16[24,896]{1,0:T(8,128)(2,1)S(1)} %get-tuple-element.189), channel_id=1, source_target_pairs={{0,8},{1,9},{2,10},{3,11},{4,12},{5,13},{6,14},{7,15},{8,0},{9,1},... | collective-permute-start | bytes 129032 | tf_op jit(solution)/shard_map/ppermute | solution.py:459
  135.8 3.5 %collective-permute-done.48 = bf16[24,896]{1,0:T(8,128)(2,1)S(1)} collective-permute-done((bf16[24,896]{1,0:T(8,128)(2,1)S(1)}, bf16[24,896]{1,0:T(8,128)(2,1)S(1)}, u32[]{:S(2)}, u32[]{:S(2)}) %collective-permute-start.48) | collective-permute-done | bytes 43040 | tf_op jit(solution)/shard_map/ppermute | solution.py:459
  140.6 1.6 reshape.47
  142.2 1.5 copy.20
  143.7 1.8 %collective-permute-done.43.m_far = bf16[512,384]{1,0:T(8,128)(2,1)} collective-permute-done((bf16[512,384]{1,0:T(8,128)(2,1)}, bf16[512,384]{1,0:T(8,128)(2,1)}, u32[]{:S(2)}, u32[]{:S(2)}) %collective-permute-start.43) | collective-permute-done | bytes 393248 | tf_op jit(solution)/shard_map/ppermute | solution.py:459
  145.5 1.8 %broadcast_select_fusion = bf16[512,384]{1,0:T(8,128)(2,1)} fusion(bf16[512,384]{1,0:T(8,128)(2,1)} %collective-permute-done.25.q_far, bf16[512,384]{1,0:T(8,128)(2,1)} %collective-permute-done.43.m_far, pred[]{:T(512)S(6)} %eq.3), kind=kLoop, calls=%fused_computation.12 | loop fusion | flops 196608 | bytes 1179649 | tf_op jit(solution)/shard_map/jit(_where)/select_n | solution.py:766
  152.9 2.9 %shard_map.158 = bf16[2,2,512,384]{3,2,1,0:T(8,128)(2,1)} custom-call(s32[3]{0:T(128)} %pad_add_fusion.b_ref.refs_0_.ids_ref, bf16[512,384]{1,0:T(8,128)(2,1)} %get-tuple-element.113.q_ref, bf16[512,384]{1,0:T(8,128)(2,1)} %collective-permute-done.25.q_far, bf16[512,384]{1,0:T(8,128)(2,1)} %shard_map.157.m_ref, ...), custom_call_target="tpu_custom_call" | custom-call | tf_op jit(solution)/shard_map/pallas_call | solution.py:435
  (171 shorter events, 42.3 us)
Async XLA Ops:
  7.2 8.5 %collective-permute-start.1 = (bf16[48,1280]{1,0:T(8,128)(2,1)}, bf16[48,1280]{1,0:T(8,128)(2,1)S(1)}, u32[]{:S(2)}, u32[]{:S(2)}) collective-permute-start(bf16[48,1280]{1,0:T(8,128)(2,1)} %get-tuple-element.84), channel_id=1, source_target_pairs={{0,4},{1,5},{2,6},{3,7},{4,0},{5,1},{6,2},{7,3},{8,12},{9,13},{10,... | collective-permute-start | bytes 368648 | tf_op jit(solution)/shard_map/ppermute | solution.py:459
  10.1 12.6 %collective-permute-start.2 = (bf16[48,1280]{1,0:T(8,128)(2,1)}, bf16[48,1280]{1,0:T(8,128)(2,1)S(1)}, u32[]{:S(2)}, u32[]{:S(2)}) collective-permute-start(bf16[48,1280]{1,0:T(8,128)(2,1)} %get-tuple-element.84), channel_id=1, source_target_pairs={{0,8},{1,9},{2,10},{3,11},{4,12},{5,13},{6,14},{7,15},{8,0},{9,1},... | collective-permute-start | bytes 368648 | tf_op jit(solution)/shard_map/ppermute | solution.py:459
  12.7 10.0 %collective-permute-start.3 = (bf16[48,1280]{1,0:T(8,128)(2,1)}, bf16[48,1280]{1,0:T(8,128)(2,1)S(1)}, u32[]{:S(2)}, u32[]{:S(2)}) collective-permute-start(bf16[48,1280]{1,0:T(8,128)(2,1)} %get-tuple-element.84), channel_id=1, source_target_pairs={{0,12},{1,13},{2,14},{3,15},{4,8},{5,9},{6,10},{7,11},{8,4},{9,5},... | collective-permute-start | bytes 368648 | tf_op jit(solution)/shard_map/ppermute | solution.py:459
  13.9 16.3 %collective-permute-start.14 = (bf16[512,384]{1,0:T(8,128)(2,1)S(1)}, bf16[512,384]{1,0:T(8,128)(2,1)S(1)}, u32[]{:S(2)}, u32[]{:S(2)}) collective-permute-start(bf16[512,384]{1,0:T(8,128)(2,1)S(1)} %bitcast.116), channel_id=1, source_target_pairs={{0,16},{16,0},{1,17},{17,1},{2,18},{18,2},{3,19},{19,3},{4,20},{20... | collective-permute-start | bytes 1179656 | tf_op jit(solution)/shard_map/ppermute | solution.py:451
  24.3 9.3 %collective-permute-start.15 = (bf16[4,48,512]{2,1,0:T(8,128)(2,1)S(1)}, bf16[4,48,512]{2,1,0:T(8,128)(2,1)}, u32[]{:S(2)}, u32[]{:S(2)}) collective-permute-start(bf16[4,48,512]{2,1,0:T(8,128)(2,1)S(1)} %pad_maximum_fusion.4.refs_3_), channel_id=1, source_target_pairs={{0,1},{1,0},{2,3},{3,2},{4,5},{5,4},{6,7},{7,6},{8,9},{9,8},{10,11... | collective-permute-start | bytes 589832 | tf_op jit(solution)/shard_map/ppermute | solution.py:459
  25.8 7.8 %collective-permute-start.16 = (bf16[4,48,512]{2,1,0:T(8,128)(2,1)S(1)}, bf16[4,48,512]{2,1,0:T(8,128)(2,1)}, u32[]{:S(2)}, u32[]{:S(2)}) collective-permute-start(bf16[4,48,512]{2,1,0:T(8,128)(2,1)S(1)} %pad_maximum_fusion.4.refs_3_), channel_id=1, source_target_pairs={{0,3},{1,2},{2,1},{3,0},{4,7},{5,6},{6,5},{7,4},{8,11},{9,10},{10,... | collective-permute-start | bytes 589832 | tf_op jit(solution)/shard_map/ppermute | solution.py:459
  26.3 7.8 %collective-permute-start.17 = (bf16[4,48,512]{2,1,0:T(8,128)(2,1)S(1)}, bf16[4,48,512]{2,1,0:T(8,128)(2,1)}, u32[]{:S(2)}, u32[]{:S(2)}) collective-permute-start(bf16[4,48,512]{2,1,0:T(8,128)(2,1)S(1)} %pad_maximum_fusion.4.refs_3_), channel_id=1, source_target_pairs={{0,16},{16,0},{1,17},{17,1},{2,18},{18,2},{3,19},{19,3},{4,20},{20... | collective-permute-start | bytes 589832 | tf_op jit(solution)/shard_map/ppermute | solution.py:451
  30.2 11.2 %collective-permute-start.11 = (bf16[4,48,768]{2,1,0:T(8,128)(2,1)S(1)}, bf16[4,48,768]{2,1,0:T(8,128)(2,1)S(1)}, u32[]{:S(2)}, u32[]{:S(2)}) collective-permute-start(bf16[4,48,768]{2,1,0:T(8,128)(2,1)S(1)} %pad_maximum_fusion.1.refs_4_), channel_id=1, source_target_pairs={{0,2},{1,3},{2,0},{3,1},{4,6},{5,7},{6,4},{7,5},{8,10},{9,11},{10,... | collective-permute-start | bytes 884744 | tf_op jit(solution)/shard_map/ppermute | solution.py:459
  34.1 19.0 %collective-permute-start.12 = (bf16[4,48,768]{2,1,0:T(8,128)(2,1)S(1)}, bf16[4,48,768]{2,1,0:T(8,128)(2,1)S(1)}, u32[]{:S(2)}, u32[]{:S(2)}) collective-permute-start(bf16[4,48,768]{2,1,0:T(8,128)(2,1)S(1)} %pad_maximum_fusion.1.refs_4_), channel_id=1, source_target_pairs={{0,1},{1,0},{2,3},{3,2},{4,5},{5,4},{6,7},{7,6},{8,9},{9,8},{10,11... | collective-permute-start | bytes 884744 | tf_op jit(solution)/shard_map/ppermute | solution.py:459
  35.3 17.9 %collective-permute-start.13 = (bf16[4,48,768]{2,1,0:T(8,128)(2,1)S(1)}, bf16[4,48,768]{2,1,0:T(8,128)(2,1)}, u32[]{:S(2)}, u32[]{:S(2)}) collective-permute-start(bf16[4,48,768]{2,1,0:T(8,128)(2,1)S(1)} %pad_maximum_fusion.1.refs_4_), channel_id=1, source_target_pairs={{0,3},{1,2},{2,1},{3,0},{4,7},{5,6},{6,5},{7,4},{8,11},{9,10},{10,... | collective-permute-start | bytes 884744 | tf_op jit(solution)/shard_map/ppermute | solution.py:459
  37.2 16.5 %collective-permute-start.4 = (bf16[48,1152]{1,0:T(8,128)(2,1)}, bf16[48,1152]{1,0:T(8,128)(2,1)S(1)}, u32[]{:S(2)}, u32[]{:S(2)}) collective-permute-start(bf16[48,1152]{1,0:T(8,128)(2,1)} %get-tuple-element.85), channel_id=1, source_target_pairs={{0,4},{1,5},{2,6},{3,7},{4,0},{5,1},{6,2},{7,3},{8,12},{9,13},{10,... | collective-permute-start | bytes 331784 | tf_op jit(solution)/shard_map/ppermute | solution.py:459
  40.4 13.3 %collective-permute-start.5 = (bf16[48,1152]{1,0:T(8,128)(2,1)}, bf16[48,1152]{1,0:T(8,128)(2,1)S(1)}, u32[]{:S(2)}, u32[]{:S(2)}) collective-permute-start(bf16[48,1152]{1,0:T(8,128)(2,1)} %get-tuple-element.85), channel_id=1, source_target_pairs={{0,8},{1,9},{2,10},{3,11},{4,12},{5,13},{6,14},{7,15},{8,0},{9,1},... | collective-permute-start | bytes 331784 | tf_op jit(solution)/shard_map/ppermute | solution.py:459
  41.4 12.3 %collective-permute-start.6 = (bf16[48,1152]{1,0:T(8,128)(2,1)}, bf16[48,1152]{1,0:T(8,128)(2,1)S(1)}, u32[]{:S(2)}, u32[]{:S(2)}) collective-permute-start(bf16[48,1152]{1,0:T(8,128)(2,1)} %get-tuple-element.85), channel_id=1, source_target_pairs={{0,12},{1,13},{2,14},{3,15},{4,8},{5,9},{6,10},{7,11},{8,4},{9,5},... | collective-permute-start | bytes 331784 | tf_op jit(solution)/shard_map/ppermute | solution.py:459
  53.8 19.1 %collective-permute-start.7 = (bf16[4,48,1152]{2,1,0:T(8,128)(2,1)S(1)}, bf16[4,48,1152]{2,1,0:T(8,128)(2,1)S(1)}, u32[]{:S(2)}, u32[]{:S(2)}) collective-permute-start(bf16[4,48,1152]{2,1,0:T(8,128)(2,1)S(1)} %pad_maximum_fusion.refs_4_), channel_id=1, source_target_pairs={{0,2},{1,3},{2,0},{3,1},{4,6},{5,7},{6,4},{7,5},{8,10},{9,11},{10,... | collective-permute-start | bytes 1327112 | tf_op jit(solution)/shard_map/ppermute | solution.py:459
  55.2 21.4 %collective-permute-start.8 = (bf16[4,48,1152]{2,1,0:T(8,128)(2,1)S(1)}, bf16[4,48,1152]{2,1,0:T(8,128)(2,1)S(1)}, u32[]{:S(2)}, u32[]{:S(2)}) collective-permute-start(bf16[4,48,1152]{2,1,0:T(8,128)(2,1)S(1)} %pad_maximum_fusion.refs_4_), channel_id=1, source_target_pairs={{0,1},{1,0},{2,3},{3,2},{4,5},{5,4},{6,7},{7,6},{8,9},{9,8},{10,11... | collective-permute-start | bytes 1327112 | tf_op jit(solution)/shard_map/ppermute | solution.py:459
  56.7 19.9 %collective-permute-start.9 = (bf16[4,48,1152]{2,1,0:T(8,128)(2,1)S(1)}, bf16[4,48,1152]{2,1,0:T(8,128)(2,1)S(1)}, u32[]{:S(2)}, u32[]{:S(2)}) collective-permute-start(bf16[4,48,1152]{2,1,0:T(8,128)(2,1)S(1)} %pad_maximum_fusion.refs_4_), channel_id=1, source_target_pairs={{0,3},{1,2},{2,1},{3,0},{4,7},{5,6},{6,5},{7,4},{8,11},{9,10},{10,... | collective-permute-start | bytes 1327112 | tf_op jit(solution)/shard_map/ppermute | solution.py:459
  82.2 15.4 %collective-permute-start.27 = (bf16[4,24,1536]{2,1,0:T(8,128)(2,1)}, bf16[4,24,1536]{2,1,0:T(8,128)(2,1)}, u32[]{:S(2)}, u32[]{:S(2)}) collective-permute-start(bf16[4,24,1536]{2,1,0:T(8,128)(2,1)} %get-tuple-element.178), channel_id=1, source_target_pairs={{0,1},{1,0},{2,3},{3,2},{4,5},{5,4},{6,7},{7,6},{8,9},{9,8},{10,11... | collective-permute-start | bytes 884744 | tf_op jit(solution)/shard_map/ppermute | solution.py:459
  83.7 14.1 %collective-permute-start.28 = (bf16[4,24,1536]{2,1,0:T(8,128)(2,1)}, bf16[4,24,1536]{2,1,0:T(8,128)(2,1)}, u32[]{:S(2)}, u32[]{:S(2)}) collective-permute-start(bf16[4,24,1536]{2,1,0:T(8,128)(2,1)} %get-tuple-element.177), channel_id=1, source_target_pairs={{0,2},{1,3},{2,0},{3,1},{4,6},{5,7},{6,4},{7,5},{8,10},{9,11},{10,... | collective-permute-start | bytes 884744 | tf_op jit(solution)/shard_map/ppermute | solution.py:459
  84.2 14.9 %collective-permute-start.29 = (bf16[4,24,1536]{2,1,0:T(8,128)(2,1)S(1)}, bf16[4,24,1536]{2,1,0:T(8,128)(2,1)}, u32[]{:S(2)}, u32[]{:S(2)}) collective-permute-start(bf16[4,24,1536]{2,1,0:T(8,128)(2,1)S(1)} %get-tuple-element.176), channel_id=1, source_target_pairs={{0,3},{1,2},{2,1},{3,0},{4,7},{5,6},{6,5},{7,4},{8,11},{9,10},{10,... | collective-permute-start | bytes 884744 | tf_op jit(solution)/shard_map/ppermute | solution.py:459
  85.7 18.1 %collective-permute-start.39 = (bf16[4,48,1152]{2,1,0:T(8,128)(2,1)S(1)}, bf16[4,48,1152]{2,1,0:T(8,128)(2,1)S(1)}, u32[]{:S(2)}, u32[]{:S(2)}) collective-permute-start(bf16[4,48,1152]{2,1,0:T(8,128)(2,1)S(1)} %pad_maximum_fusion.refs_4_), channel_id=1, source_target_pairs={{0,16},{16,0},{1,17},{17,1},{2,18},{18,2},{3,19},{19,3},{4,20},{20... | collective-permute-start | bytes 1327112 | tf_op jit(solution)/shard_map/ppermute | solution.py:451
  85.7 19.5 %collective-permute-start.40 = (bf16[4,48,1152]{2,1,0:T(8,128)(2,1)}, bf16[4,48,1152]{2,1,0:T(8,128)(2,1)}, u32[]{:S(2)}, u32[]{:S(2)}) collective-permute-start(bf16[4,48,1152]{2,1,0:T(8,128)(2,1)} %copy-done.8), channel_id=1, source_target_pairs={{0,16},{16,0},{1,17},{17,1},{2,18},{18,2},{3,19},{19,3},{4,20},{20... | collective-permute-start | bytes 1327112 | tf_op jit(solution)/shard_map/ppermute | solution.py:451
  97.6 9.9 %collective-permute-start.41 = (bf16[4,48,1152]{2,1,0:T(8,128)(2,1)S(1)}, bf16[4,48,1152]{2,1,0:T(8,128)(2,1)S(1)}, u32[]{:S(2)}, u32[]{:S(2)}) collective-permute-start(bf16[4,48,1152]{2,1,0:T(8,128)(2,1)S(1)} %copy-done.10), channel_id=1, source_target_pairs={{0,16},{16,0},{1,17},{17,1},{2,18},{18,2},{3,19},{19,3},{4,20},{20... | collective-permute-start | bytes 1327112 | tf_op jit(solution)/shard_map/ppermute | solution.py:451
  101.0 7.9 %collective-permute-start.42 = (bf16[4,48,1152]{2,1,0:T(8,128)(2,1)S(1)}, bf16[4,48,1152]{2,1,0:T(8,128)(2,1)S(1)}, u32[]{:S(2)}, u32[]{:S(2)}) collective-permute-start(bf16[4,48,1152]{2,1,0:T(8,128)(2,1)S(1)} %copy-done.12), channel_id=1, source_target_pairs={{0,16},{16,0},{1,17},{17,1},{2,18},{18,2},{3,19},{19,3},{4,20},{20... | collective-permute-start | bytes 1327112 | tf_op jit(solution)/shard_map/ppermute | solution.py:451
  102.0 7.5 %collective-permute-start.34 = (bf16[24,1536]{1,0:T(8,128)(2,1)S(1)}, bf16[24,1536]{1,0:T(8,128)(2,1)S(1)}, u32[]{:S(2)}, u32[]{:S(2)}) collective-permute-start(bf16[24,1536]{1,0:T(8,128)(2,1)S(1)} %get-tuple-element.186), channel_id=1, source_target_pairs={{0,4},{1,5},{2,6},{3,7},{4,0},{5,1},{6,2},{7,3},{8,12},{9,13},{10,... | collective-permute-start | bytes 221192 | tf_op jit(solution)/shard_map/ppermute | solution.py:459
  105.2 23.9 %collective-permute-start.38 = (bf16[2,2,192,256]{3,2,1,0:T(8,128)(2,1)}, bf16[2,2,192,256]{3,2,1,0:T(8,128)(2,1)S(1)}, u32[]{:S(2)}, u32[]{:S(2)}) collective-permute-start(bf16[2,2,192,256]{3,2,1,0:T(8,128)(2,1)} %convert_element_type.89), channel_id=1, source_target_pairs={{0,1},{1,0},{2,3},{3,2},{4,5},{5,4},{6,7},{7,6},{8,9},{9,8},{10,11... | collective-permute-start | bytes 1179656 | tf_op jit(solution)/shard_map/ppermute | solution.py:459
  107.5 19.5 %collective-permute-start.36 = (bf16[24,1536]{1,0:T(8,128)(2,1)S(1)}, bf16[24,1536]{1,0:T(8,128)(2,1)S(1)}, u32[]{:S(2)}, u32[]{:S(2)}) collective-permute-start(bf16[24,1536]{1,0:T(8,128)(2,1)S(1)} %get-tuple-element.184), channel_id=1, source_target_pairs={{0,12},{1,13},{2,14},{3,15},{4,8},{5,9},{6,10},{7,11},{8,4},{9,5},... | collective-permute-start | bytes 221192 | tf_op jit(solution)/shard_map/ppermute | solution.py:459
  108.9 20.1 %collective-permute-start.31 = (bf16[4,24,896]{2,1,0:T(8,128)(2,1)}, bf16[4,24,896]{2,1,0:T(8,128)(2,1)S(1)}, u32[]{:S(2)}, u32[]{:S(2)}) collective-permute-start(bf16[4,24,896]{2,1,0:T(8,128)(2,1)} %get-tuple-element.183), channel_id=1, source_target_pairs={{0,1},{1,0},{2,3},{3,2},{4,5},{5,4},{6,7},{7,6},{8,9},{9,8},{10,11... | collective-permute-start | bytes 516104 | tf_op jit(solution)/shard_map/ppermute | solution.py:459
  109.5 19.6 %collective-permute-start.32 = (bf16[4,24,896]{2,1,0:T(8,128)(2,1)}, bf16[4,24,896]{2,1,0:T(8,128)(2,1)S(1)}, u32[]{:S(2)}, u32[]{:S(2)}) collective-permute-start(bf16[4,24,896]{2,1,0:T(8,128)(2,1)} %get-tuple-element.182), channel_id=1, source_target_pairs={{0,2},{1,3},{2,0},{3,1},{4,6},{5,7},{6,4},{7,5},{8,10},{9,11},{10,... | collective-permute-start | bytes 516104 | tf_op jit(solution)/shard_map/ppermute | solution.py:459
  111.1 18.0 %collective-permute-start.33 = (bf16[4,24,896]{2,1,0:T(8,128)(2,1)}, bf16[4,24,896]{2,1,0:T(8,128)(2,1)S(1)}, u32[]{:S(2)}, u32[]{:S(2)}) collective-permute-start(bf16[4,24,896]{2,1,0:T(8,128)(2,1)} %get-tuple-element.181), channel_id=1, source_target_pairs={{0,3},{1,2},{2,1},{3,0},{4,7},{5,6},{6,5},{7,4},{8,11},{9,10},{10,... | collective-permute-start | bytes 516104 | tf_op jit(solution)/shard_map/ppermute | solution.py:459
  127.0 16.8 %collective-permute-start.25 = (bf16[512,384]{1,0:T(8,128)(2,1)S(1)}, bf16[512,384]{1,0:T(8,128)(2,1)}, u32[]{:S(2)}, u32[]{:S(2)}) collective-permute-start(bf16[512,384]{1,0:T(8,128)(2,1)S(1)} %copy-done.3), channel_id=1, source_target_pairs={{0,1},{1,0},{2,3},{3,2},{4,5},{5,4},{6,7},{7,6},{8,9},{9,8},{10,11... | collective-permute-start | bytes 1179656 | tf_op jit(solution)/shard_map/ppermute | solution.py:459
  129.1 16.5 %collective-permute-start.43 = (bf16[512,384]{1,0:T(8,128)(2,1)}, bf16[512,384]{1,0:T(8,128)(2,1)}, u32[]{:S(2)}, u32[]{:S(2)}) collective-permute-start(bf16[512,384]{1,0:T(8,128)(2,1)} %shard_map.157.m_ref), channel_id=1, source_target_pairs={{0,1},{1,0},{2,3},{3,2},{4,5},{5,4},{6,7},{7,6},{8,9},{9,8},{10,11... | collective-permute-start | bytes 1179656 | tf_op jit(solution)/shard_map/ppermute | solution.py:459
  135.5 16.7 %collective-permute-start.44 = (bf16[512,384]{1,0:T(8,128)(2,1)}, bf16[512,384]{1,0:T(8,128)(2,1)}, u32[]{:S(2)}, u32[]{:S(2)}) collective-permute-start(bf16[512,384]{1,0:T(8,128)(2,1)} %broadcast_select_fusion.1), channel_id=1, source_target_pairs={{0,16},{16,0},{1,17},{17,1},{2,18},{18,2},{3,19},{19,3},{4,20},{20... | collective-permute-start | bytes 1179656 | tf_op jit(solution)/shard_map/ppermute | solution.py:451
  (48 other events, 362.5 us)

commit v3 on v2

v3 whole, which is shorter than its diff:
```python
import functools
import math

import jax
import jax.numpy as jnp
from jax import lax
from jax.experimental import pallas as pl
from jax.experimental.pallas import tpu as pltpu
from jax.sharding import PartitionSpec as P

HD = 32
HEADS_STEP = 4
EPSILON = 1e-06
MASKED_SCORE = -1e30
LOG2E = 1.4426950408889634
BF16 = jnp.bfloat16
F32 = jnp.float32
PACE = 3600000


def nn(left, right):
    return lax.dot_general(left, right, (((1,), (0,)), ((), ())), preferred_element_type=F32)


def nt(left, right):
    return lax.dot_general(left, right, (((1,), (1,)), ((), ())), preferred_element_type=F32)


def tn(left, right):
    return lax.dot_general(left, right, (((0,), (0,)), ((), ())), preferred_element_type=F32)


def gelu_parts(v):
    a = jnp.abs(v)
    t = 1.0 / (1.0 + (0.3275911 / math.sqrt(2.0)) * a)
    bell = jnp.exp2(v * v * (-0.5 * LOG2E))
    poly = t * (
        0.5 * 0.254829592
        + t * (0.5 * -0.284496736 + t * (0.5 * 1.421413741 + t * (0.5 * -1.453152027 + t * (0.5 * 1.061405429))))
    )
    tail = poly * bell
    return jnp.where(v < 0, tail, 1.0 - tail), bell


def norm_cols(values, gain, shift):
    centred = values - jnp.mean(values, axis=0, keepdims=True)
    spread = jnp.mean(centred * centred, axis=0, keepdims=True)
    rstd = lax.rsqrt(spread + EPSILON)
    hat = centred * rstd
    return hat, rstd, hat * gain + shift


def norm_cols_back(upstream, hat, rstd, gain):
    t = upstream * gain
    return rstd * (t - jnp.mean(t, axis=0, keepdims=True) - hat * jnp.mean(t * hat, axis=0, keepdims=True))


def columns_of(query_ref, momentum_ref, scratch):
    scratch[...] = jnp.zeros_like(scratch)
    scratch[0:8, :] = query_ref[...]
    scratch[8:16, :] = momentum_ref[...]
    return scratch[...].T


def place_columns(plan, chunk_refs, shard, width, me, cols_ref):
    for ref, spots in zip(chunk_refs, plan):
        for index, (mask, u) in spots:
            if u == 0:
                rows = pl.ds(pl.multiple_of((me ^ mask) * shard, 16), shard)
                cols_ref[rows, :] = ref[index + (slice(None), slice(width, width + 128))].astype(F32)


def place_weights(plan, own_refs, got_refs, shard, ids, targets):
    b, me, t = ids
    for half, refs in ((b, own_refs), (1 - b, got_refs)):
        for ref, spots in zip(refs, plan):
            for index, (mask, u) in spots:
                rows = pl.ds(pl.multiple_of((me ^ mask) * shard, 16), shard)
                for target, to, start, wide in targets:
                    block = ref[index + (slice(0, shard), slice(start, start + wide))]
                    target[half, t ^ u, rows, to : to + wide] = block


def attend(x, segs, w1_ref, cols, q_ref, k_ref, v_ref, bias_ref, ctx_ref, pb_refs, inv_ref, score_refs, keep=None):
    tensors, width = w1_ref.shape[1], w1_ref.shape[2]
    group = width // tensors
    heads_g = group // HD
    nseq, slots = len(segs), segs[0].shape[1]
    x_t = x.astype(F32).T
    hat, rstd, normed = norm_cols(x_t, cols[:, 0:1], cols[:, 2:3])
    normed_low = normed.astype(BF16)
    if keep is not None:
        keep(hat, rstd, normed_low)
    rows = x_t.shape[1]
    for t in range(tensors):
        qk = tn(w1_ref[0, t], normed_low).astype(BF16)
        q_ref[t * heads_g : (t + 1) * heads_g] = qk[:group].reshape(heads_g, HD, rows)
        k_ref[t * heads_g : (t + 1) * heads_g] = qk[group:].reshape(heads_g, HD, rows)
        vo = tn(w1_ref[1, t], normed_low).astype(BF16)
        v_ref[t * heads_g : (t + 1) * heads_g, 0:HD] = vo[:group].reshape(heads_g, HD, rows)
    v_ref[:, HD:, :] = jnp.ones((v_ref.shape[0], v_ref.shape[1] - HD, rows), BF16)
    for s in range(nseq):
        across = jnp.broadcast_to(segs[s].astype(F32), (slots, slots))
        bias_ref[s] = jnp.where(across == across.T, 0.0, MASKED_SCORE)
    heads = tensors * heads_g
    parts = [slice(s * slots, (s + 1) * slots) for s in range(nseq)]
    ctx_ref[:, :heads_g] = jnp.zeros((tensors, heads_g, HD, rows), BF16)

    def score(h, s):
        score_refs[s][...] = tn(k_ref[h, :, parts[s]], q_ref[h, :, parts[s]])

    def soften(h, s):
        scores = score_refs[s][...] + bias_ref[s]
        top = jnp.max(scores, axis=0, keepdims=True)
        pb_refs[s][h] = jnp.exp2((scores - top) * (HD**-0.5 * LOG2E)).astype(BF16)

    def blend(h, s):
        both = nn(v_ref[h, :, parts[s]], pb_refs[s][h])
        inv = 1.0 / both[HD : HD + 1]
        if inv_ref is not None:
            inv_ref[h, :, parts[s]] = jnp.broadcast_to(inv, (8, slots))
        ctx_ref[h // heads_g, heads_g + h % heads_g, :, parts[s]] = (both[:HD] * inv).astype(BF16)

    def one_head(h, carry):
        for s in range(nseq):
            if s + 1 < nseq:
                score(h, s + 1)
            else:
                score(jnp.minimum(h + 1, heads - 1), 0)
            if s:
                blend(h, s - 1)
            else:
                blend(jnp.maximum(h - 1, 0), nseq - 1)
            soften(h, s)
        return carry

    score(0, 0)

    def some_heads(g, carry):
        for h in range(HEADS_STEP):
            one_head(g * HEADS_STEP + h, carry)
        return carry

    lax.fori_loop(0, heads // HEADS_STEP, some_heads, 0)
    blend(heads - 1, nseq - 1)
    attn = sum(nn(w1_ref[1, t], ctx_ref[t].reshape(width, rows)) for t in range(tensors))
    return x_t, attn


def pack_kernel(b_ref, *refs):
    far, keep_ref, send_ref, near, sems = refs[:6], refs[6], refs[7], refs[8:14], refs[14]
    copies = [pltpu.make_async_copy(there, here, sems.at[i]) for i, (there, here) in enumerate(zip(far, near))]
    for copy in copies:
        copy.start()
    qkv_ref, out_ref, up_ref, down_ref, gain_ref, bias_ref = near
    first = b_ref[0] == 0
    shard, width = up_ref.shape[0], 2 * out_ref.shape[1]
    for copy in copies:
        copy.wait()
    vec = jnp.concatenate([gain_ref[...], bias_ref[...], jnp.zeros((2, shard), F32)], axis=0)
    vec = jnp.concatenate([vec, jnp.zeros((8, 128 - shard), F32)], axis=1)
    none = jnp.zeros((8, 128), F32)
    vec = jnp.concatenate([jnp.where(first, vec, none), jnp.where(first, none, vec), jnp.zeros((112, 128), F32)], axis=0)
    vec = vec.T[:shard, :].astype(BF16)
    half_0 = jnp.concatenate([qkv_ref[0], qkv_ref[1]], axis=1).astype(BF16)
    half_1 = jnp.concatenate([qkv_ref[2], out_ref[...]], axis=1).astype(BF16)
    up, down = up_ref[...].astype(BF16), down_ref[...].astype(BF16)
    for ref, is_first in ((keep_ref, first), (send_ref, jnp.logical_not(first))):
        ref[:, :width] = jnp.where(is_first, half_0, half_1)
        ref[:, width : width + 128] = vec
        ref[:, width + 128 :] = jnp.where(is_first, up, down)


def split_kernel(width, b_ref, got_ref, far_ref, first_ref, second_ref, keep_ref, sems):
    copy = pltpu.make_async_copy(far_ref, keep_ref, sems.at[0])
    copy.start()
    first = b_ref[0] == 0
    got = got_ref[...]
    copy.wait()
    keep = keep_ref[...]
    query, momentum = jnp.where(first, keep, got), jnp.where(first, got, keep)
    units = second_ref.shape[1] // 2
    first_ref[:, :width] = query[:, :width]
    first_ref[:, width : width + 128] = keep[:, width : width + 128] + got[:, width : width + 128]
    first_ref[:, width + 128 :] = momentum[:, :width]
    second_ref[:, :units] = query[:, width + 128 :]
    second_ref[:, units:] = momentum[:, width + 128 :]


def attention_kernel(plan, shard, *refs):
    ids_ref, got_crops, seg_ref, refs = refs[0], refs[1], refs[2], refs[3:]
    ids = ids_ref[0], ids_ref[1], ids_ref[2]
    slots = seg_ref.shape[2]
    nseq = got_crops.shape[0] // slots
    if plan is None:
        w1_given, vec_q, w1_m, vec_m = refs[:4]
        refs = refs[4:]
    else:
        own, got = refs[: len(plan)], refs[len(plan) : 2 * len(plan)]
        refs = refs[2 * len(plan) :]
    crops_ref, res_ref, res_m_ref, cols_ref, refs = refs[0], refs[1], refs[2], refs[3], refs[4:]
    w1_ref, hat_ref, rstd_ref, normed_ref, q_ref, k_ref, v_ref, inv_ref, ctx_ref, *pb_refs = refs[: 9 + nseq]
    refs = refs[9 + nseq :]
    score_refs, pb_m, refs = refs[:nseq], refs[nseq : 2 * nseq], refs[2 * nseq :]
    q_m, k_m, v_m, ctx_m, bias_ref, mine_ref, spare, sems = refs
    first = nseq * (2 * ids[2] + ids[0])
    copy = pltpu.make_async_copy(crops_ref.at[pl.ds(first, nseq)], mine_ref, sems.at[0])
    copy.start()
    if plan is None:
        w1_ref[...] = w1_given[...]
        cols_ref[...] = columns_of(vec_q, vec_m, spare)
    else:
        wide, w1_m = w1_ref.shape[3], spare
        place_columns(plan, own, shard, wide, ids[1], cols_ref)
        place_weights(plan, own, got, shard, ids, [(w1_ref, 0, 0, wide), (w1_m, 0, wide + 128, wide)])
    cols = cols_ref[...]

    def keep(hat, rstd, normed):
        hat_ref[...] = hat
        rstd_ref[...] = jnp.broadcast_to(rstd, rstd_ref.shape)
        normed_ref[...] = normed

    copy.wait()

    def rows_of(encoder):
        mine = mine_ref[...].reshape(got_crops.shape)
        segs = [seg_ref[1 - encoder, pl.ds(first + s, 1), :] for s in range(nseq)]
        return jnp.where(ids[0] == encoder, got_crops[...], mine), segs

    x_t, attn = attend(
        *rows_of(0), w1_ref, cols, q_ref, k_ref, v_ref, bias_ref, ctx_ref, pb_refs, inv_ref, score_refs, keep
    )
    res_ref[...] = x_t + attn + cols[:, 3:4]
    cols = cols[:, 8:]
    x_t, attn = attend(*rows_of(1), w1_m, cols, q_m, k_m, v_m, bias_ref, ctx_m, pb_m, None, score_refs)
    res_m_ref[...] = x_t + attn + cols[:, 3:4]


def momentum_mlp_kernel(plan, shard, *refs):
    ids_ref, res_ref, cols_ref, query_ref, refs = refs[0], refs[1], refs[2], refs[3], refs[4:]
    ids = ids_ref[0], ids_ref[1], ids_ref[2]
    cols = cols_ref[...][:, 8:]
    if plan is None:
        w2_ref, out_ref, own_ref, send_ref, acc_ref = refs
    else:
        own, got = refs[: len(plan)], refs[len(plan) : 2 * len(plan)]
        out_ref, own_ref, send_ref, acc_ref, w2_ref = refs[2 * len(plan) :]
        place_weights(plan, own, got, shard, ids, [(w2_ref, 0, 0, w2_ref.shape[3])])
    res = res_ref[...]
    _, _, normed = norm_cols(res, cols[:, 1:2], cols[:, 4:5])
    rows_low = normed.T.astype(BF16)
    acc_ref[...] = res + cols[:, 5:6]
    tensors, units = w2_ref.shape[1], w2_ref.shape[3]
    chunk = 256
    parts = units // chunk

    def step(i, carry):
        t, c = i // parts, pl.ds(pl.multiple_of((i % parts) * chunk, chunk), chunk)
        pre = nn(rows_low, w2_ref[0, t, :, c])
        half, _ = gelu_parts(pre)
        acc_ref[...] += nt(w2_ref[1, t, :, c], (pre * half).astype(BF16))
        return carry

    lax.fori_loop(0, tensors * parts, step, 0)
    momentum, query = acc_ref[...].T.astype(BF16), query_ref[...]
    first = ids[0] == 0
    out_ref[...] = momentum
    own_ref[...] = jnp.where(first, momentum, query)
    send_ref[...] = jnp.where(first, query, momentum)


def store_grads(plan, ids, ref, t, cols, values):
    if plan is None:
        ref[t, :, cols] = values
        return
    dp, final = plan
    me, mine = ids[1], ids[2]
    share = values.shape[0] // dp
    size = final.bit_length()
    for i in range(dp):
        mask = me ^ i
        ref[(mask & final) * 2 + (mine ^ t), mask >> (size), :, cols] = values[i * share : (i + 1) * share]


def query_mlp_kernel(plan, chunks, shard, *refs):
    ids_ref, res_ref, cols_ref = refs[:3]
    cot_here, sems, refs = refs[-2], refs[-1], refs[3:-2]
    ids = ids_ref[0], ids_ref[1], ids_ref[2]
    b = ids[0]
    if chunks is None:
        w2_ref, cot_ref, refs = refs[0], refs[1], refs[2:]
    else:
        own, got = refs[: len(chunks)], refs[len(chunks) : 2 * len(chunks)]
        cot_ref, w2_ref, refs = refs[2 * len(chunks)], refs[-1], refs[2 * len(chunks) + 1 : -1]
    nseq = cot_here.shape[0]
    copy = pltpu.make_async_copy(cot_ref.at[pl.ds(nseq * (2 * ids[2] + b), nseq)], cot_here, sems.at[0])
    copy.start()
    if chunks is not None:
        place_weights(chunks, own, got, shard, ids, [(w2_ref, 0, 0, w2_ref.shape[3])])
    out_ref, keep_ref, send_ref, dres_ref, vgrad_ref, acc_ref, dn_ref, n2t_ref, gt_ref = refs
    cols = cols_ref[...]
    res = res_ref[...]
    hat, rstd, normed = norm_cols(res, cols[:, 1:2], cols[:, 4:5])
    n2t_ref[...] = normed.astype(BF16)
    rows_low = normed.T.astype(BF16)
    copy.wait()
    cot = cot_here[...].reshape(-1, cot_here.shape[2])
    cot_t = cot.astype(F32).T
    gt_ref[...] = cot_t.astype(BF16)
    acc_ref[...] = res + cols[:, 5:6]
    dn_ref[...] = jnp.zeros_like(dn_ref)
    tensors, width, units = w2_ref.shape[1], w2_ref.shape[2], w2_ref.shape[3]
    chunk = 256
    parts = units // chunk
    half_rows = width // 2

    def step(i, carry):
        t, off = i // parts, pl.multiple_of((i % parts) * chunk, chunk)
        c = pl.ds(off, chunk)
        up, down = w2_ref[0, t, :, c], w2_ref[1, t, :, c]
        pre = nn(rows_low, up)
        d_hidden = nn(cot, down)
        half, bell = gelu_parts(pre)
        hidden = (pre * half).astype(BF16)
        d_pre = (d_hidden * (half + pre * bell * (1.0 / math.sqrt(2.0 * math.pi)))).astype(BF16)
        acc_ref[...] += nt(down, hidden)
        dn_ref[...] += nt(up, d_pre)
        for ref, which in ((keep_ref, b), (send_ref, 1 - b)):
            rows = pl.ds(pl.multiple_of(which * half_rows, 16), half_rows)
            store_grads(plan, ids, ref, t, c, nn(n2t_ref[rows, :], d_pre).astype(BF16))
            later = pl.ds(pl.multiple_of(units + off, chunk), chunk)
            store_grads(plan, ids, ref, t, later, nn(gt_ref[rows, :], hidden).astype(BF16))
        return carry

    lax.fori_loop(0, tensors * parts, step, 0)
    out_ref[...] = acc_ref[...].T.astype(BF16)
    d_n2 = dn_ref[...]
    d_res = cot_t + norm_cols_back(d_n2, hat, rstd, cols[:, 1:2])
    dres_ref[...] = d_res
    lane = lax.broadcasted_iota(jnp.int32, vgrad_ref.shape, 1)
    total = jnp.zeros(vgrad_ref.shape, F32)
    for j, term in ((1, d_n2 * hat), (3, d_res), (4, d_n2), (5, cot_t)):
        total = total + jnp.where(lane == 64 + j, jnp.sum(term, axis=1, keepdims=True), 0.0)
    vgrad_ref[...] = total


def query_back_kernel(plan, nseq, *refs):
    ids_ref, dres_ref, vgrad_ref, cols_ref = refs[:4]
    w1_ref, hat_ref, rstd_ref, normed_ref, q_ref, k_ref, v_ref, inv_ref, ctx_ref, *pb_refs = refs[4 : 13 + nseq]
    refs = refs[13 + nseq :]
    crop_keep_ref, crop_send_ref, keep_ref, send_ref, dctx_ref, dproj_ref, dattn_ref, vg_ref, crop_ref = refs[:9]
    dp_refs, ds_refs, delta_refs = (refs[9 + i * nseq : 9 + (i + 1) * nseq] for i in range(3))
    ids = ids_ref[0], ids_ref[1], ids_ref[2]
    b = ids[0]
    tensors, width = w1_ref.shape[1], w1_ref.shape[2]
    group = width // tensors
    heads_g = group // HD
    heads, slots = pb_refs[0].shape[0], pb_refs[0].shape[1]
    rows = nseq * slots
    d_attn = dres_ref[...].astype(BF16)
    dattn_ref[...] = d_attn
    for t in range(tensors):
        vo = tn(w1_ref[1, t], d_attn).astype(BF16)
        dctx_ref[t * heads_g : (t + 1) * heads_g] = vo[group:].reshape(heads_g, HD, rows)
    dproj_ref[:, 3 * heads_g :] = jnp.zeros((tensors, heads_g, HD, rows), BF16)
    parts = [slice(s * slots, (s + 1) * slots) for s in range(nseq)]
    scale = HD**-0.5

    def d_weights(h, s):
        t, hh = h // heads_g, h % heads_g
        low_ctx = dctx_ref[h, :, parts[s]].astype(F32) * inv_ref[h, 0:1, parts[s]]
        delta = jnp.sum(low_ctx * ctx_ref[t, heads_g + hh, :, parts[s]].astype(F32), axis=0, keepdims=True)
        delta_refs[s][...] = jnp.broadcast_to(delta, (8, slots))
        low_ctx = low_ctx.astype(BF16)
        dp_refs[s][...] = tn(v_ref[h, 0:HD, parts[s]], low_ctx)
        dproj_ref[t, 2 * heads_g + hh, :, parts[s]] = nt(low_ctx, pb_refs[s][h]).astype(BF16)

    def harden(h, s):
        ds_refs[s][...] = (pb_refs[s][h].astype(F32) * (dp_refs[s][...] - delta_refs[s][0:1, :])).astype(BF16)

    def d_inputs(h, s):
        t, hh = h // heads_g, h % heads_g
        d_scores = ds_refs[s][...]
        dproj_ref[t, hh, :, parts[s]] = (nn(k_ref[h, :, parts[s]], d_scores) * scale).astype(BF16)
        dproj_ref[t, heads_g + hh, :, parts[s]] = (nt(q_ref[h, :, parts[s]], d_scores) * scale).astype(BF16)

    def one_head(h, carry):
        for s in range(nseq):
            if s + 1 < nseq:
                d_weights(h, s + 1)
            else:
                d_weights(jnp.minimum(h + 1, heads - 1), 0)
            if s:
                d_inputs(h, s - 1)
            else:
                d_inputs(jnp.maximum(h - 1, 0), nseq - 1)
            harden(h, s)
        return carry

    def some_heads(g, carry):
        for h in range(HEADS_STEP):
            one_head(g * HEADS_STEP + h, carry)
        return carry

    d_weights(0, 0)
    lax.fori_loop(0, heads // HEADS_STEP, some_heads, 0)
    d_inputs(heads - 1, nseq - 1)
    d_normed = jnp.zeros((width, rows), F32)
    for t in range(tensors):
        d_t = dproj_ref[t].reshape(4 * group, rows)
        d_normed += nn(w1_ref[0, t], d_t[: 2 * group]) + nn(w1_ref[1, t], d_t[2 * group :])
    hat = hat_ref[...]
    cols = cols_ref[...]
    crop_ref[...] = dres_ref[...] + norm_cols_back(d_normed, hat, rstd_ref[0:1, :], cols[:, 0:1])
    lane = lax.broadcasted_iota(jnp.int32, vgrad_ref.shape, 1)
    total = vgrad_ref[...]
    for j, term in ((0, d_normed * hat), (2, d_normed)):
        total = total + jnp.where(lane == 64 + j, jnp.sum(term, axis=1, keepdims=True), 0.0)
    vg_ref[...] = total
    half_rows = width // 2
    tile = (3 * group) // 128 * 128
    for ref, which in ((keep_ref, b), (send_ref, 1 - b)):
        part = pl.ds(pl.multiple_of(which * half_rows, 16), half_rows)
        left, right = normed_ref[part, :], dattn_ref[part, :]
        for t in range(tensors):
            d_t = dproj_ref[t].reshape(4 * group, rows)
            grads = nt(left, d_t[: 3 * group + 64])
            outs = nt(right, ctx_ref[t, heads_g:].reshape(group, rows))
            outs = jnp.concatenate([outs, jnp.zeros((half_rows, 64), F32)], axis=1)
            grads = jnp.concatenate([grads[:, :tile], grads[:, tile:] + vg_ref[part, :], outs], axis=1)
            store_grads(plan, ids, ref, t, slice(None), grads.astype(BF16))
    for s in range(nseq):
        part = slice(s * slots, (s + 1) * slots)
        crop_keep_ref[s] = crop_ref[pl.ds(pl.multiple_of(b * half_rows, 16), half_rows), part]
        crop_send_ref[s] = crop_ref[pl.ds(pl.multiple_of((1 - b) * half_rows, 16), half_rows), part].astype(BF16)


def chip_sum_kernel(keep_ref, got_ref, own_ref, *sends):
    total = keep_ref[...].astype(F32) + got_ref[...].astype(F32)
    own_ref[...] = total[0]
    for j, ref in enumerate(sends):
        ref[...] = total[1 + j].astype(BF16)


def half_sum_kernel(keep_ref, got_ref, own_ref, send_ref):
    half = own_ref.shape[0]
    own_ref[...] = keep_ref[:half].astype(F32) + got_ref[:half].astype(F32)
    send_ref[...] = (keep_ref[half:].astype(F32) + got_ref[half:].astype(F32)).astype(BF16)


def x_sum_kernel(own_ref, got_ref, keep_ref, send_ref):
    total = own_ref[...] + got_ref[...].astype(F32)
    keep_ref[...] = total[0]
    send_ref[...] = total[1].astype(BF16)


def near_sum_kernel(*refs):
    mlp, attn, own_ref, sends = refs[:2], refs[2:6], refs[6], refs[7:]
    wide = mlp[0].shape[2]
    for part, cols in ((mlp, slice(0, wide)), (attn, slice(wide, None))):
        total = part[0][...]
        for ref in part[1:]:
            total = total + ref[...].astype(F32)
        own_ref[:, cols] = total[0]
        for k, ref in enumerate(sends):
            ref[:, cols] = total[1 + k].astype(BF16)


def shares_kernel(units, group, *refs):
    own_ref, got, (qkv_ref, out_ref, up_ref, down_ref, gain_ref, bias_ref) = refs[0], refs[1:-6], refs[-6:]
    total = own_ref[...]
    for ref in got:
        total = total + ref[...].astype(F32)
    up_ref[...] = total[:, :units]
    down_ref[...] = total[:, units : 2 * units]
    attn = total[:, 2 * units :]
    for j in range(3):
        qkv_ref[j] = attn[:, j * group : (j + 1) * group]
    tile = 3 * group // 128 * 128
    vec = attn[:, tile : tile + 128]
    share = vec.shape[0]
    vec = jnp.concatenate([vec, jnp.zeros((128 - share, 128), F32)], axis=0).T
    gain_ref[...] = vec[64:66, :share]
    bias_ref[...] = vec[66:70, :share]
    out_ref[...] = attn[:, tile + 128 : tile + 128 + group]


def crop_pair_kernel(ids_ref, keep_ref, got_ref, pair_ref):
    b = ids_ref[0]
    pair_ref[b] = keep_ref[...].astype(BF16)
    pair_ref[1 - b] = got_ref[...]


def crop_kernel(ids_ref, keep_ref, got_ref, far_ref, out_ref):
    b, t = ids_ref[0], ids_ref[2]
    out_ref[t, b] = keep_ref[...]
    out_ref[t, 1 - b] = got_ref[...].astype(F32)
    out_ref[1 - t] = far_ref[...].astype(F32)


def pick_kernel(ids_ref, query_ref, momentum_ref, own_ref, send_ref):
    first = ids_ref[0] == 0
    own_ref[...] = jnp.where(first, momentum_ref[...], query_ref[...])
    send_ref[...] = jnp.where(first, query_ref[...], momentum_ref[...])


def encoded_kernel(ids_ref, own_ref, own_far, got_ref, got_far, out_ref, sems):
    b, t = ids_ref[0], ids_ref[2]
    places = ((own_ref, t, b), (own_far, 1 - t, b), (got_ref, t, 1 - b), (got_far, 1 - t, 1 - b))
    copies = [pltpu.make_async_copy(part, out_ref.at[i, j], sems.at[n]) for n, (part, i, j) in enumerate(places)]
    for copy in copies:
        copy.start()
    for copy in copies:
        copy.wait()


def call(kernel, out_shapes, scratch, args, smem=0, hbm=0, hbm_outs=0, copies=0, stream=False, limit=24):
    place, hold = pl.BlockSpec(memory_space=pltpu.VMEM), pl.BlockSpec(memory_space=pltpu.HBM)
    inner = args[smem : len(args) - hbm]
    if stream:
        specs = [pl.BlockSpec(x.shape, lambda i, n=x.ndim: (0,) * n) for x in inner]
    else:
        specs = [place] * len(inner)
    return pl.pallas_call(
        kernel,
        grid=(1,) if stream else (),
        out_shape=[jax.ShapeDtypeStruct(s, d) for s, d in out_shapes],
        in_specs=[pl.BlockSpec(memory_space=pltpu.SMEM)] * smem + specs + [hold] * hbm,
        out_specs=[place] * (len(out_shapes) - hbm_outs) + [hold] * hbm_outs,
        scratch_shapes=[pltpu.VMEM(s, d) for s, d in scratch]
        + ([pltpu.SemaphoreType.DMA((copies,))] if copies else []),
        compiler_params=pltpu.CompilerParams(vmem_limit_bytes=limit * 1024 * 1024),
    )(*args)


SPAN = ("dp", "tensor")


def swap_cores(block):
    return lax.ppermute(block, "branch", [(0, 1), (1, 0)])


def exchange(block, dp_mask, t_mask):
    dp, tensors = lax.axis_size("dp"), lax.axis_size("tensor")
    pairs = [
        (i * tensors + t, (i ^ dp_mask) * tensors + (t ^ t_mask)) for i in range(dp) for t in range(tensors)
    ]
    return lax.ppermute(block, SPAN, pairs)


def after(value, *deps):
    return lax.optimization_barrier((value, *deps))[0]


def dp_groups():
    bits = lax.axis_size("dp").bit_length() - 1
    groups, high = [], bits
    while high >= 2:
        high -= 2
        groups.append((high, 4))
    last = (0, 2) if high == 1 else None
    return groups, last


def put(whole, block, index):
    return lax.dynamic_update_slice(whole, block, index)


def gather(block):
    groups, last = dp_groups()
    me, t = lax.axis_index("dp"), lax.axis_index("tensor")
    tensors = lax.axis_size("tensor")
    for number, (shift, size) in enumerate(groups):
        lead, tail = block.shape[:number], block.shape[number:]
        whole = jnp.zeros(lead + (size,) + tail, block.dtype)
        mine = (me >> shift) & (size - 1)
        pieces = [(0, block)] + [(k, exchange(block, k << shift, 0)) for k in range(1, size)]
        for k, piece in pieces:
            whole = put(whole, jnp.expand_dims(piece, number), (0,) * number + (mine ^ k,) + (0,) * len(tail))
        block = whole
    lead, tail = block.shape[: len(groups)], block.shape[len(groups) :]
    size = last[1] if last else 1
    mine = me & (size - 1)
    whole = jnp.zeros((tensors,) + lead + (size,) + tail, block.dtype)
    for k in range(size):
        for u in range(tensors):
            piece = block if k == u == 0 else exchange(block, k, u)
            piece = jnp.expand_dims(jnp.expand_dims(piece, len(lead)), 0)
            whole = put(whole, piece, (t ^ u,) + (0,) * len(lead) + (mine ^ k,) + (0,) * len(tail))
    return whole.reshape((tensors, lax.axis_size("dp")) + tail)


def scatter_sum(block):
    groups, last = dp_groups()
    me, t = lax.axis_index("dp"), lax.axis_index("tensor")
    tensors = lax.axis_size("tensor")
    tail = block.shape[2:]
    size = last[1] if last else 1
    lead = tuple(g[1] for g in groups)
    block = block.reshape((tensors,) + lead + (size,) + tail)
    mine = me & (size - 1)

    def take(k, u):
        start = (t ^ u,) + (0,) * len(lead) + (mine ^ k,) + (0,) * len(tail)
        piece = lax.dynamic_slice(block, start, (1,) + lead + (1,) + tail)
        return piece.reshape(lead + tail)

    total = take(0, 0).astype(F32)
    for k in range(size):
        for u in range(tensors):
            if k or u:
                total = total + exchange(take(k, u), k, u).astype(F32)
    for number in reversed(range(len(groups))):
        shift, size = groups[number]
        mine = (me >> shift) & (size - 1)
        low = total.astype(BF16)

        def part(k, whole=low, number=number, mine=mine):
            return lax.dynamic_index_in_dim(whole, mine ^ k, number, keepdims=False)

        total = part(0, total).astype(F32)
        for k in range(1, size):
            total = total + exchange(part(k), k << shift, 0).astype(F32)
    return total


def stack_peers(block, stage):
    return jnp.stack([block] + [exchange(block, *peer) for peer in stage]), [(0, 0)] + stage


def chunks_of(block, masks, stage):
    pieces = [((0, 0), block)] + [(peer, exchange(block, *peer)) for peer in stage]
    return [
        (piece, [((j,), (m ^ peer[0], u ^ peer[1])) for j, (m, u) in enumerate(masks)]) for peer, piece in pieces
    ]


def gathered(shards, on_query, me, tensors, width, units):
    qkv, out_t, up, down_t, gains, biases = shards
    shard = up.shape[0]
    small = jnp.concatenate([gains, biases], axis=0).astype(BF16)
    vec_rows = put(jnp.zeros((8, width), BF16), small, (0, me * shard))
    half_0 = jnp.concatenate([qkv[0], qkv[1]], axis=1).astype(BF16)
    half_1 = jnp.concatenate([qkv[2], out_t], axis=1).astype(BF16)
    half_0, half_1 = (jnp.concatenate([half, vec_rows], axis=0) for half in (half_0, half_1))
    mlp_0, mlp_1 = up.astype(BF16), down_t.astype(BF16)

    def finish(first, second):
        keep, got = jnp.where(on_query, first, second), swap_cores(jnp.where(on_query, second, first))
        both = []
        for block in (jnp.where(on_query, keep, got), jnp.where(on_query, got, keep)):
            own = gather(block)
            other = swap_cores(own)
            both.append(jnp.stack([jnp.where(on_query, own, other), jnp.where(on_query, other, own)]))
        return both

    def parts_of(whole):
        vec = jnp.sum(whole[0, 0, :, shard:].astype(F32), axis=0)
        return whole[:, :, :, :shard].reshape(2, tensors, width, width), vec

    (wq_1, vec_q), (wm_1, vec_m) = (parts_of(whole) for whole in finish(half_0, half_1))
    wq_2, wm_2 = (whole.reshape(2, tensors, width, units) for whole in finish(mlp_0, mlp_1))
    return [wq_1, vec_q, wm_1, vec_m], [wq_2], [wm_2]


def on_device(
    crops, segment_ids, cotangent, qkv_weight, out_weight, up_weight, down_weight, gain_rows, biases
):
    branch, me, t = lax.axis_index("branch"), lax.axis_index("dp"), lax.axis_index("tensor")
    dp, tensors = lax.axis_size("dp"), lax.axis_size("tensor")
    on_query = branch == 0
    _, sequences, slots, width = crops.shape
    nseq = sequences // (2 * tensors)
    rows = nseq * slots
    shard = qkv_weight.shape[1]
    group = out_weight.shape[1]
    units = up_weight.shape[2]
    heads = tensors * group // HD
    heads_g = group // HD
    share = width // (2 * dp)
    ids = jnp.stack([branch, me, t]).astype(jnp.int32)
    fine = tensors == 2 and dp == 8 and shard % 16 == 0
    near = [(k << 1, 0) for k in range(1, 4)]
    both_ways = [(1, 0), (0, 1), (1, 1)]

    w1_shape, w2_shape = (2, tensors, width, width), (2, tensors, width, units)
    head_block = ((heads, HD, rows), BF16)
    v_block = ((heads, HD + 16, rows), BF16)
    ctx_block = ((tensors, 2 * heads_g, HD, rows), BF16)
    bias_block = ((nseq, slots, slots), F32)
    score_block, pb_block = ((slots, slots), F32), ((heads, slots, slots), BF16)
    col_block, vec_block = ((width, 128), F32), ((128, width), F32)
    crop_block = ((nseq, slots, width), BF16)
    wide_f, wide_b = ((width, rows), F32), ((width, rows), BF16)
    kept = [(w1_shape, BF16), wide_f, ((8, rows), F32), wide_b, head_block, head_block, v_block]
    kept = kept + [((heads, 8, rows), F32), ctx_block] + [pb_block] * nseq
    grads_1, grads_2 = (tensors, width // 2, 4 * group + 128), (tensors, width // 2, 2 * units)
    scatter = None
    if fine:
        grads_1, grads_2 = (4, dp // 2, share, grads_1[2]), (4, dp // 2, share, grads_2[2])
        scatter = (dp, 1)

    def attention(plan, weights, got_crops):
        return call(
            functools.partial(attention_kernel, plan, shard),
            [wide_f, wide_f, col_block] + kept,
            [score_block] * nseq
            + [pb_block] * nseq
            + [head_block, head_block, v_block, ctx_block, bias_block, crop_block]
            + [(w1_shape, BF16) if plan else vec_block],
            (ids, got_crops, segment_ids, *weights, crops[0]),
            smem=1,
            hbm=1,
            copies=1,
        )

    def query_mlp(plan, weights, res, cols):
        return call(
            functools.partial(query_mlp_kernel, scatter, plan, shard),
            [((rows, width), BF16), (grads_2, BF16), (grads_2, BF16), wide_f, col_block],
            [wide_f, wide_f, wide_b, wide_b] + ([(w2_shape, BF16)] if plan else []) + [crop_block],
            (ids, res, cols, *weights, cotangent),
            smem=1,
            hbm=1,
            copies=1,
        )

    def query_back(d_res, vgrad, cols, saved):
        return call(
            functools.partial(query_back_kernel, scatter, nseq),
            [((nseq, width // 2, slots), F32), ((nseq, width // 2, slots), BF16), (grads_1, BF16), (grads_1, BF16)],
            [head_block, ((tensors, 4 * heads_g, HD, rows), BF16), wide_b, col_block, wide_f]
            + [score_block] * nseq
            + [((slots, slots), BF16)] * nseq
            + [((8, slots), F32)] * nseq,
            (ids, d_res, vgrad, cols, *saved),
            smem=1,
        )

    def momentum_mlp(plan, weights, res_m, cols, out_q):
        return call(
            functools.partial(momentum_mlp_kernel, plan, shard),
            [((rows, width), BF16)] * 3,
            [wide_f] + ([(w2_shape, BF16)] if plan else []),
            (ids, res_m, cols, out_q, *weights),
            smem=1,
        )

    shards = (
        qkv_weight[0].transpose(1, 0, 2),
        out_weight[0].T,
        up_weight[0],
        down_weight[0].T,
        gain_rows[0],
        biases[0],
    )
    other = nseq * (2 * t + 1 - branch)
    send_crops = lax.dynamic_slice(crops[0], (other, 0, 0), (nseq, slots, width)).reshape(rows, width)

    if fine:
        block = ((shard, width + 128 + units), BF16)
        keep, send = call(
            pack_kernel, [block] * 2, [(x.shape, F32) for x in shards], (ids, *shards), smem=1, hbm=6, copies=6, limit=56
        )
        block_1, block_2 = call(
            functools.partial(split_kernel, width),
            [((shard, 2 * width + 128), BF16), ((shard, 2 * units), BF16)],
            [block],
            (ids, swap_cores(send), keep),
            smem=1,
            hbm=1,
            copies=1,
        )
        masks = [(0, 0)] + near
        plan = [[((j,), (m ^ n, u)) for j, (m, _) in enumerate(masks)] for n, u in [(0, 0)] + both_ways]
        got_crops = swap_cores(send_crops)
        far_1 = [exchange(block_1, *peer) for peer in near]
        stack_1, got_crops = after((jnp.stack([block_1, *far_1]), got_crops))
        own_1 = [stack_1] + [exchange(stack_1, *peer) for peer in both_ways]
        got_1 = [swap_cores(x) for x in own_1]
        parts = [block_2] + [exchange(block_2, *peer) for peer in near]
        stack_q, stack_m = (jnp.stack([x[..., cols] for x in parts]) for cols in (slice(0, units), slice(units, None)))
        own_q = [stack_q] + [exchange(stack_q, *peer) for peer in both_ways]
        res, res_m, cols, *saved = attention(plan, own_1 + got_1, after(got_crops, stack_q, stack_m))
        own_q, res, res_m, stack_m = after((own_q, res, res_m, stack_m))
        got_q = [swap_cores(x) for x in own_q]
        own_m = [stack_m] + [exchange(stack_m, *peer) for peer in both_ways]
        out_q, keep_g2, send_g2, d_res, vgrad = query_mlp(plan, own_q + got_q, res, cols)
        own_m, out_q, keep_g2, send_g2, d_res, vgrad = after((own_m, out_q, keep_g2, send_g2, d_res, vgrad))
        got_m = [swap_cores(x) for x in own_m]

        part = (2, dp // 2, share, 2 * units)
        mlp_own, mlp_send = call(half_sum_kernel, [(part, F32), (part, BF16)], [], (keep_g2, swap_cores(send_g2)))
        mlp_got = exchange(mlp_send, 1, 0)
        far_q = exchange(out_q, 0, 1)
        res_m = after(res_m, mlp_own)
        out_m, out_own, out_send = momentum_mlp(plan, own_m + got_m, res_m, cols, out_q)
        far_q, out_m, out_send = after((far_q, out_m, out_send))
        far_m = exchange(out_m, 0, 1)
        crop_keep, crop_send, keep_g1, send_g1 = query_back(after(d_res, out_m), vgrad, cols, saved)
        mlp_got, far_m, crop_send, send_g1 = after((mlp_got, far_m, crop_send, send_g1))
        part = (dp // 2, share, 2 * units)
        mlp_own, mlp_send = call(x_sum_kernel, [(part, F32), (part, BF16)], [], (mlp_own, mlp_got))
        mlp_got = exchange(mlp_send, 0, 1)
        part = (dp // 2, share, grads_1[3])
        attn_own, *attn_sends = call(
            chip_sum_kernel, [(part, F32)] + [(part, BF16)] * 3, [], (keep_g1, swap_cores(send_g1))
        )
        attn_got = [exchange(x, *peer) for x, peer in zip(attn_sends, [(0, 1), (1, 0), (1, 1)])]
        half = (nseq, width // 2, slots)
        crop_got = swap_cores(crop_send)
        (pair,) = call(crop_pair_kernel, [((2, *half), BF16)], [], (ids, crop_keep, crop_got), smem=1)
        attn_got, mlp_got, pair = after((attn_got, mlp_got, pair))
        crop_far = exchange(pair, 0, 1)
        wide = 2 * units + grads_1[3]
        own, *sends = call(
            near_sum_kernel,
            [((share, wide), F32)] + [((share, wide), BF16)] * 3,
            [],
            (mlp_own, mlp_got, attn_own, *attn_got),
        )
        got = [exchange(x, *peer) for x, peer in zip(sends, near)]
        qkv_grad, out_grad, up_grad, down_grad, gain_grad, bias_grad = call(
            functools.partial(shares_kernel, units, group),
            [
                ((3, share, group), F32),
                ((share, group), F32),
                ((share, units), F32),
                ((share, units), F32),
                ((2, share), F32),
                ((4, share), F32),
            ],
            [],
            (own, *got),
        )
        qkv_grad, out_grad, down_grad = qkv_grad.transpose(1, 0, 2), out_grad.T, down_grad.T
        (crop_grad,) = call(
            crop_kernel, [((tensors, 2, *half), F32)], [], (ids, crop_keep, crop_got, crop_far), smem=1
        )
        crop_grad = crop_grad.reshape(sequences, width // 2, slots).transpose(0, 2, 1)
        far_own, far_send = call(pick_kernel, [((rows, width), BF16)] * 2, [], (ids, far_q, far_m), smem=1)
        (encoded,) = call(
            encoded_kernel,
            [((tensors, 2, rows, width), BF16)],
            [],
            (ids, out_own, far_own, swap_cores(out_send), swap_cores(far_send)),
            smem=1,
            hbm=4,
            hbm_outs=1,
            copies=4,
        )
        encoded = encoded.reshape(1, sequences, slots, width)
        return (encoded, crop_grad, qkv_grad, out_grad, up_grad, down_grad, gain_grad, bias_grad)

    weights_1, weights_2, weights_4 = gathered(shards, on_query, me, tensors, width, units)
    got_crops = swap_cores(send_crops)
    res, res_m, cols, *saved = attention(None, weights_1, got_crops)
    out_q, keep_g2, send_g2, d_res, vgrad = query_mlp(None, weights_2, res, cols)
    crop_keep, crop_send, keep_g1, send_g1 = query_back(d_res, vgrad, cols, saved)
    _, out_own, out_send = momentum_mlp(None, weights_4, res_m, cols, out_q)

    def shares(keep, send):
        both = (keep.astype(F32) + swap_cores(send).astype(F32)).astype(BF16)
        return scatter_sum(both.reshape(tensors, dp, share, both.shape[-1]))

    mlp_share, attn_share = shares(keep_g2, send_g2), shares(keep_g1, send_g1)
    qkv_grad = attn_share[:, : 3 * group].reshape(share, 3, group)
    vec_grad = attn_share[:, 3 * group : 3 * group + 6].T
    out_grad = attn_share[:, 3 * group + 64 : 4 * group + 64].T
    up_grad, down_grad = mlp_share[:, :units], mlp_share[:, units:].T

    mine = (2, nseq, width // 2, slots)
    pair = jnp.zeros(mine, F32)
    pair = put(pair, crop_keep[None], (branch, 0, 0, 0))
    pair = put(pair, swap_cores(crop_send).astype(F32)[None], (1 - branch, 0, 0, 0))
    far = exchange(pair.astype(BF16), 0, 1)
    crop_grad = jnp.zeros((tensors,) + mine, F32)
    crop_grad = put(crop_grad, pair[None], (t, 0, 0, 0, 0))
    crop_grad = put(crop_grad, far.astype(F32)[None], (1 - t, 0, 0, 0, 0))
    crop_grad = crop_grad.reshape(sequences, width // 2, slots).transpose(0, 2, 1)

    pair = jnp.zeros((2, rows, width), BF16)
    pair = put(put(pair, out_own[None], (branch, 0, 0)), swap_cores(out_send)[None], (1 - branch, 0, 0))
    encoded = jnp.zeros((tensors, 2, rows, width), BF16)
    encoded = put(encoded, pair[None], (t, 0, 0, 0))
    encoded = put(encoded, exchange(pair, 0, 1)[None], (1 - t, 0, 0, 0))
    encoded = encoded.reshape(1, sequences, slots, width)

    return (encoded, crop_grad, qkv_grad, out_grad, up_grad, down_grad, vec_grad[:2], vec_grad[2:])


def solution(mesh):
    placed = (
        P("branch", "dp", None, None),
        P(None, "dp", None),
        P("dp", None, None),
        P("branch", "dp", None, "tensor"),
        P("branch", "tensor", "dp"),
        P("branch", "dp", "tensor"),
        P("branch", "tensor", "dp"),
        P("branch", None, "dp"),
        P("branch", None, "dp"),
    )
    return jax.shard_map(
        on_device,
        mesh=mesh,
        in_specs=placed,
        out_specs=(
            P("branch", "dp", None, None),
            P("dp", None, "branch"),
            P(("branch", "dp"), None, "tensor"),
            P("tensor", ("branch", "dp")),
            P(("branch", "dp"), "tensor"),
            P("tensor", ("branch", "dp")),
            P(None, ("branch", "dp")),
            P(None, ("branch", "dp")),
        ),
        check_vma=False,
    )
```

time: 157 us -> 131 us (0.83)
  local copies, waits for them, and re-layouts: 17.5 us -> 2.66 us
  Pallas kernels: 53.8 us -> 43.7 us
  other arithmetic: 8.4 us -> 0.72 us
  waiting for transfers between devices: 31 us -> 37.4 us
    ppermute x30 -> x26, waiting for transfers between devices: 25.9 us -> 36.6 us  [exchange(): return lax.ppermute(block, SPAN, pairs)]
    pallas_call x7 -> x15, Pallas kernels: 53.8 us -> 43.7 us  [call(): pl.pallas_call(kernel, grid=(1,) if stream else (), out_shape=[jax.ShapeD...]
    unnamed x65 -> x12, local copies, waits for them, and re-layouts: 6.43 us -> 1.58 us
    ppermute x19, waiting for transfers between devices: 5.14 us -> 0.83 us  [swap_cores(): return lax.ppermute(block, 'branch', [(0, 1), (1, 0)])]
    convert_element_type x5 -> x0, other arithmetic: 3.87 us -> none  [the longest x2 1.71 us: chip_sum(): return (keep.astype(F32) + swap_cores(send).astype(F32)).astype(BF16)]
    select_n x3 -> x0, other arithmetic: 3.61 us -> none  [the longest x1 1.79 us: on_device(): got_far = swap_cores(jnp.where(on_query, far_q, far_m))]
    squeeze x5 -> x0, local copies, waits for them, and re-layouts: 3.04 us -> none  [the longest x2 1.71 us: near_pieces(): return [exchange(both[j], j // 2, j % 2) for j in range(1, both.shape[0])]]
    transpose x3 -> x0, local copies, waits for them, and re-layouts: 2.9 us -> none  [the longest x1 1.35 us: on_device(): out_grad = attn_share[:, 3 * group + 64:4 * group + 64].T]
  transfers between devices with their start and end apart: 49 -> 45, of which waited for: 14 -> 14; matrix products, arithmetic and copies ran while one was open for 13% -> 1% of each run, Pallas kernels for 30% -> 30%
where the time goes in v3:
time: 131 us
  starting transfers between devices  45.2 us (35%)
  Pallas kernels  43.7 us (33%)
  waiting for transfers between devices  37.4 us (29%)
  local copies, waits for them, and re-layouts  2.66 us (2%)
    pallas_call x15, Pallas kernels, call(): pl.pallas_call(kernel, grid=(1,) if stream else (), out_shape=[jax.ShapeD...  43.7 us
    ppermute x26, starting transfers between devices, exchange(): return lax.ppermute(block, SPAN, pairs)  41.2 us
    ppermute x26, waiting for transfers between devices, exchange(): return lax.ppermute(block, SPAN, pairs)  36.6 us
    ppermute x19, starting transfers between devices, swap_cores(): return lax.ppermute(block, 'branch', [(0, 1), (1, 0)])  3.99 us
  transfers between devices with their start and end apart: 45, of which 14 were waited for; matrix products, arithmetic and copies ran while one was open for 1% of the time, Pallas kernels for 30%

profile of v3, /device:TPU:0, one launch (start us, length us, event | category | flops | bytes accessed | tf_op | source)
XLA Modules:
  0.0 130.6 jit_solution(11335645588578742125)
XLA Ops:
  1.2 2.6 %shard_map.152 = (bf16[48,1280]{1,0:T(8,128)(2,1)}, bf16[48,1280]{1,0:T(8,128)(2,1)}) custom-call(s32[3]{0:T(128)} %pad_add_fusion.b_ref.refs_0_.ids_ref, f32[3,48,192]{2,1,0:T(8,128)} %bitcast.49, f32[48,192]{1,0:T(8,128)} %bitcast.55, f32[48,768]{1,0:T(8,128)} %bitcast.50, f32[48,768]{1,0:T(8,128)} %bitcast.51, f32[2,48]{1,0:T(2,128)} %bitcast.57, ...), custom_call_target="tpu_custom_call" | custom-call | tf_op jit(solution)/shard_map/pallas_call | solution.py:524
  7.9 3.1 %collective-permute-start.7 = (bf16[48,896]{1,0:T(8,128)(2,1)S(1)}, bf16[48,896]{1,0:T(8,128)(2,1)S(1)}, u32[]{:S(2)}, u32[]{:S(2)}) collective-permute-start(bf16[48,896]{1,0:T(8,128)(2,1)S(1)} %get-tuple-element.94), channel_id=1, source_target_pairs={{0,4},{1,5},{2,6},{3,7},{4,0},{5,1},{6,2},{7,3},{8,12},{9,13},{10,... | collective-permute-start | bytes 258056 | tf_op jit(solution)/shard_map/ppermute | solution.py:548
  10.9 2.6 %collective-permute-start.8 = (bf16[48,896]{1,0:T(8,128)(2,1)S(1)}, bf16[48,896]{1,0:T(8,128)(2,1)S(1)}, u32[]{:S(2)}, u32[]{:S(2)}) collective-permute-start(bf16[48,896]{1,0:T(8,128)(2,1)S(1)} %get-tuple-element.94), channel_id=1, source_target_pairs={{0,8},{1,9},{2,10},{3,11},{4,12},{5,13},{6,14},{7,15},{8,0},{9,1},... | collective-permute-start | bytes 258056 | tf_op jit(solution)/shard_map/ppermute | solution.py:548
  14.4 3.6 %collective-permute-start.2 = (bf16[48,1536]{1,0:T(8,128)(2,1)S(1)}, bf16[48,1536]{1,0:T(8,128)(2,1)S(1)}, u32[]{:S(2)}, u32[]{:S(2)}) collective-permute-start(bf16[48,1536]{1,0:T(8,128)(2,1)S(1)} %get-tuple-element.93), channel_id=1, source_target_pairs={{0,8},{1,9},{2,10},{3,11},{4,12},{5,13},{6,14},{7,15},{8,0},{9,1},... | collective-permute-start | bytes 442376 | tf_op jit(solution)/shard_map/ppermute | solution.py:548
  18.0 2.6 %collective-permute-done.8 = bf16[48,896]{1,0:T(8,128)(2,1)S(1)} collective-permute-done((bf16[48,896]{1,0:T(8,128)(2,1)S(1)}, bf16[48,896]{1,0:T(8,128)(2,1)S(1)}, u32[]{:S(2)}, u32[]{:S(2)}) %collective-permute-start.8) | collective-permute-done | bytes 86048 | tf_op jit(solution)/shard_map/ppermute | solution.py:548
  20.5 2.8 %collective-permute-start.3 = (bf16[48,1536]{1,0:T(8,128)(2,1)S(1)}, bf16[48,1536]{1,0:T(8,128)(2,1)S(1)}, u32[]{:S(2)}, u32[]{:S(2)}) collective-permute-start(bf16[48,1536]{1,0:T(8,128)(2,1)S(1)} %get-tuple-element.93), channel_id=1, source_target_pairs={{0,12},{1,13},{2,14},{3,15},{4,8},{5,9},{6,10},{7,11},{8,4},{9,5},... | collective-permute-start | bytes 442376 | tf_op jit(solution)/shard_map/ppermute | solution.py:548
  23.5 1.6 %collective-permute-start.11 = (bf16[4,48,896]{2,1,0:T(8,128)(2,1)S(1)}, bf16[4,48,896]{2,1,0:T(8,128)(2,1)S(1)}, u32[]{:S(2)}, u32[]{:S(2)}) collective-permute-start(bf16[4,48,896]{2,1,0:T(8,128)(2,1)S(1)} %pad_maximum_fusion.refs_3_), channel_id=1, source_target_pairs={{0,2},{1,3},{2,0},{3,1},{4,6},{5,7},{6,4},{7,5},{8,10},{9,11},{10,... | collective-permute-start | bytes 1032200 | tf_op jit(solution)/shard_map/ppermute | solution.py:548
  25.0 1.6 %collective-permute-start.12 = (bf16[4,48,896]{2,1,0:T(8,128)(2,1)S(1)}, bf16[4,48,896]{2,1,0:T(8,128)(2,1)S(1)}, u32[]{:S(2)}, u32[]{:S(2)}) collective-permute-start(bf16[4,48,896]{2,1,0:T(8,128)(2,1)S(1)} %pad_maximum_fusion.refs_3_), channel_id=1, source_target_pairs={{0,1},{1,0},{2,3},{3,2},{4,5},{5,4},{6,7},{7,6},{8,9},{9,8},{10,11... | collective-permute-start | bytes 1032200 | tf_op jit(solution)/shard_map/ppermute | solution.py:548
  27.1 4.9 %collective-permute-done.2 = bf16[48,1536]{1,0:T(8,128)(2,1)S(1)} collective-permute-done((bf16[48,1536]{1,0:T(8,128)(2,1)S(1)}, bf16[48,1536]{1,0:T(8,128)(2,1)S(1)}, u32[]{:S(2)}, u32[]{:S(2)}) %collective-permute-start.2) | collective-permute-done | bytes 147488 | tf_op jit(solution)/shard_map/ppermute | solution.py:548
  32.6 4.8 %collective-permute-done.12.refs_5_ = bf16[4,48,896]{2,1,0:T(8,128)(2,1)S(1)} collective-permute-done((bf16[4,48,896]{2,1,0:T(8,128)(2,1)S(1)}, bf16[4,48,896]{2,1,0:T(8,128)(2,1)S(1)}, u32[]{:S(2)}, u32[]{:S(2)}) %collective-permute-start.12) | collective-permute-done | bytes 344096 | tf_op jit(solution)/shard_map/ppermute | solution.py:548
  38.7 1.6 %collective-permute-start.5 = (bf16[4,48,768]{2,1,0:T(8,128)(2,1)S(1)}, bf16[4,48,768]{2,1,0:T(8,128)(2,1)S(1)}, u32[]{:S(2)}, u32[]{:S(2)}) collective-permute-start(bf16[4,48,768]{2,1,0:T(8,128)(2,1)S(1)} %pad_maximum_fusion.1.refs_3_), channel_id=1, source_target_pairs={{0,1},{1,0},{2,3},{3,2},{4,5},{5,4},{6,7},{7,6},{8,9},{9,8},{10,11... | collective-permute-start | bytes 884744 | tf_op jit(solution)/shard_map/ppermute | solution.py:548
  41.7 10.6 %shard_map.154 = (f32[384,512]{1,0:T(8,128)S(1)}, f32[384,512]{1,0:T(8,128)S(1)}, f32[384,128]{1,0:T(8,128)S(1)}, bf16[2,2,384,384]{3,2,1,0:T(8,128)(2,1)S(1)}, ...) custom-call(s32[3]{0:T(128)S(1)} %copy-done.3, ...), custom_call_target="tpu_custom_call" | custom-call | tf_op jit(solution)/shard_map/pallas_call | solution.py:524
  52.8 1.4 %collective-permute-done.6.refs_6_ = bf16[4,48,768]{2,1,0:T(8,128)(2,1)S(1)} collective-permute-done((bf16[4,48,768]{2,1,0:T(8,128)(2,1)S(1)}, bf16[4,48,768]{2,1,0:T(8,128)(2,1)S(1)}, u32[]{:S(2)}, u32[]{:S(2)}) %collective-permute-start.6) | collective-permute-done | bytes 294944 | tf_op jit(solution)/shard_map/ppermute | solution.py:548
  56.1 1.5 %collective-permute-start.19 = (bf16[4,48,768]{2,1,0:T(8,128)(2,1)S(1)}, bf16[4,48,768]{2,1,0:T(8,128)(2,1)S(1)}, u32[]{:S(2)}, u32[]{:S(2)}) collective-permute-start(bf16[4,48,768]{2,1,0:T(8,128)(2,1)S(1)} %pad_maximum_fusion.2.refs_4_), channel_id=1, source_target_pairs={{0,1},{1,0},{2,3},{3,2},{4,5},{5,4},{6,7},{7,6},{8,9},{9,8},{10,11... | collective-permute-start | bytes 884744 | tf_op jit(solution)/shard_map/ppermute | solution.py:548
  58.8 10.1 %shard_map.155 = (bf16[512,384]{1,0:T(8,128)(2,1)S(1)}, bf16[4,4,24,1536]{3,2,1,0:T(8,128)(2,1)S(1)}, bf16[4,4,24,1536]{3,2,1,0:T(8,128)(2,1)S(1)}, f32[384,512]{1,0:T(8,128)S(1)}, f32[384,128]{1,0:T(8,128)S(1)}) custom-call(s32[3]{0:T(128)S(1)} %copy-done.3, f32[384,512]{1,0:T(8,128)S(1)} %get-tuple-element.102.refs_1_, ...), custom_call_target="tpu_custom_call" | custom-call | tf_op jit(solution)/shard_map/pallas_call | solution.py:524
  69.0 2.2 %collective-permute-done.19.refs_6_ = bf16[4,48,768]{2,1,0:T(8,128)(2,1)S(1)} collective-permute-done((bf16[4,48,768]{2,1,0:T(8,128)(2,1)S(1)}, bf16[4,48,768]{2,1,0:T(8,128)(2,1)S(1)}, u32[]{:S(2)}, u32[]{:S(2)}) %collective-permute-start.19) | collective-permute-done | bytes 294944 | tf_op jit(solution)/shard_map/ppermute | solution.py:548
  71.7 1.3 %collective-permute-start.30 = (bf16[512,384]{1,0:T(8,128)(2,1)S(1)}, bf16[512,384]{1,0:T(8,128)(2,1)S(1)}, u32[]{:S(2)}, u32[]{:S(2)}) collective-permute-start(bf16[512,384]{1,0:T(8,128)(2,1)S(1)} %get-tuple-element.117.refs_3_), channel_id=1, source_target_pairs={{0,1},{1,0},{2,3},{3,2},{4,5},{5,4},{6,7},{7,6},{8,9},{9,8},{10,11... | collective-permute-start | bytes 1179656 | tf_op jit(solution)/shard_map/ppermute | solution.py:548
  75.8 7.0 %shard_map.157 = (bf16[512,384]{1,0:T(8,128)(2,1)S(1)}, bf16[512,384]{1,0:T(8,128)(2,1)S(1)}, bf16[512,384]{1,0:T(8,128)(2,1)S(1)}) custom-call(s32[3]{0:T(128)S(1)} %copy-done.4, f32[384,512]{1,0:T(8,128)S(1)} %get-tuple-element.116.refs_1_, f32[384,128]{1,0:T(8,128)S(1)} %get-tuple-element.103.refs_2_.refs_3_, ...), custom_call_target="tpu_custom_call" | custom-call | tf_op jit(solution)/shard_map/pallas_call | solution.py:524
  82.8 1.4 %collective-permute-start.32 = (bf16[512,384]{1,0:T(8,128)(2,1)S(1)}, bf16[512,384]{1,0:T(8,128)(2,1)S(1)}, u32[]{:S(2)}, u32[]{:S(2)}) collective-permute-start(bf16[512,384]{1,0:T(8,128)(2,1)S(1)} %get-tuple-element.127), channel_id=1, source_target_pairs={{0,1},{1,0},{2,3},{3,2},{4,5},{5,4},{6,7},{7,6},{8,9},{9,8},{10,11... | collective-permute-start | bytes 1179656 | tf_op jit(solution)/shard_map/ppermute | solution.py:548
  84.2 6.6 %shard_map.158 = (f32[2,192,256]{2,1,0:T(8,128)S(1)}, bf16[2,192,256]{2,1,0:T(8,128)(2,1)S(1)}, bf16[4,4,24,896]{3,2,1,0:T(8,128)(2,1)S(1)}, bf16[4,4,24,896]{3,2,1,0:T(8,128)(2,1)S(1)}) custom-call(s32[3]{0:T(128)S(1)} %copy-done.4, f32[384,512]{1,0:T(8,128)S(1)} %get-tuple-element.129.refs_1_, f32[384,128]{1,0:T(8,128)S(1)} %get-tuple-element.130.refs_2_, ...), custom_call_target="tpu_custom_call" | custom-call | tf_op jit(solution)/shard_map/pallas_call | solution.py:524
  90.8 3.2 %collective-permute-done.32.momentum_ref = bf16[512,384]{1,0:T(8,128)(2,1)S(1)} collective-permute-done((bf16[512,384]{1,0:T(8,128)(2,1)S(1)}, bf16[512,384]{1,0:T(8,128)(2,1)S(1)}, u32[]{:S(2)}, u32[]{:S(2)}) %collective-permute-start.32) | collective-permute-done | bytes 393248 | tf_op jit(solution)/shard_map/ppermute | solution.py:548
  94.6 1.4 %collective-permute-start.40 = (bf16[4,24,1536]{2,1,0:T(8,128)(2,1)S(1)}, bf16[4,24,1536]{2,1,0:T(8,128)(2,1)S(1)}, u32[]{:S(2)}, u32[]{:S(2)}) collective-permute-start(bf16[4,24,1536]{2,1,0:T(8,128)(2,1)S(1)} %get-tuple-element.156), channel_id=1, source_target_pairs={{0,1},{1,0},{2,3},{3,2},{4,5},{5,4},{6,7},{7,6},{8,9},{9,8},{10,11... | collective-permute-start | bytes 884744 | tf_op jit(solution)/shard_map/ppermute | solution.py:548
  96.3 1.4 %collective-permute-start.37 = (bf16[4,24,896]{2,1,0:T(8,128)(2,1)S(1)}, bf16[4,24,896]{2,1,0:T(8,128)(2,1)S(1)}, u32[]{:S(2)}, u32[]{:S(2)}) collective-permute-start(bf16[4,24,896]{2,1,0:T(8,128)(2,1)S(1)} %get-tuple-element.152), channel_id=1, source_target_pairs={{0,1},{1,0},{2,3},{3,2},{4,5},{5,4},{6,7},{7,6},{8,9},{9,8},{10,11... | collective-permute-start | bytes 516104 | tf_op jit(solution)/shard_map/ppermute | solution.py:548
  100.5 7.7 %collective-permute-done.40.refs_1_ = bf16[4,24,1536]{2,1,0:T(8,128)(2,1)S(1)} collective-permute-done((bf16[4,24,1536]{2,1,0:T(8,128)(2,1)S(1)}, bf16[4,24,1536]{2,1,0:T(8,128)(2,1)S(1)}, u32[]{:S(2)}, u32[]{:S(2)}) %collective-permute-start.40) | collective-permute-done | bytes 294944 | tf_op jit(solution)/shard_map/ppermute | solution.py:548
  108.8 2.1 %collective-permute-done.37.refs_3_ = bf16[4,24,896]{2,1,0:T(8,128)(2,1)S(1)} collective-permute-done((bf16[4,24,896]{2,1,0:T(8,128)(2,1)S(1)}, bf16[4,24,896]{2,1,0:T(8,128)(2,1)S(1)}, u32[]{:S(2)}, u32[]{:S(2)}) %collective-permute-start.37) | collective-permute-done | bytes 172064 | tf_op jit(solution)/shard_map/ppermute | solution.py:548
  111.0 1.4 %collective-permute-start.41 = (bf16[2,2,192,256]{3,2,1,0:T(8,128)(2,1)S(1)}, bf16[2,2,192,256]{3,2,1,0:T(8,128)(2,1)S(1)}, u32[]{:S(2)}, u32[]{:S(2)}) collective-permute-start(bf16[2,2,192,256]{3,2,1,0:T(8,128)(2,1)S(1)} %shard_map.163), channel_id=1, source_target_pairs={{0,1},{1,0},{2,3},{3,2},{4,5},{5,4},{6,7},{7,6},{8,9},{9,8},{10,11... | collective-permute-start | bytes 1179656 | tf_op jit(solution)/shard_map/ppermute | solution.py:548
  112.5 3.8 %collective-permute-start.42 = (bf16[24,2432]{1,0:T(8,128)(2,1)S(1)}, bf16[24,2432]{1,0:T(8,128)(2,1)S(1)}, u32[]{:S(2)}, u32[]{:S(2)}) collective-permute-start(bf16[24,2432]{1,0:T(8,128)(2,1)S(1)} %get-tuple-element.165), channel_id=1, source_target_pairs={{0,4},{1,5},{2,6},{3,7},{4,0},{5,1},{6,2},{7,3},{8,12},{9,13},{10,... | collective-permute-start | bytes 350216 | tf_op jit(solution)/shard_map/ppermute | solution.py:548
  116.3 2.1 %collective-permute-start.43 = (bf16[24,2432]{1,0:T(8,128)(2,1)S(1)}, bf16[24,2432]{1,0:T(8,128)(2,1)S(1)}, u32[]{:S(2)}, u32[]{:S(2)}) collective-permute-start(bf16[24,2432]{1,0:T(8,128)(2,1)S(1)} %get-tuple-element.166), channel_id=1, source_target_pairs={{0,8},{1,9},{2,10},{3,11},{4,12},{5,13},{6,14},{7,15},{8,0},{9,1},... | collective-permute-start | bytes 350216 | tf_op jit(solution)/shard_map/ppermute | solution.py:548
  118.5 1.4 %collective-permute-start.44 = (bf16[24,2432]{1,0:T(8,128)(2,1)S(1)}, bf16[24,2432]{1,0:T(8,128)(2,1)S(1)}, u32[]{:S(2)}, u32[]{:S(2)}) collective-permute-start(bf16[24,2432]{1,0:T(8,128)(2,1)S(1)} %get-tuple-element.167), channel_id=1, source_target_pairs={{0,12},{1,13},{2,14},{3,15},{4,8},{5,9},{6,10},{7,11},{8,4},{9,5},... | collective-permute-start | bytes 350216 | tf_op jit(solution)/shard_map/ppermute | solution.py:548
  119.9 1.7 %shard_map.160 = bf16[2,2,512,384]{3,2,1,0:T(8,128)(2,1)} custom-call(s32[3]{0:T(128)S(1)} %copy-done.4, bf16[512,384]{1,0:T(8,128)(2,1)S(1)} %get-tuple-element.122.own_ref, bf16[512,384]{1,0:T(8,128)(2,1)S(1)} %get-tuple-element.145.own_far, bf16[512,384]{1,0:T(8,128)(2,1)S(1)} %collective-permute-done.33.got_ref, ...), custom_call_target="tpu_custom_call" | custom-call | tf_op jit(solution)/shard_map/pallas_call | solution.py:524
  121.6 6.4 %collective-permute-done.43.refs_2_ = bf16[24,2432]{1,0:T(8,128)(2,1)S(1)} collective-permute-done((bf16[24,2432]{1,0:T(8,128)(2,1)S(1)}, bf16[24,2432]{1,0:T(8,128)(2,1)S(1)}, u32[]{:S(2)}, u32[]{:S(2)}) %collective-permute-start.43) | collective-permute-done | bytes 116768 | tf_op jit(solution)/shard_map/ppermute | solution.py:548
  128.8 1.8 %shard_map.164 = f32[2,2,2,192,256]{4,3,2,1,0:T(8,128)} custom-call(s32[3]{0:T(128)S(1)} %copy-done.4, f32[2,192,256]{2,1,0:T(8,128)S(1)} %get-tuple-element.148.keep_ref, bf16[2,192,256]{2,1,0:T(8,128)(2,1)S(1)} %collective-permute-done.35.got_ref, bf16[2,2,192,256]{3,2,1,0:T(8,128)(2,1)S(1)} %collective-permute-done.41.far_ref), custom_call_target="tpu_custom_call" | custom-call | tf_op jit(solution)/shard_map/pallas_call | solution.py:524
  (94 shorter events, 21.2 us)
Async XLA Ops:
  5.4 18.1 %collective-permute-start.10 = (bf16[512,384]{1,0:T(8,128)(2,1)S(1)}, bf16[512,384]{1,0:T(8,128)(2,1)S(1)}, u32[]{:S(2)}, u32[]{:S(2)}) collective-permute-start(bf16[512,384]{1,0:T(8,128)(2,1)S(1)} %bitcast.48), channel_id=1, source_target_pairs={{0,16},{16,0},{1,17},{17,1},{2,18},{18,2},{3,19},{19,3},{4,20},{20... | collective-permute-start | bytes 1179656 | tf_op jit(solution)/shard_map/ppermute | solution.py:540
  7.9 6.6 %collective-permute-start.7 = (bf16[48,896]{1,0:T(8,128)(2,1)S(1)}, bf16[48,896]{1,0:T(8,128)(2,1)S(1)}, u32[]{:S(2)}, u32[]{:S(2)}) collective-permute-start(bf16[48,896]{1,0:T(8,128)(2,1)S(1)} %get-tuple-element.94), channel_id=1, source_target_pairs={{0,4},{1,5},{2,6},{3,7},{4,0},{5,1},{6,2},{7,3},{8,12},{9,13},{10,... | collective-permute-start | bytes 258056 | tf_op jit(solution)/shard_map/ppermute | solution.py:548
  10.9 9.6 %collective-permute-start.8 = (bf16[48,896]{1,0:T(8,128)(2,1)S(1)}, bf16[48,896]{1,0:T(8,128)(2,1)S(1)}, u32[]{:S(2)}, u32[]{:S(2)}) collective-permute-start(bf16[48,896]{1,0:T(8,128)(2,1)S(1)} %get-tuple-element.94), channel_id=1, source_target_pairs={{0,8},{1,9},{2,10},{3,11},{4,12},{5,13},{6,14},{7,15},{8,0},{9,1},... | collective-permute-start | bytes 258056 | tf_op jit(solution)/shard_map/ppermute | solution.py:548
  13.5 9.9 %collective-permute-start.9 = (bf16[48,896]{1,0:T(8,128)(2,1)S(1)}, bf16[48,896]{1,0:T(8,128)(2,1)S(1)}, u32[]{:S(2)}, u32[]{:S(2)}) collective-permute-start(bf16[48,896]{1,0:T(8,128)(2,1)S(1)} %get-tuple-element.94), channel_id=1, source_target_pairs={{0,12},{1,13},{2,14},{3,15},{4,8},{5,9},{6,10},{7,11},{8,4},{9,5},... | collective-permute-start | bytes 258056 | tf_op jit(solution)/shard_map/ppermute | solution.py:548
  13.5 11.5 %collective-permute-start.1 = (bf16[48,1536]{1,0:T(8,128)(2,1)S(1)}, bf16[48,1536]{1,0:T(8,128)(2,1)S(1)}, u32[]{:S(2)}, u32[]{:S(2)}) collective-permute-start(bf16[48,1536]{1,0:T(8,128)(2,1)S(1)} %get-tuple-element.93), channel_id=1, source_target_pairs={{0,4},{1,5},{2,6},{3,7},{4,0},{5,1},{6,2},{7,3},{8,12},{9,13},{10,... | collective-permute-start | bytes 442376 | tf_op jit(solution)/shard_map/ppermute | solution.py:548
  14.4 17.5 %collective-permute-start.2 = (bf16[48,1536]{1,0:T(8,128)(2,1)S(1)}, bf16[48,1536]{1,0:T(8,128)(2,1)S(1)}, u32[]{:S(2)}, u32[]{:S(2)}) collective-permute-start(bf16[48,1536]{1,0:T(8,128)(2,1)S(1)} %get-tuple-element.93), channel_id=1, source_target_pairs={{0,8},{1,9},{2,10},{3,11},{4,12},{5,13},{6,14},{7,15},{8,0},{9,1},... | collective-permute-start | bytes 442376 | tf_op jit(solution)/shard_map/ppermute | solution.py:548
  20.5 12.0 %collective-permute-start.3 = (bf16[48,1536]{1,0:T(8,128)(2,1)S(1)}, bf16[48,1536]{1,0:T(8,128)(2,1)S(1)}, u32[]{:S(2)}, u32[]{:S(2)}) collective-permute-start(bf16[48,1536]{1,0:T(8,128)(2,1)S(1)} %get-tuple-element.93), channel_id=1, source_target_pairs={{0,12},{1,13},{2,14},{3,15},{4,8},{5,9},{6,10},{7,11},{8,4},{9,5},... | collective-permute-start | bytes 442376 | tf_op jit(solution)/shard_map/ppermute | solution.py:548
  23.5 9.0 %collective-permute-start.11 = (bf16[4,48,896]{2,1,0:T(8,128)(2,1)S(1)}, bf16[4,48,896]{2,1,0:T(8,128)(2,1)S(1)}, u32[]{:S(2)}, u32[]{:S(2)}) collective-permute-start(bf16[4,48,896]{2,1,0:T(8,128)(2,1)S(1)} %pad_maximum_fusion.refs_3_), channel_id=1, source_target_pairs={{0,2},{1,3},{2,0},{3,1},{4,6},{5,7},{6,4},{7,5},{8,10},{9,11},{10,... | collective-permute-start | bytes 1032200 | tf_op jit(solution)/shard_map/ppermute | solution.py:548
  25.0 12.4 %collective-permute-start.12 = (bf16[4,48,896]{2,1,0:T(8,128)(2,1)S(1)}, bf16[4,48,896]{2,1,0:T(8,128)(2,1)S(1)}, u32[]{:S(2)}, u32[]{:S(2)}) collective-permute-start(bf16[4,48,896]{2,1,0:T(8,128)(2,1)S(1)} %pad_maximum_fusion.refs_3_), channel_id=1, source_target_pairs={{0,1},{1,0},{2,3},{3,2},{4,5},{5,4},{6,7},{7,6},{8,9},{9,8},{10,11... | collective-permute-start | bytes 1032200 | tf_op jit(solution)/shard_map/ppermute | solution.py:548
  26.6 10.8 %collective-permute-start.13 = (bf16[4,48,896]{2,1,0:T(8,128)(2,1)S(1)}, bf16[4,48,896]{2,1,0:T(8,128)(2,1)S(1)}, u32[]{:S(2)}, u32[]{:S(2)}) collective-permute-start(bf16[4,48,896]{2,1,0:T(8,128)(2,1)S(1)} %pad_maximum_fusion.refs_3_), channel_id=1, source_target_pairs={{0,3},{1,2},{2,1},{3,0},{4,7},{5,6},{6,5},{7,4},{8,11},{9,10},{10,... | collective-permute-start | bytes 1032200 | tf_op jit(solution)/shard_map/ppermute | solution.py:548
  32.0 6.7 %collective-permute-start.14 = (bf16[4,48,896]{2,1,0:T(8,128)(2,1)S(1)}, bf16[4,48,896]{2,1,0:T(8,128)(2,1)S(1)}, u32[]{:S(2)}, u32[]{:S(2)}) collective-permute-start(bf16[4,48,896]{2,1,0:T(8,128)(2,1)S(1)} %pad_maximum_fusion.refs_3_), channel_id=1, source_target_pairs={{0,16},{16,0},{1,17},{17,1},{2,18},{18,2},{3,19},{19,3},{4,20},{20... | collective-permute-start | bytes 1032200 | tf_op jit(solution)/shard_map/ppermute | solution.py:540
  32.5 7.8 %collective-permute-start.15 = (bf16[4,48,896]{2,1,0:T(8,128)(2,1)S(1)}, bf16[4,48,896]{2,1,0:T(8,128)(2,1)S(1)}, u32[]{:S(2)}, u32[]{:S(2)}) collective-permute-start(bf16[4,48,896]{2,1,0:T(8,128)(2,1)S(1)} %collective-permute-done.11.refs_4_), channel_id=1, source_target_pairs={{0,16},{16,0},{1,17},{17,1},{2,18},{18,2},{3,19},{19,3},{4,20},{20... | collective-permute-start | bytes 1032200 | tf_op jit(solution)/shard_map/ppermute | solution.py:540
  38.0 14.2 %collective-permute-start.4 = (bf16[4,48,768]{2,1,0:T(8,128)(2,1)S(1)}, bf16[4,48,768]{2,1,0:T(8,128)(2,1)S(1)}, u32[]{:S(2)}, u32[]{:S(2)}) collective-permute-start(bf16[4,48,768]{2,1,0:T(8,128)(2,1)S(1)} %pad_maximum_fusion.1.refs_3_), channel_id=1, source_target_pairs={{0,2},{1,3},{2,0},{3,1},{4,6},{5,7},{6,4},{7,5},{8,10},{9,11},{10,... | collective-permute-start | bytes 884744 | tf_op jit(solution)/shard_map/ppermute | solution.py:548
  38.7 14.1 %collective-permute-start.5 = (bf16[4,48,768]{2,1,0:T(8,128)(2,1)S(1)}, bf16[4,48,768]{2,1,0:T(8,128)(2,1)S(1)}, u32[]{:S(2)}, u32[]{:S(2)}) collective-permute-start(bf16[4,48,768]{2,1,0:T(8,128)(2,1)S(1)} %pad_maximum_fusion.1.refs_3_), channel_id=1, source_target_pairs={{0,1},{1,0},{2,3},{3,2},{4,5},{5,4},{6,7},{7,6},{8,9},{9,8},{10,11... | collective-permute-start | bytes 884744 | tf_op jit(solution)/shard_map/ppermute | solution.py:548
  40.3 13.9 %collective-permute-start.6 = (bf16[4,48,768]{2,1,0:T(8,128)(2,1)S(1)}, bf16[4,48,768]{2,1,0:T(8,128)(2,1)S(1)}, u32[]{:S(2)}, u32[]{:S(2)}) collective-permute-start(bf16[4,48,768]{2,1,0:T(8,128)(2,1)S(1)} %pad_maximum_fusion.1.refs_3_), channel_id=1, source_target_pairs={{0,3},{1,2},{2,1},{3,0},{4,7},{5,6},{6,5},{7,4},{8,11},{9,10},{10,... | collective-permute-start | bytes 884744 | tf_op jit(solution)/shard_map/ppermute | solution.py:548
  55.3 13.7 %collective-permute-start.18 = (bf16[4,48,768]{2,1,0:T(8,128)(2,1)S(1)}, bf16[4,48,768]{2,1,0:T(8,128)(2,1)S(1)}, u32[]{:S(2)}, u32[]{:S(2)}) collective-permute-start(bf16[4,48,768]{2,1,0:T(8,128)(2,1)S(1)} %pad_maximum_fusion.2.refs_4_), channel_id=1, source_target_pairs={{0,2},{1,3},{2,0},{3,1},{4,6},{5,7},{6,4},{7,5},{8,10},{9,11},{10,... | collective-permute-start | bytes 884744 | tf_op jit(solution)/shard_map/ppermute | solution.py:548
  56.1 15.1 %collective-permute-start.19 = (bf16[4,48,768]{2,1,0:T(8,128)(2,1)S(1)}, bf16[4,48,768]{2,1,0:T(8,128)(2,1)S(1)}, u32[]{:S(2)}, u32[]{:S(2)}) collective-permute-start(bf16[4,48,768]{2,1,0:T(8,128)(2,1)S(1)} %pad_maximum_fusion.2.refs_4_), channel_id=1, source_target_pairs={{0,1},{1,0},{2,3},{3,2},{4,5},{5,4},{6,7},{7,6},{8,9},{9,8},{10,11... | collective-permute-start | bytes 884744 | tf_op jit(solution)/shard_map/ppermute | solution.py:548
  57.6 13.6 %collective-permute-start.20 = (bf16[4,48,768]{2,1,0:T(8,128)(2,1)S(1)}, bf16[4,48,768]{2,1,0:T(8,128)(2,1)S(1)}, u32[]{:S(2)}, u32[]{:S(2)}) collective-permute-start(bf16[4,48,768]{2,1,0:T(8,128)(2,1)S(1)} %pad_maximum_fusion.2.refs_4_), channel_id=1, source_target_pairs={{0,3},{1,2},{2,1},{3,0},{4,7},{5,6},{6,5},{7,4},{8,11},{9,10},{10,... | collective-permute-start | bytes 884744 | tf_op jit(solution)/shard_map/ppermute | solution.py:548
  71.7 11.1 %collective-permute-start.30 = (bf16[512,384]{1,0:T(8,128)(2,1)S(1)}, bf16[512,384]{1,0:T(8,128)(2,1)S(1)}, u32[]{:S(2)}, u32[]{:S(2)}) collective-permute-start(bf16[512,384]{1,0:T(8,128)(2,1)S(1)} %get-tuple-element.117.refs_3_), channel_id=1, source_target_pairs={{0,1},{1,0},{2,3},{3,2},{4,5},{5,4},{6,7},{7,6},{8,9},{9,8},{10,11... | collective-permute-start | bytes 1179656 | tf_op jit(solution)/shard_map/ppermute | solution.py:548
  74.5 19.5 %collective-permute-start.31 = (bf16[2,4,24,1536]{3,2,1,0:T(8,128)(2,1)S(1)}, bf16[2,4,24,1536]{3,2,1,0:T(8,128)(2,1)S(1)}, u32[]{:S(2)}, u32[]{:S(2)}) collective-permute-start(bf16[2,4,24,1536]{3,2,1,0:T(8,128)(2,1)S(1)} %get-tuple-element.126), channel_id=1, source_target_pairs={{0,2},{1,3},{2,0},{3,1},{4,6},{5,7},{6,4},{7,5},{8,10},{9,11},{10,... | collective-permute-start | bytes 1769480 | tf_op jit(solution)/shard_map/ppermute | solution.py:548
  82.8 11.2 %collective-permute-start.32 = (bf16[512,384]{1,0:T(8,128)(2,1)S(1)}, bf16[512,384]{1,0:T(8,128)(2,1)S(1)}, u32[]{:S(2)}, u32[]{:S(2)}) collective-permute-start(bf16[512,384]{1,0:T(8,128)(2,1)S(1)} %get-tuple-element.127), channel_id=1, source_target_pairs={{0,1},{1,0},{2,3},{3,2},{4,5},{5,4},{6,7},{7,6},{8,9},{9,8},{10,11... | collective-permute-start | bytes 1179656 | tf_op jit(solution)/shard_map/ppermute | solution.py:548
  94.0 5.9 %collective-permute-start.35 = (bf16[2,192,256]{2,1,0:T(8,128)(2,1)S(1)}, bf16[2,192,256]{2,1,0:T(8,128)(2,1)S(1)}, u32[]{:S(2)}, u32[]{:S(2)}) collective-permute-start(bf16[2,192,256]{2,1,0:T(8,128)(2,1)S(1)} %get-tuple-element.149), channel_id=1, source_target_pairs={{0,16},{16,0},{1,17},{17,1},{2,18},{18,2},{3,19},{19,3},{4,20},{20... | collective-permute-start | bytes 589832 | tf_op jit(solution)/shard_map/ppermute | solution.py:540
  94.6 13.6 %collective-permute-start.40 = (bf16[4,24,1536]{2,1,0:T(8,128)(2,1)S(1)}, bf16[4,24,1536]{2,1,0:T(8,128)(2,1)S(1)}, u32[]{:S(2)}, u32[]{:S(2)}) collective-permute-start(bf16[4,24,1536]{2,1,0:T(8,128)(2,1)S(1)} %get-tuple-element.156), channel_id=1, source_target_pairs={{0,1},{1,0},{2,3},{3,2},{4,5},{5,4},{6,7},{7,6},{8,9},{9,8},{10,11... | collective-permute-start | bytes 884744 | tf_op jit(solution)/shard_map/ppermute | solution.py:548
  96.3 14.7 %collective-permute-start.37 = (bf16[4,24,896]{2,1,0:T(8,128)(2,1)S(1)}, bf16[4,24,896]{2,1,0:T(8,128)(2,1)S(1)}, u32[]{:S(2)}, u32[]{:S(2)}) collective-permute-start(bf16[4,24,896]{2,1,0:T(8,128)(2,1)S(1)} %get-tuple-element.152), channel_id=1, source_target_pairs={{0,1},{1,0},{2,3},{3,2},{4,5},{5,4},{6,7},{7,6},{8,9},{9,8},{10,11... | collective-permute-start | bytes 516104 | tf_op jit(solution)/shard_map/ppermute | solution.py:548
  97.7 13.2 %collective-permute-start.38 = (bf16[4,24,896]{2,1,0:T(8,128)(2,1)S(1)}, bf16[4,24,896]{2,1,0:T(8,128)(2,1)S(1)}, u32[]{:S(2)}, u32[]{:S(2)}) collective-permute-start(bf16[4,24,896]{2,1,0:T(8,128)(2,1)S(1)} %get-tuple-element.153), channel_id=1, source_target_pairs={{0,2},{1,3},{2,0},{3,1},{4,6},{5,7},{6,4},{7,5},{8,10},{9,11},{10,... | collective-permute-start | bytes 516104 | tf_op jit(solution)/shard_map/ppermute | solution.py:548
  98.7 12.3 %collective-permute-start.39 = (bf16[4,24,896]{2,1,0:T(8,128)(2,1)S(1)}, bf16[4,24,896]{2,1,0:T(8,128)(2,1)S(1)}, u32[]{:S(2)}, u32[]{:S(2)}) collective-permute-start(bf16[4,24,896]{2,1,0:T(8,128)(2,1)S(1)} %get-tuple-element.154), channel_id=1, source_target_pairs={{0,3},{1,2},{2,1},{3,0},{4,7},{5,6},{6,5},{7,4},{8,11},{9,10},{10,... | collective-permute-start | bytes 516104 | tf_op jit(solution)/shard_map/ppermute | solution.py:548
  99.9 18.6 %collective-permute-start.33 = (bf16[512,384]{1,0:T(8,128)(2,1)S(1)}, bf16[512,384]{1,0:T(8,128)(2,1)S(1)}, u32[]{:S(2)}, u32[]{:S(2)}) collective-permute-start(bf16[512,384]{1,0:T(8,128)(2,1)S(1)} %get-tuple-element.146), channel_id=1, source_target_pairs={{0,16},{16,0},{1,17},{17,1},{2,18},{18,2},{3,19},{19,3},{4,20},{20... | collective-permute-start | bytes 1179656 | tf_op jit(solution)/shard_map/ppermute | solution.py:540
  108.3 11.6 %collective-permute-start.34 = (bf16[512,384]{1,0:T(8,128)(2,1)S(1)}, bf16[512,384]{1,0:T(8,128)(2,1)S(1)}, u32[]{:S(2)}, u32[]{:S(2)}) collective-permute-start(bf16[512,384]{1,0:T(8,128)(2,1)S(1)} %get-tuple-element.147), channel_id=1, source_target_pairs={{0,16},{16,0},{1,17},{17,1},{2,18},{18,2},{3,19},{19,3},{4,20},{20... | collective-permute-start | bytes 1179656 | tf_op jit(solution)/shard_map/ppermute | solution.py:540
  111.0 17.8 %collective-permute-start.41 = (bf16[2,2,192,256]{3,2,1,0:T(8,128)(2,1)S(1)}, bf16[2,2,192,256]{3,2,1,0:T(8,128)(2,1)S(1)}, u32[]{:S(2)}, u32[]{:S(2)}) collective-permute-start(bf16[2,2,192,256]{3,2,1,0:T(8,128)(2,1)S(1)} %shard_map.163), channel_id=1, source_target_pairs={{0,1},{1,0},{2,3},{3,2},{4,5},{5,4},{6,7},{7,6},{8,9},{9,8},{10,11... | collective-permute-start | bytes 1179656 | tf_op jit(solution)/shard_map/ppermute | solution.py:548
  112.5 9.1 %collective-permute-start.42 = (bf16[24,2432]{1,0:T(8,128)(2,1)S(1)}, bf16[24,2432]{1,0:T(8,128)(2,1)S(1)}, u32[]{:S(2)}, u32[]{:S(2)}) collective-permute-start(bf16[24,2432]{1,0:T(8,128)(2,1)S(1)} %get-tuple-element.165), channel_id=1, source_target_pairs={{0,4},{1,5},{2,6},{3,7},{4,0},{5,1},{6,2},{7,3},{8,12},{9,13},{10,... | collective-permute-start | bytes 350216 | tf_op jit(solution)/shard_map/ppermute | solution.py:548
  116.3 11.7 %collective-permute-start.43 = (bf16[24,2432]{1,0:T(8,128)(2,1)S(1)}, bf16[24,2432]{1,0:T(8,128)(2,1)S(1)}, u32[]{:S(2)}, u32[]{:S(2)}) collective-permute-start(bf16[24,2432]{1,0:T(8,128)(2,1)S(1)} %get-tuple-element.166), channel_id=1, source_target_pairs={{0,8},{1,9},{2,10},{3,11},{4,12},{5,13},{6,14},{7,15},{8,0},{9,1},... | collective-permute-start | bytes 350216 | tf_op jit(solution)/shard_map/ppermute | solution.py:548
  118.5 9.6 %collective-permute-start.44 = (bf16[24,2432]{1,0:T(8,128)(2,1)S(1)}, bf16[24,2432]{1,0:T(8,128)(2,1)S(1)}, u32[]{:S(2)}, u32[]{:S(2)}) collective-permute-start(bf16[24,2432]{1,0:T(8,128)(2,1)S(1)} %get-tuple-element.167), channel_id=1, source_target_pairs={{0,12},{1,13},{2,14},{3,15},{4,8},{5,9},{6,10},{7,11},{8,4},{9,5},... | collective-permute-start | bytes 350216 | tf_op jit(solution)/shard_map/ppermute | solution.py:548
  (19 other events, 131.3 us)

commit v4 on v3

--- a/solution.py
+++ b/solution.py
@@ -28,6 +28,10 @@
 
 def tn(left, right):
     return lax.dot_general(left, right, (((0,), (0,)), ((), ())), preferred_element_type=F32)
+
+
+def place():
+    return lax.axis_index("branch"), lax.axis_index("dp"), lax.axis_index("tensor")
 
 
 def gelu_parts(v):
@@ -147,13 +151,13 @@
     return x_t, attn
 
 
-def pack_kernel(b_ref, *refs):
+def pack_kernel(*refs):
     far, keep_ref, send_ref, near, sems = refs[:6], refs[6], refs[7], refs[8:14], refs[14]
     copies = [pltpu.make_async_copy(there, here, sems.at[i]) for i, (there, here) in enumerate(zip(far, near))]
     for copy in copies:
         copy.start()
     qkv_ref, out_ref, up_ref, down_ref, gain_ref, bias_ref = near
-    first = b_ref[0] == 0
+    first = lax.axis_index("branch") == 0
     shard, width = up_ref.shape[0], 2 * out_ref.shape[1]
     for copy in copies:
         copy.wait()
@@ -171,10 +175,10 @@
         ref[:, width + 128 :] = jnp.where(is_first, up, down)
 
 
-def split_kernel(width, b_ref, got_ref, far_ref, first_ref, second_ref, keep_ref, sems):
+def split_kernel(width, got_ref, far_ref, first_ref, second_ref, keep_ref, sems):
     copy = pltpu.make_async_copy(far_ref, keep_ref, sems.at[0])
     copy.start()
-    first = b_ref[0] == 0
+    first = lax.axis_index("branch") == 0
     got = got_ref[...]
     copy.wait()
     keep = keep_ref[...]
@@ -188,8 +192,8 @@
 
 
 def attention_kernel(plan, shard, *refs):
-    ids_ref, got_crops, seg_ref, refs = refs[0], refs[1], refs[2], refs[3:]
-    ids = ids_ref[0], ids_ref[1], ids_ref[2]
+    got_crops, seg_ref, refs = refs[0], refs[1], refs[2:]
+    ids = place()
     slots = seg_ref.shape[2]
     nseq = got_crops.shape[0] // slots
     if plan is None:
@@ -237,15 +241,20 @@
 
 
 def momentum_mlp_kernel(plan, shard, *refs):
-    ids_ref, res_ref, cols_ref, query_ref, refs = refs[0], refs[1], refs[2], refs[3], refs[4:]
-    ids = ids_ref[0], ids_ref[1], ids_ref[2]
+    res_ref, cols_ref, query_ref, refs = refs[0], refs[1], refs[2], refs[3:]
+    ids = place()
     cols = cols_ref[...][:, 8:]
     if plan is None:
         w2_ref, out_ref, own_ref, send_ref, acc_ref = refs
     else:
-        own, got = refs[: len(plan)], refs[len(plan) : 2 * len(plan)]
-        out_ref, own_ref, send_ref, acc_ref, w2_ref = refs[2 * len(plan) :]
-        place_weights(plan, own, got, shard, ids, [(w2_ref, 0, 0, w2_ref.shape[3])])
+        count = sum(len(part) for part in plan)
+        own, got = refs[:count], refs[count : 2 * count]
+        out_ref, own_ref, send_ref, acc_ref, w2_ref = refs[2 * count :]
+        at, wide = 0, own[0].shape[-1]
+        for i, part in enumerate(plan):
+            targets = [(w2_ref, i * wide, 0, wide)]
+            place_weights(part, own[at : at + len(part)], got[at : at + len(part)], shard, ids, targets)
+            at += len(part)
     res = res_ref[...]
     _, _, normed = norm_cols(res, cols[:, 1:2], cols[:, 4:5])
     rows_low = normed.T.astype(BF16)
@@ -261,7 +270,7 @@
         acc_ref[...] += nt(w2_ref[1, t, :, c], (pre * half).astype(BF16))
         return carry
 
-    lax.fori_loop(0, tensors * parts, step, 0)
+    lax.fori_loop(0, tensors * parts, step, 0, unroll=6)
     momentum, query = acc_ref[...].T.astype(BF16), query_ref[...]
     first = ids[0] == 0
     out_ref[...] = momentum
@@ -283,9 +292,9 @@
 
 
 def query_mlp_kernel(plan, chunks, shard, *refs):
-    ids_ref, res_ref, cols_ref = refs[:3]
-    cot_here, sems, refs = refs[-2], refs[-1], refs[3:-2]
-    ids = ids_ref[0], ids_ref[1], ids_ref[2]
+    res_ref, cols_ref = refs[:2]
+    cot_here, sems, refs = refs[-2], refs[-1], refs[2:-2]
+    ids = place()
     b = ids[0]
     if chunks is None:
         w2_ref, cot_ref, refs = refs[0], refs[1], refs[2:]
@@ -332,7 +341,7 @@
             store_grads(plan, ids, ref, t, later, nn(gt_ref[rows, :], hidden).astype(BF16))
         return carry
 
-    lax.fori_loop(0, tensors * parts, step, 0)
+    lax.fori_loop(0, tensors * parts, step, 0, unroll=6)
     out_ref[...] = acc_ref[...].T.astype(BF16)
     d_n2 = dn_ref[...]
     d_res = cot_t + norm_cols_back(d_n2, hat, rstd, cols[:, 1:2])
@@ -345,12 +354,12 @@
 
 
 def query_back_kernel(plan, nseq, *refs):
-    ids_ref, dres_ref, vgrad_ref, cols_ref = refs[:4]
-    w1_ref, hat_ref, rstd_ref, normed_ref, q_ref, k_ref, v_ref, inv_ref, ctx_ref, *pb_refs = refs[4 : 13 + nseq]
-    refs = refs[13 + nseq :]
+    dres_ref, vgrad_ref, cols_ref = refs[:3]
+    w1_ref, hat_ref, rstd_ref, normed_ref, q_ref, k_ref, v_ref, inv_ref, ctx_ref, *pb_refs = refs[3 : 12 + nseq]
+    refs = refs[12 + nseq :]
     crop_keep_ref, crop_send_ref, keep_ref, send_ref, dctx_ref, dproj_ref, dattn_ref, vg_ref, crop_ref = refs[:9]
     dp_refs, ds_refs, delta_refs = (refs[9 + i * nseq : 9 + (i + 1) * nseq] for i in range(3))
-    ids = ids_ref[0], ids_ref[1], ids_ref[2]
+    ids = place()
     b = ids[0]
     tensors, width = w1_ref.shape[1], w1_ref.shape[2]
     group = width // tensors
@@ -485,27 +494,27 @@
     out_ref[...] = attn[:, tile + 128 : tile + 128 + group]
 
 
-def crop_pair_kernel(ids_ref, keep_ref, got_ref, pair_ref):
-    b = ids_ref[0]
+def crop_pair_kernel(keep_ref, got_ref, pair_ref):
+    b = lax.axis_index("branch")
     pair_ref[b] = keep_ref[...].astype(BF16)
     pair_ref[1 - b] = got_ref[...]
 
 
-def crop_kernel(ids_ref, keep_ref, got_ref, far_ref, out_ref):
-    b, t = ids_ref[0], ids_ref[2]
+def crop_kernel(keep_ref, got_ref, far_ref, out_ref):
+    b, _, t = place()
     out_ref[t, b] = keep_ref[...]
     out_ref[t, 1 - b] = got_ref[...].astype(F32)
     out_ref[1 - t] = far_ref[...].astype(F32)
 
 
-def pick_kernel(ids_ref, query_ref, momentum_ref, own_ref, send_ref):
-    first = ids_ref[0] == 0
+def pick_kernel(query_ref, momentum_ref, own_ref, send_ref):
+    first = lax.axis_index("branch") == 0
     own_ref[...] = jnp.where(first, momentum_ref[...], query_ref[...])
     send_ref[...] = jnp.where(first, query_ref[...], momentum_ref[...])
 
 
-def encoded_kernel(ids_ref, own_ref, own_far, got_ref, got_far, out_ref, sems):
-    b, t = ids_ref[0], ids_ref[2]
+def encoded_kernel(own_ref, own_far, got_ref, got_far, out_ref, sems):
+    b, _, t = place()
     places = ((own_ref, t, b), (own_far, 1 - t, b), (got_ref, t, 1 - b), (got_far, 1 - t, 1 - b))
     copies = [pltpu.make_async_copy(part, out_ref.at[i, j], sems.at[n]) for n, (part, i, j) in enumerate(places)]
     for copy in copies:
@@ -514,9 +523,9 @@
         copy.wait()
 
 
-def call(kernel, out_shapes, scratch, args, smem=0, hbm=0, hbm_outs=0, copies=0, stream=False, limit=24):
+def call(kernel, out_shapes, scratch, args, hbm=0, hbm_outs=0, copies=0, stream=False, limit=24):
     place, hold = pl.BlockSpec(memory_space=pltpu.VMEM), pl.BlockSpec(memory_space=pltpu.HBM)
-    inner = args[smem : len(args) - hbm]
+    inner = args[: len(args) - hbm]
     if stream:
         specs = [pl.BlockSpec(x.shape, lambda i, n=x.ndim: (0,) * n) for x in inner]
     else:
@@ -525,7 +534,7 @@
         kernel,
         grid=(1,) if stream else (),
         out_shape=[jax.ShapeDtypeStruct(s, d) for s, d in out_shapes],
-        in_specs=[pl.BlockSpec(memory_space=pltpu.SMEM)] * smem + specs + [hold] * hbm,
+        in_specs=specs + [hold] * hbm,
         out_specs=[place] * (len(out_shapes) - hbm_outs) + [hold] * hbm_outs,
         scratch_shapes=[pltpu.VMEM(s, d) for s, d in scratch]
         + ([pltpu.SemaphoreType.DMA((copies,))] if copies else []),
@@ -678,7 +687,6 @@
     heads = tensors * group // HD
     heads_g = group // HD
     share = width // (2 * dp)
-    ids = jnp.stack([branch, me, t]).astype(jnp.int32)
     fine = tensors == 2 and dp == 8 and shard % 16 == 0
     near = [(k << 1, 0) for k in range(1, 4)]
     both_ways = [(1, 0), (0, 1), (1, 1)]
@@ -708,8 +716,7 @@
             + [pb_block] * nseq
             + [head_block, head_block, v_block, ctx_block, bias_block, crop_block]
             + [(w1_shape, BF16) if plan else vec_block],
-            (ids, got_crops, segment_ids, *weights, crops[0]),
-            smem=1,
+            (got_crops, segment_ids, *weights, crops[0]),
             hbm=1,
             copies=1,
         )
@@ -719,8 +726,7 @@
             functools.partial(query_mlp_kernel, scatter, plan, shard),
             [((rows, width), BF16), (grads_2, BF16), (grads_2, BF16), wide_f, col_block],
             [wide_f, wide_f, wide_b, wide_b] + ([(w2_shape, BF16)] if plan else []) + [crop_block],
-            (ids, res, cols, *weights, cotangent),
-            smem=1,
+            (res, cols, *weights, cotangent),
             hbm=1,
             copies=1,
         )
@@ -733,8 +739,7 @@
             + [score_block] * nseq
             + [((slots, slots), BF16)] * nseq
             + [((8, slots), F32)] * nseq,
-            (ids, d_res, vgrad, cols, *saved),
-            smem=1,
+            (d_res, vgrad, cols, *saved),
         )
 
     def momentum_mlp(plan, weights, res_m, cols, out_q):
@@ -742,8 +747,7 @@
             functools.partial(momentum_mlp_kernel, plan, shard),
             [((rows, width), BF16)] * 3,
             [wide_f] + ([(w2_shape, BF16)] if plan else []),
-            (ids, res_m, cols, out_q, *weights),
-            smem=1,
+            (res_m, cols, out_q, *weights),
         )
 
     shards = (
@@ -760,14 +764,13 @@
     if fine:
         block = ((shard, width + 128 + units), BF16)
         keep, send = call(
-            pack_kernel, [block] * 2, [(x.shape, F32) for x in shards], (ids, *shards), smem=1, hbm=6, copies=6, limit=56
+            pack_kernel, [block] * 2, [(x.shape, F32) for x in shards], shards, hbm=6, copies=6, limit=56
         )
         block_1, block_2 = call(
             functools.partial(split_kernel, width),
             [((shard, 2 * width + 128), BF16), ((shard, 2 * units), BF16)],
             [block],
-            (ids, swap_cores(send), keep),
-            smem=1,
+            (swap_cores(send), keep),
             hbm=1,
             copies=1,
         )
@@ -778,13 +781,20 @@
         stack_1, got_crops = after((jnp.stack([block_1, *far_1]), got_crops))
         own_1 = [stack_1] + [exchange(stack_1, *peer) for peer in both_ways]
         got_1 = [swap_cores(x) for x in own_1]
-        parts = [block_2] + [exchange(block_2, *peer) for peer in near]
-        stack_q, stack_m = (jnp.stack([x[..., cols] for x in parts]) for cols in (slice(0, units), slice(units, None)))
+        parts = after([block_2] + [exchange(block_2, *peer) for peer in near], own_1[1], own_1[2])
+        stack_q, stack_a, stack_b = (
+            jnp.stack([x[..., start : start + wide] for x in parts])
+            for start, wide in ((0, units), (units, units // 2), (units + units // 2, units // 2))
+        )
+        by_y = [[((v, j), (m ^ n, v)) for v in range(2) for j, (m, _) in enumerate(masks)] for n in range(2)]
+        by_x = [[((n, j), (m ^ n, v)) for n in range(2) for j, (m, _) in enumerate(masks)] for v in range(2)]
         own_q = [stack_q] + [exchange(stack_q, *peer) for peer in both_ways]
-        res, res_m, cols, *saved = attention(plan, own_1 + got_1, after(got_crops, stack_q, stack_m))
-        own_q, res, res_m, stack_m = after((own_q, res, res_m, stack_m))
+        got_a, got_b = exchange(stack_a, 0, 1), exchange(stack_b, 1, 0)
+        res, res_m, cols, *saved = attention(plan, own_1 + got_1, after(got_crops, stack_q, stack_a, stack_b))
+        own_q, got_a, got_b, res, res_m = after((own_q, got_a, got_b, res, res_m))
         got_q = [swap_cores(x) for x in own_q]
-        own_m = [stack_m] + [exchange(stack_m, *peer) for peer in both_ways]
+        stack_a, stack_b = jnp.stack([stack_a, got_a]), jnp.stack([stack_b, got_b])
+        own_m = [stack_a, exchange(stack_a, 1, 0), stack_b, exchange(stack_b, 0, 1)]
         out_q, keep_g2, send_g2, d_res, vgrad = query_mlp(plan, own_q + got_q, res, cols)
         own_m, out_q, keep_g2, send_g2, d_res, vgrad = after((own_m, out_q, keep_g2, send_g2, d_res, vgrad))
         got_m = [swap_cores(x) for x in own_m]
@@ -794,7 +804,7 @@
         mlp_got = exchange(mlp_send, 1, 0)
         far_q = exchange(out_q, 0, 1)
         res_m = after(res_m, mlp_own)
-        out_m, out_own, out_send = momentum_mlp(plan, own_m + got_m, res_m, cols, out_q)
+        out_m, out_own, out_send = momentum_mlp((by_y, by_x), own_m + got_m, res_m, cols, out_q)
         far_q, out_m, out_send = after((far_q, out_m, out_send))
         far_m = exchange(out_m, 0, 1)
         crop_keep, crop_send, keep_g1, send_g1 = query_back(after(d_res, out_m), vgrad, cols, saved)
@@ -809,7 +819,7 @@
         attn_got = [exchange(x, *peer) for x, peer in zip(attn_sends, [(0, 1), (1, 0), (1, 1)])]
         half = (nseq, width // 2, slots)
         crop_got = swap_cores(crop_send)
-        (pair,) = call(crop_pair_kernel, [((2, *half), BF16)], [], (ids, crop_keep, crop_got), smem=1)
+        (pair,) = call(crop_pair_kernel, [((2, *half), BF16)], [], (crop_keep, crop_got))
         attn_got, mlp_got, pair = after((attn_got, mlp_got, pair))
         crop_far = exchange(pair, 0, 1)
         wide = 2 * units + grads_1[3]
@@ -820,6 +830,10 @@
             (mlp_own, mlp_got, attn_own, *attn_got),
         )
         got = [exchange(x, *peer) for x, peer in zip(sends, near)]
+        (crop_grad,) = call(
+            crop_kernel, [((tensors, 2, *half), F32)], [], (crop_keep, crop_got, crop_far)
+        )
+        got, crop_grad = after((got, crop_grad))
         qkv_grad, out_grad, up_grad, down_grad, gain_grad, bias_grad = call(
             functools.partial(shares_kernel, units, group),
             [
@@ -834,17 +848,13 @@
             (own, *got),
         )
         qkv_grad, out_grad, down_grad = qkv_grad.transpose(1, 0, 2), out_grad.T, down_grad.T
-        (crop_grad,) = call(
-            crop_kernel, [((tensors, 2, *half), F32)], [], (ids, crop_keep, crop_got, crop_far), smem=1
-        )
         crop_grad = crop_grad.reshape(sequences, width // 2, slots).transpose(0, 2, 1)
-        far_own, far_send = call(pick_kernel, [((rows, width), BF16)] * 2, [], (ids, far_q, far_m), smem=1)
+        far_own, far_send = call(pick_kernel, [((rows, width), BF16)] * 2, [], (far_q, far_m))
         (encoded,) = call(
             encoded_kernel,
             [((tensors, 2, rows, width), BF16)],
             [],
-            (ids, out_own, far_own, swap_cores(out_send), swap_cores(far_send)),
-            smem=1,
+            (out_own, far_own, swap_cores(out_send), swap_cores(far_send)),
             hbm=4,
             hbm_outs=1,
             copies=4,

time: 131 us -> 123 us (0.939)
  Pallas kernels: 43.7 us -> 33.1 us
  waiting for transfers between devices: 37.4 us -> 46.7 us
  starting transfers between devices: 45.2 us -> 39.8 us
    pallas_call x15, Pallas kernels: 43.7 us -> 33.1 us  [call(): pl.pallas_call(kernel, grid=(1,) if stream else (), out_shape=[jax.ShapeD...]
    ppermute x26 -> x27, waiting for transfers between devices: 36.6 us -> 44.5 us  [exchange(): return lax.ppermute(block, SPAN, pairs)]
    ppermute x26 -> x27, starting transfers between devices: 41.2 us -> 35.2 us  [exchange(): return lax.ppermute(block, SPAN, pairs)]
    ppermute x19, waiting for transfers between devices: 0.83 us -> 2.18 us  [swap_cores(): return lax.ppermute(block, 'branch', [(0, 1), (1, 0)])]
  transfers between devices with their start and end apart: 45 -> 46, of which waited for: 14 -> 16; matrix products, arithmetic and copies ran while one was open for 1% -> 0% of each run, Pallas kernels for 30% -> 26%
where the time goes in v4:
time: 123 us
  waiting for transfers between devices  46.7 us (38%)
  starting transfers between devices  39.8 us (32%)
  Pallas kernels  33.1 us (27%)
  local copies, waits for them, and re-layouts  2.01 us (2%)
    ppermute x27, waiting for transfers between devices, exchange(): return lax.ppermute(block, SPAN, pairs)  44.5 us
    ppermute x27, starting transfers between devices, exchange(): return lax.ppermute(block, SPAN, pairs)  35.2 us
    pallas_call x15, Pallas kernels, call(): pl.pallas_call(kernel, grid=(1,) if stream else (), out_shape=[jax.ShapeD...  33.1 us
    ppermute x19, starting transfers between devices, swap_cores(): return lax.ppermute(block, 'branch', [(0, 1), (1, 0)])  4.59 us
  transfers between devices with their start and end apart: 46, of which 16 were waited for; matrix products, arithmetic and copies ran while one was open for 0% of the time, Pallas kernels for 26%

profile of v4, /device:TPU:0, one launch (start us, length us, event | category | flops | bytes accessed | tf_op | source)
XLA Modules:
  0.0 122.7 jit_solution(17653400250113285313)
XLA Ops:
  2.2 1.9 %shard_map.152 = (bf16[48,1280]{1,0:T(8,128)(2,1)}, bf16[48,1280]{1,0:T(8,128)(2,1)}) custom-call(f32[3,48,192]{2,1,0:T(8,128)} %bitcast.60, f32[48,192]{1,0:T(8,128)} %bitcast.68, f32[48,768]{1,0:T(8,128)} %bitcast.61, f32[48,768]{1,0:T(8,128)} %bitcast.62, f32[2,48]{1,0:T(2,128)} %bitcast.70, f32[4,48]{1,0:T(4,128)} %bitcast.69), custom_call_target="tpu_custom_call" | custom-call | tf_op jit(solution)/shard_map/pallas_call | solution.py:533
  4.3 1.5 %collective-permute-done.got_ref = bf16[48,1280]{1,0:T(8,128)(2,1)S(1)} collective-permute-done((bf16[48,1280]{1,0:T(8,128)(2,1)}, bf16[48,1280]{1,0:T(8,128)(2,1)S(1)}, u32[]{:S(2)}, u32[]{:S(2)}) %collective-permute-start) | collective-permute-done | bytes 122912 | tf_op jit(solution)/shard_map/ppermute | solution.py:549
  6.8 2.8 %collective-permute-start.4 = (bf16[48,896]{1,0:T(8,128)(2,1)S(1)}, bf16[48,896]{1,0:T(8,128)(2,1)S(1)}, u32[]{:S(2)}, u32[]{:S(2)}) collective-permute-start(bf16[48,896]{1,0:T(8,128)(2,1)S(1)} %get-tuple-element.103), channel_id=1, source_target_pairs={{0,4},{1,5},{2,6},{3,7},{4,0},{5,1},{6,2},{7,3},{8,12},{9,13},{10,... | collective-permute-start | bytes 258056 | tf_op jit(solution)/shard_map/ppermute | solution.py:557
  9.6 2.6 %collective-permute-start.5 = (bf16[48,896]{1,0:T(8,128)(2,1)S(1)}, bf16[48,896]{1,0:T(8,128)(2,1)S(1)}, u32[]{:S(2)}, u32[]{:S(2)}) collective-permute-start(bf16[48,896]{1,0:T(8,128)(2,1)S(1)} %get-tuple-element.103), channel_id=1, source_target_pairs={{0,8},{1,9},{2,10},{3,11},{4,12},{5,13},{6,14},{7,15},{8,0},{9,1},... | collective-permute-start | bytes 258056 | tf_op jit(solution)/shard_map/ppermute | solution.py:557
  12.7 6.7 %collective-permute-done.5 = bf16[48,896]{1,0:T(8,128)(2,1)S(1)} collective-permute-done((bf16[48,896]{1,0:T(8,128)(2,1)S(1)}, bf16[48,896]{1,0:T(8,128)(2,1)S(1)}, u32[]{:S(2)}, u32[]{:S(2)}) %collective-permute-start.5) | collective-permute-done | bytes 86048 | tf_op jit(solution)/shard_map/ppermute | solution.py:557
  19.4 1.6 %collective-permute-start.8 = (bf16[4,48,896]{2,1,0:T(8,128)(2,1)S(1)}, bf16[4,48,896]{2,1,0:T(8,128)(2,1)S(1)}, u32[]{:S(2)}, u32[]{:S(2)}) collective-permute-start(bf16[4,48,896]{2,1,0:T(8,128)(2,1)S(1)} %pad_maximum_fusion.refs_2_), channel_id=1, source_target_pairs={{0,2},{1,3},{2,0},{3,1},{4,6},{5,7},{6,4},{7,5},{8,10},{9,11},{10,... | collective-permute-start | bytes 1032200 | tf_op jit(solution)/shard_map/ppermute | solution.py:557
  21.0 1.5 %collective-permute-start.9 = (bf16[4,48,896]{2,1,0:T(8,128)(2,1)S(1)}, bf16[4,48,896]{2,1,0:T(8,128)(2,1)S(1)}, u32[]{:S(2)}, u32[]{:S(2)}) collective-permute-start(bf16[4,48,896]{2,1,0:T(8,128)(2,1)S(1)} %pad_maximum_fusion.refs_2_), channel_id=1, source_target_pairs={{0,1},{1,0},{2,3},{3,2},{4,5},{5,4},{6,7},{7,6},{8,9},{9,8},{10,11... | collective-permute-start | bytes 1032200 | tf_op jit(solution)/shard_map/ppermute | solution.py:557
  22.5 1.8 %collective-permute-start.1 = (bf16[48,1536]{1,0:T(8,128)(2,1)S(1)}, bf16[48,1536]{1,0:T(8,128)(2,1)S(1)}, u32[]{:S(2)}, u32[]{:S(2)}) collective-permute-start(bf16[48,1536]{1,0:T(8,128)(2,1)S(1)} %get-tuple-element.105), channel_id=1, source_target_pairs={{0,4},{1,5},{2,6},{3,7},{4,0},{5,1},{6,2},{7,3},{8,12},{9,13},{10,... | collective-permute-start | bytes 442376 | tf_op jit(solution)/shard_map/ppermute | solution.py:557
  24.3 1.6 %collective-permute-start.2 = (bf16[48,1536]{1,0:T(8,128)(2,1)S(1)}, bf16[48,1536]{1,0:T(8,128)(2,1)S(1)}, u32[]{:S(2)}, u32[]{:S(2)}) collective-permute-start(bf16[48,1536]{1,0:T(8,128)(2,1)S(1)} %get-tuple-element.105), channel_id=1, source_target_pairs={{0,8},{1,9},{2,10},{3,11},{4,12},{5,13},{6,14},{7,15},{8,0},{9,1},... | collective-permute-start | bytes 442376 | tf_op jit(solution)/shard_map/ppermute | solution.py:557
  26.9 2.3 %collective-permute-done.1 = bf16[48,1536]{1,0:T(8,128)(2,1)S(1)} collective-permute-done((bf16[48,1536]{1,0:T(8,128)(2,1)S(1)}, bf16[48,1536]{1,0:T(8,128)(2,1)S(1)}, u32[]{:S(2)}, u32[]{:S(2)}) %collective-permute-start.1) | collective-permute-done | bytes 147488 | tf_op jit(solution)/shard_map/ppermute | solution.py:557
  29.7 7.6 %collective-permute-done.2 = bf16[48,1536]{1,0:T(8,128)(2,1)S(1)} collective-permute-done((bf16[48,1536]{1,0:T(8,128)(2,1)S(1)}, bf16[48,1536]{1,0:T(8,128)(2,1)S(1)}, u32[]{:S(2)}, u32[]{:S(2)}) %collective-permute-start.2) | collective-permute-done | bytes 147488 | tf_op jit(solution)/shard_map/ppermute | solution.py:557
  39.7 2.4 %collective-permute-start.12 = (bf16[4,48,768]{2,1,0:T(8,128)(2,1)S(1)}, bf16[4,48,768]{2,1,0:T(8,128)(2,1)S(1)}, u32[]{:S(2)}, u32[]{:S(2)}) collective-permute-start(bf16[4,48,768]{2,1,0:T(8,128)(2,1)S(1)} %pad_maximum_fusion.1.refs_2_), channel_id=1, source_target_pairs={{0,3},{1,2},{2,1},{3,0},{4,7},{5,6},{6,5},{7,4},{8,11},{9,10},{10,... | collective-permute-start | bytes 884744 | tf_op jit(solution)/shard_map/ppermute | solution.py:557
  43.4 9.8 %shard_map.154 = (f32[384,512]{1,0:T(8,128)S(1)}, f32[384,512]{1,0:T(8,128)S(1)}, f32[384,128]{1,0:T(8,128)S(1)}, bf16[2,2,384,384]{3,2,1,0:T(8,128)(2,1)S(1)}, ...) custom-call(bf16[512,384]{1,0:T(8,128)(2,1)S(1)} %collective-permute, ...), custom_call_target="tpu_custom_call" | custom-call | tf_op jit(solution)/shard_map/pallas_call | solution.py:533
  53.2 4.0 %collective-permute-done.14 = bf16[4,48,384]{2,1,0:T(8,128)(2,1)S(1)} collective-permute-done((bf16[4,48,384]{2,1,0:T(8,128)(2,1)S(1)}, bf16[4,48,384]{2,1,0:T(8,128)(2,1)S(1)}, u32[]{:S(2)}, u32[]{:S(2)}) %collective-permute-start.14) | collective-permute-done | bytes 147488 | tf_op jit(solution)/shard_map/ppermute | solution.py:557
  59.3 1.6 %collective-permute-start.20 = (bf16[2,4,48,384]{3,2,1,0:T(8,128)(2,1)S(1)}, bf16[2,4,48,384]{3,2,1,0:T(8,128)(2,1)S(1)}, u32[]{:S(2)}, u32[]{:S(2)}) collective-permute-start(bf16[2,4,48,384]{3,2,1,0:T(8,128)(2,1)S(1)} %pad_maximum_fusion.2.refs_3_), channel_id=1, source_target_pairs={{0,2},{1,3},{2,0},{3,1},{4,6},{5,7},{6,4},{7,5},{8,10},{9,11},{10,... | collective-permute-start | bytes 884744 | tf_op jit(solution)/shard_map/ppermute | solution.py:557
  60.9 7.5 %shard_map.155 = (bf16[512,384]{1,0:T(8,128)(2,1)S(1)}, bf16[4,4,24,1536]{3,2,1,0:T(8,128)(2,1)S(1)}, bf16[4,4,24,1536]{3,2,1,0:T(8,128)(2,1)S(1)}, f32[384,512]{1,0:T(8,128)S(1)}, f32[384,128]{1,0:T(8,128)S(1)}) custom-call(f32[384,512]{1,0:T(8,128)S(1)} %get-tuple-element.116.refs_0_, f32[384,128]{1,0:T(8,128)S(1)} %get-tuple-element.117.refs_1_.refs_2_, ...), custom_call_target="tpu_custom_call" | custom-call | tf_op jit(solution)/shard_map/pallas_call | solution.py:533
  69.0 1.4 %collective-permute-start.31 = (bf16[512,384]{1,0:T(8,128)(2,1)S(1)}, bf16[512,384]{1,0:T(8,128)(2,1)S(1)}, u32[]{:S(2)}, u32[]{:S(2)}) collective-permute-start(bf16[512,384]{1,0:T(8,128)(2,1)S(1)} %get-tuple-element.131.refs_2_), channel_id=1, source_target_pairs={{0,1},{1,0},{2,3},{3,2},{4,5},{5,4},{6,7},{7,6},{8,9},{9,8},{10,11... | collective-permute-start | bytes 1179656 | tf_op jit(solution)/shard_map/ppermute | solution.py:557
  73.0 3.6 %shard_map.157 = (bf16[512,384]{1,0:T(8,128)(2,1)S(1)}, bf16[512,384]{1,0:T(8,128)(2,1)S(1)}, bf16[512,384]{1,0:T(8,128)(2,1)S(1)}) custom-call(f32[384,512]{1,0:T(8,128)S(1)} %get-tuple-element.130.refs_0_, f32[384,128]{1,0:T(8,128)S(1)} %get-tuple-element.117.refs_1_.refs_2_, bf16[512,384]{1,0:T(8,128)(2,1)S(1)} %get-tuple-element.131.refs_2_, ...), custom_call_target="tpu_custom_call" | custom-call | tf_op jit(solution)/shard_map/pallas_call | solution.py:533
  76.7 3.4 %collective-permute-done.31.query_ref = bf16[512,384]{1,0:T(8,128)(2,1)S(1)} collective-permute-done((bf16[512,384]{1,0:T(8,128)(2,1)S(1)}, bf16[512,384]{1,0:T(8,128)(2,1)S(1)}, u32[]{:S(2)}, u32[]{:S(2)}) %collective-permute-start.31) | collective-permute-done | bytes 393248 | tf_op jit(solution)/shard_map/ppermute | solution.py:557
  80.1 1.4 %collective-permute-start.33 = (bf16[512,384]{1,0:T(8,128)(2,1)S(1)}, bf16[512,384]{1,0:T(8,128)(2,1)S(1)}, u32[]{:S(2)}, u32[]{:S(2)}) collective-permute-start(bf16[512,384]{1,0:T(8,128)(2,1)S(1)} %get-tuple-element.141), channel_id=1, source_target_pairs={{0,1},{1,0},{2,3},{3,2},{4,5},{5,4},{6,7},{7,6},{8,9},{9,8},{10,11... | collective-permute-start | bytes 1179656 | tf_op jit(solution)/shard_map/ppermute | solution.py:557
  81.5 6.0 %shard_map.158 = (f32[2,192,256]{2,1,0:T(8,128)S(1)}, bf16[2,192,256]{2,1,0:T(8,128)(2,1)S(1)}, bf16[4,4,24,896]{3,2,1,0:T(8,128)(2,1)S(1)}, bf16[4,4,24,896]{3,2,1,0:T(8,128)(2,1)S(1)}) custom-call(f32[384,512]{1,0:T(8,128)S(1)} %get-tuple-element.143.refs_0_, f32[384,128]{1,0:T(8,128)S(1)} %get-tuple-element.144.refs_1_, ...), custom_call_target="tpu_custom_call" | custom-call | tf_op jit(solution)/shard_map/pallas_call | solution.py:533
  87.5 2.8 %collective-permute-done.33.momentum_ref = bf16[512,384]{1,0:T(8,128)(2,1)S(1)} collective-permute-done((bf16[512,384]{1,0:T(8,128)(2,1)S(1)}, bf16[512,384]{1,0:T(8,128)(2,1)S(1)}, u32[]{:S(2)}, u32[]{:S(2)}) %collective-permute-start.33) | collective-permute-done | bytes 393248 | tf_op jit(solution)/shard_map/ppermute | solution.py:557
  91.0 1.4 %collective-permute-start.40 = (bf16[4,24,1536]{2,1,0:T(8,128)(2,1)S(1)}, bf16[4,24,1536]{2,1,0:T(8,128)(2,1)S(1)}, u32[]{:S(2)}, u32[]{:S(2)}) collective-permute-start(bf16[4,24,1536]{2,1,0:T(8,128)(2,1)S(1)} %get-tuple-element.169), channel_id=1, source_target_pairs={{0,1},{1,0},{2,3},{3,2},{4,5},{5,4},{6,7},{7,6},{8,9},{9,8},{10,11... | collective-permute-start | bytes 884744 | tf_op jit(solution)/shard_map/ppermute | solution.py:557
  92.7 1.4 %collective-permute-start.37 = (bf16[4,24,896]{2,1,0:T(8,128)(2,1)S(1)}, bf16[4,24,896]{2,1,0:T(8,128)(2,1)S(1)}, u32[]{:S(2)}, u32[]{:S(2)}) collective-permute-start(bf16[4,24,896]{2,1,0:T(8,128)(2,1)S(1)} %get-tuple-element.166), channel_id=1, source_target_pairs={{0,1},{1,0},{2,3},{3,2},{4,5},{5,4},{6,7},{7,6},{8,9},{9,8},{10,11... | collective-permute-start | bytes 516104 | tf_op jit(solution)/shard_map/ppermute | solution.py:557
  96.4 8.2 %collective-permute-done.40.refs_1_ = bf16[4,24,1536]{2,1,0:T(8,128)(2,1)S(1)} collective-permute-done((bf16[4,24,1536]{2,1,0:T(8,128)(2,1)S(1)}, bf16[4,24,1536]{2,1,0:T(8,128)(2,1)S(1)}, u32[]{:S(2)}, u32[]{:S(2)}) %collective-permute-start.40) | collective-permute-done | bytes 294944 | tf_op jit(solution)/shard_map/ppermute | solution.py:557
  104.6 2.7 %collective-permute-done.37.refs_3_ = bf16[4,24,896]{2,1,0:T(8,128)(2,1)S(1)} collective-permute-done((bf16[4,24,896]{2,1,0:T(8,128)(2,1)S(1)}, bf16[4,24,896]{2,1,0:T(8,128)(2,1)S(1)}, u32[]{:S(2)}, u32[]{:S(2)}) %collective-permute-start.37) | collective-permute-done | bytes 172064 | tf_op jit(solution)/shard_map/ppermute | solution.py:557
  107.4 1.4 %collective-permute-start.45 = (bf16[2,2,192,256]{3,2,1,0:T(8,128)(2,1)S(1)}, bf16[2,2,192,256]{3,2,1,0:T(8,128)(2,1)S(1)}, u32[]{:S(2)}, u32[]{:S(2)}) collective-permute-start(bf16[2,2,192,256]{3,2,1,0:T(8,128)(2,1)S(1)} %shard_map.163), channel_id=1, source_target_pairs={{0,1},{1,0},{2,3},{3,2},{4,5},{5,4},{6,7},{7,6},{8,9},{9,8},{10,11... | collective-permute-start | bytes 1179656 | tf_op jit(solution)/shard_map/ppermute | solution.py:557
  108.9 2.3 %collective-permute-start.42 = (bf16[24,2432]{1,0:T(8,128)(2,1)S(1)}, bf16[24,2432]{1,0:T(8,128)(2,1)S(1)}, u32[]{:S(2)}, u32[]{:S(2)}) collective-permute-start(bf16[24,2432]{1,0:T(8,128)(2,1)S(1)} %get-tuple-element.177), channel_id=1, source_target_pairs={{0,4},{1,5},{2,6},{3,7},{4,0},{5,1},{6,2},{7,3},{8,12},{9,13},{10,... | collective-permute-start | bytes 350216 | tf_op jit(solution)/shard_map/ppermute | solution.py:557
  112.0 1.6 %collective-permute-start.44 = (bf16[24,2432]{1,0:T(8,128)(2,1)S(1)}, bf16[24,2432]{1,0:T(8,128)(2,1)S(1)}, u32[]{:S(2)}, u32[]{:S(2)}) collective-permute-start(bf16[24,2432]{1,0:T(8,128)(2,1)S(1)} %get-tuple-element.179), channel_id=1, source_target_pairs={{0,12},{1,13},{2,14},{3,15},{4,8},{5,9},{6,10},{7,11},{8,4},{9,5},... | collective-permute-start | bytes 350216 | tf_op jit(solution)/shard_map/ppermute | solution.py:557
  114.8 2.7 %collective-permute-done.45.far_ref = bf16[2,2,192,256]{3,2,1,0:T(8,128)(2,1)S(1)} collective-permute-done((bf16[2,2,192,256]{3,2,1,0:T(8,128)(2,1)S(1)}, bf16[2,2,192,256]{3,2,1,0:T(8,128)(2,1)S(1)}, u32[]{:S(2)}, u32[]{:S(2)}) %collective-permute-start.45) | collective-permute-done | bytes 393248 | tf_op jit(solution)/shard_map/ppermute | solution.py:557
  117.5 1.3 %shard_map.165 = f32[2,2,2,192,256]{4,3,2,1,0:T(8,128)} custom-call(f32[2,192,256]{2,1,0:T(8,128)S(1)} %get-tuple-element.170.keep_ref, bf16[2,192,256]{2,1,0:T(8,128)(2,1)S(1)} %collective-permute-done.41.got_ref, bf16[2,2,192,256]{3,2,1,0:T(8,128)(2,1)S(1)} %collective-permute-done.45.far_ref), custom_call_target="tpu_custom_call" | custom-call | tf_op jit(solution)/shard_map/pallas_call | solution.py:533
  118.8 3.2 %collective-permute-done.43.refs_2_ = bf16[24,2432]{1,0:T(8,128)(2,1)S(1)} collective-permute-done((bf16[24,2432]{1,0:T(8,128)(2,1)S(1)}, bf16[24,2432]{1,0:T(8,128)(2,1)S(1)}, u32[]{:S(2)}, u32[]{:S(2)}) %collective-permute-start.43) | collective-permute-done | bytes 116768 | tf_op jit(solution)/shard_map/ppermute | solution.py:557
  (94 shorter events, 19.7 us)
Async XLA Ops:
  1.7 17.7 %collective-permute-start.7 = (bf16[512,384]{1,0:T(8,128)(2,1)S(1)}, bf16[512,384]{1,0:T(8,128)(2,1)S(1)}, u32[]{:S(2)}, u32[]{:S(2)}) collective-permute-start(bf16[512,384]{1,0:T(8,128)(2,1)S(1)} %bitcast.59), channel_id=1, source_target_pairs={{0,16},{16,0},{1,17},{17,1},{2,18},{18,2},{3,19},{19,3},{4,20},{20... | collective-permute-start | bytes 1179656 | tf_op jit(solution)/shard_map/ppermute | solution.py:549
  6.8 5.8 %collective-permute-start.4 = (bf16[48,896]{1,0:T(8,128)(2,1)S(1)}, bf16[48,896]{1,0:T(8,128)(2,1)S(1)}, u32[]{:S(2)}, u32[]{:S(2)}) collective-permute-start(bf16[48,896]{1,0:T(8,128)(2,1)S(1)} %get-tuple-element.103), channel_id=1, source_target_pairs={{0,4},{1,5},{2,6},{3,7},{4,0},{5,1},{6,2},{7,3},{8,12},{9,13},{10,... | collective-permute-start | bytes 258056 | tf_op jit(solution)/shard_map/ppermute | solution.py:557
  9.6 9.7 %collective-permute-start.5 = (bf16[48,896]{1,0:T(8,128)(2,1)S(1)}, bf16[48,896]{1,0:T(8,128)(2,1)S(1)}, u32[]{:S(2)}, u32[]{:S(2)}) collective-permute-start(bf16[48,896]{1,0:T(8,128)(2,1)S(1)} %get-tuple-element.103), channel_id=1, source_target_pairs={{0,8},{1,9},{2,10},{3,11},{4,12},{5,13},{6,14},{7,15},{8,0},{9,1},... | collective-permute-start | bytes 258056 | tf_op jit(solution)/shard_map/ppermute | solution.py:557
  12.2 7.1 %collective-permute-start.6 = (bf16[48,896]{1,0:T(8,128)(2,1)S(1)}, bf16[48,896]{1,0:T(8,128)(2,1)S(1)}, u32[]{:S(2)}, u32[]{:S(2)}) collective-permute-start(bf16[48,896]{1,0:T(8,128)(2,1)S(1)} %get-tuple-element.103), channel_id=1, source_target_pairs={{0,12},{1,13},{2,14},{3,15},{4,8},{5,9},{6,10},{7,11},{8,4},{9,5},... | collective-permute-start | bytes 258056 | tf_op jit(solution)/shard_map/ppermute | solution.py:557
  19.4 17.9 %collective-permute-start.8 = (bf16[4,48,896]{2,1,0:T(8,128)(2,1)S(1)}, bf16[4,48,896]{2,1,0:T(8,128)(2,1)S(1)}, u32[]{:S(2)}, u32[]{:S(2)}) collective-permute-start(bf16[4,48,896]{2,1,0:T(8,128)(2,1)S(1)} %pad_maximum_fusion.refs_2_), channel_id=1, source_target_pairs={{0,2},{1,3},{2,0},{3,1},{4,6},{5,7},{6,4},{7,5},{8,10},{9,11},{10,... | collective-permute-start | bytes 1032200 | tf_op jit(solution)/shard_map/ppermute | solution.py:557
  21.0 16.3 %collective-permute-start.9 = (bf16[4,48,896]{2,1,0:T(8,128)(2,1)S(1)}, bf16[4,48,896]{2,1,0:T(8,128)(2,1)S(1)}, u32[]{:S(2)}, u32[]{:S(2)}) collective-permute-start(bf16[4,48,896]{2,1,0:T(8,128)(2,1)S(1)} %pad_maximum_fusion.refs_2_), channel_id=1, source_target_pairs={{0,1},{1,0},{2,3},{3,2},{4,5},{5,4},{6,7},{7,6},{8,9},{9,8},{10,11... | collective-permute-start | bytes 1032200 | tf_op jit(solution)/shard_map/ppermute | solution.py:557
  22.5 6.7 %collective-permute-start.1 = (bf16[48,1536]{1,0:T(8,128)(2,1)S(1)}, bf16[48,1536]{1,0:T(8,128)(2,1)S(1)}, u32[]{:S(2)}, u32[]{:S(2)}) collective-permute-start(bf16[48,1536]{1,0:T(8,128)(2,1)S(1)} %get-tuple-element.105), channel_id=1, source_target_pairs={{0,4},{1,5},{2,6},{3,7},{4,0},{5,1},{6,2},{7,3},{8,12},{9,13},{10,... | collective-permute-start | bytes 442376 | tf_op jit(solution)/shard_map/ppermute | solution.py:557
  24.3 13.0 %collective-permute-start.2 = (bf16[48,1536]{1,0:T(8,128)(2,1)S(1)}, bf16[48,1536]{1,0:T(8,128)(2,1)S(1)}, u32[]{:S(2)}, u32[]{:S(2)}) collective-permute-start(bf16[48,1536]{1,0:T(8,128)(2,1)S(1)} %get-tuple-element.105), channel_id=1, source_target_pairs={{0,8},{1,9},{2,10},{3,11},{4,12},{5,13},{6,14},{7,15},{8,0},{9,1},... | collective-permute-start | bytes 442376 | tf_op jit(solution)/shard_map/ppermute | solution.py:557
  25.8 11.5 %collective-permute-start.3 = (bf16[48,1536]{1,0:T(8,128)(2,1)S(1)}, bf16[48,1536]{1,0:T(8,128)(2,1)S(1)}, u32[]{:S(2)}, u32[]{:S(2)}) collective-permute-start(bf16[48,1536]{1,0:T(8,128)(2,1)S(1)} %get-tuple-element.105), channel_id=1, source_target_pairs={{0,12},{1,13},{2,14},{3,15},{4,8},{5,9},{6,10},{7,11},{8,4},{9,5},... | collective-permute-start | bytes 442376 | tf_op jit(solution)/shard_map/ppermute | solution.py:557
  29.2 8.8 %collective-permute-start.15 = (bf16[4,48,896]{2,1,0:T(8,128)(2,1)S(1)}, bf16[4,48,896]{2,1,0:T(8,128)(2,1)S(1)}, u32[]{:S(2)}, u32[]{:S(2)}) collective-permute-start(bf16[4,48,896]{2,1,0:T(8,128)(2,1)S(1)} %pad_maximum_fusion.refs_2_), channel_id=1, source_target_pairs={{0,3},{1,2},{2,1},{3,0},{4,7},{5,6},{6,5},{7,4},{8,11},{9,10},{10,... | collective-permute-start | bytes 1032200 | tf_op jit(solution)/shard_map/ppermute | solution.py:557
  38.0 4.8 %collective-permute-start.19 = (bf16[4,48,896]{2,1,0:T(8,128)(2,1)S(1)}, bf16[4,48,896]{2,1,0:T(8,128)(2,1)S(1)}, u32[]{:S(2)}, u32[]{:S(2)}) collective-permute-start(bf16[4,48,896]{2,1,0:T(8,128)(2,1)S(1)} %collective-permute-done.15.refs_5_), channel_id=1, source_target_pairs={{0,16},{16,0},{1,17},{17,1},{2,18},{18,2},{3,19},{19,3},{4,20},{20... | collective-permute-start | bytes 1032200 | tf_op jit(solution)/shard_map/ppermute | solution.py:549
  38.6 18.9 %collective-permute-start.10 = (bf16[4,48,768]{2,1,0:T(8,128)(2,1)S(1)}, bf16[4,48,768]{2,1,0:T(8,128)(2,1)S(1)}, u32[]{:S(2)}, u32[]{:S(2)}) collective-permute-start(bf16[4,48,768]{2,1,0:T(8,128)(2,1)S(1)} %pad_maximum_fusion.1.refs_2_), channel_id=1, source_target_pairs={{0,2},{1,3},{2,0},{3,1},{4,6},{5,7},{6,4},{7,5},{8,10},{9,11},{10,... | collective-permute-start | bytes 884744 | tf_op jit(solution)/shard_map/ppermute | solution.py:557
  39.2 18.3 %collective-permute-start.11 = (bf16[4,48,768]{2,1,0:T(8,128)(2,1)S(1)}, bf16[4,48,768]{2,1,0:T(8,128)(2,1)S(1)}, u32[]{:S(2)}, u32[]{:S(2)}) collective-permute-start(bf16[4,48,768]{2,1,0:T(8,128)(2,1)S(1)} %pad_maximum_fusion.1.refs_2_), channel_id=1, source_target_pairs={{0,1},{1,0},{2,3},{3,2},{4,5},{5,4},{6,7},{7,6},{8,9},{9,8},{10,11... | collective-permute-start | bytes 884744 | tf_op jit(solution)/shard_map/ppermute | solution.py:557
  39.7 17.8 %collective-permute-start.12 = (bf16[4,48,768]{2,1,0:T(8,128)(2,1)S(1)}, bf16[4,48,768]{2,1,0:T(8,128)(2,1)S(1)}, u32[]{:S(2)}, u32[]{:S(2)}) collective-permute-start(bf16[4,48,768]{2,1,0:T(8,128)(2,1)S(1)} %pad_maximum_fusion.1.refs_2_), channel_id=1, source_target_pairs={{0,3},{1,2},{2,1},{3,0},{4,7},{5,6},{6,5},{7,4},{8,11},{9,10},{10,... | collective-permute-start | bytes 884744 | tf_op jit(solution)/shard_map/ppermute | solution.py:557
  42.3 14.9 %collective-permute-start.14 = (bf16[4,48,384]{2,1,0:T(8,128)(2,1)S(1)}, bf16[4,48,384]{2,1,0:T(8,128)(2,1)S(1)}, u32[]{:S(2)}, u32[]{:S(2)}) collective-permute-start(bf16[4,48,384]{2,1,0:T(8,128)(2,1)S(1)} %get-tuple-element.193), channel_id=1, source_target_pairs={{0,2},{1,3},{2,0},{3,1},{4,6},{5,7},{6,4},{7,5},{8,10},{9,11},{10,... | collective-permute-start | bytes 442376 | tf_op jit(solution)/shard_map/ppermute | solution.py:557
  42.9 14.6 %collective-permute-start.13 = (bf16[4,48,384]{2,1,0:T(8,128)(2,1)S(1)}, bf16[4,48,384]{2,1,0:T(8,128)(2,1)S(1)}, u32[]{:S(2)}, u32[]{:S(2)}) collective-permute-start(bf16[4,48,384]{2,1,0:T(8,128)(2,1)S(1)} %get-tuple-element.195), channel_id=1, source_target_pairs={{0,1},{1,0},{2,3},{3,2},{4,5},{5,4},{6,7},{7,6},{8,9},{9,8},{10,11... | collective-permute-start | bytes 442376 | tf_op jit(solution)/shard_map/ppermute | solution.py:557
  58.6 9.8 %collective-permute-start.21 = (bf16[2,4,48,384]{3,2,1,0:T(8,128)(2,1)S(1)}, bf16[2,4,48,384]{3,2,1,0:T(8,128)(2,1)S(1)}, u32[]{:S(2)}, u32[]{:S(2)}) collective-permute-start(bf16[2,4,48,384]{3,2,1,0:T(8,128)(2,1)S(1)} %pad_maximum_fusion.3.refs_5_), channel_id=1, source_target_pairs={{0,1},{1,0},{2,3},{3,2},{4,5},{5,4},{6,7},{7,6},{8,9},{9,8},{10,11... | collective-permute-start | bytes 884744 | tf_op jit(solution)/shard_map/ppermute | solution.py:557
  59.3 9.1 %collective-permute-start.20 = (bf16[2,4,48,384]{3,2,1,0:T(8,128)(2,1)S(1)}, bf16[2,4,48,384]{3,2,1,0:T(8,128)(2,1)S(1)}, u32[]{:S(2)}, u32[]{:S(2)}) collective-permute-start(bf16[2,4,48,384]{3,2,1,0:T(8,128)(2,1)S(1)} %pad_maximum_fusion.2.refs_3_), channel_id=1, source_target_pairs={{0,2},{1,3},{2,0},{3,1},{4,6},{5,7},{6,4},{7,5},{8,10},{9,11},{10,... | collective-permute-start | bytes 884744 | tf_op jit(solution)/shard_map/ppermute | solution.py:557
  69.0 11.1 %collective-permute-start.31 = (bf16[512,384]{1,0:T(8,128)(2,1)S(1)}, bf16[512,384]{1,0:T(8,128)(2,1)S(1)}, u32[]{:S(2)}, u32[]{:S(2)}) collective-permute-start(bf16[512,384]{1,0:T(8,128)(2,1)S(1)} %get-tuple-element.131.refs_2_), channel_id=1, source_target_pairs={{0,1},{1,0},{2,3},{3,2},{4,5},{5,4},{6,7},{7,6},{8,9},{9,8},{10,11... | collective-permute-start | bytes 1179656 | tf_op jit(solution)/shard_map/ppermute | solution.py:557
  71.8 18.6 %collective-permute-start.32 = (bf16[2,4,24,1536]{3,2,1,0:T(8,128)(2,1)S(1)}, bf16[2,4,24,1536]{3,2,1,0:T(8,128)(2,1)S(1)}, u32[]{:S(2)}, u32[]{:S(2)}) collective-permute-start(bf16[2,4,24,1536]{3,2,1,0:T(8,128)(2,1)S(1)} %get-tuple-element.140), channel_id=1, source_target_pairs={{0,2},{1,3},{2,0},{3,1},{4,6},{5,7},{6,4},{7,5},{8,10},{9,11},{10,... | collective-permute-start | bytes 1769480 | tf_op jit(solution)/shard_map/ppermute | solution.py:557
  80.1 10.3 %collective-permute-start.33 = (bf16[512,384]{1,0:T(8,128)(2,1)S(1)}, bf16[512,384]{1,0:T(8,128)(2,1)S(1)}, u32[]{:S(2)}, u32[]{:S(2)}) collective-permute-start(bf16[512,384]{1,0:T(8,128)(2,1)S(1)} %get-tuple-element.141), channel_id=1, source_target_pairs={{0,1},{1,0},{2,3},{3,2},{4,5},{5,4},{6,7},{7,6},{8,9},{9,8},{10,11... | collective-permute-start | bytes 1179656 | tf_op jit(solution)/shard_map/ppermute | solution.py:557
  90.4 5.9 %collective-permute-start.41 = (bf16[2,192,256]{2,1,0:T(8,128)(2,1)S(1)}, bf16[2,192,256]{2,1,0:T(8,128)(2,1)S(1)}, u32[]{:S(2)}, u32[]{:S(2)}) collective-permute-start(bf16[2,192,256]{2,1,0:T(8,128)(2,1)S(1)} %get-tuple-element.171), channel_id=1, source_target_pairs={{0,16},{16,0},{1,17},{17,1},{2,18},{18,2},{3,19},{19,3},{4,20},{20... | collective-permute-start | bytes 589832 | tf_op jit(solution)/shard_map/ppermute | solution.py:549
  91.0 13.6 %collective-permute-start.40 = (bf16[4,24,1536]{2,1,0:T(8,128)(2,1)S(1)}, bf16[4,24,1536]{2,1,0:T(8,128)(2,1)S(1)}, u32[]{:S(2)}, u32[]{:S(2)}) collective-permute-start(bf16[4,24,1536]{2,1,0:T(8,128)(2,1)S(1)} %get-tuple-element.169), channel_id=1, source_target_pairs={{0,1},{1,0},{2,3},{3,2},{4,5},{5,4},{6,7},{7,6},{8,9},{9,8},{10,11... | collective-permute-start | bytes 884744 | tf_op jit(solution)/shard_map/ppermute | solution.py:557
  92.7 14.7 %collective-permute-start.37 = (bf16[4,24,896]{2,1,0:T(8,128)(2,1)S(1)}, bf16[4,24,896]{2,1,0:T(8,128)(2,1)S(1)}, u32[]{:S(2)}, u32[]{:S(2)}) collective-permute-start(bf16[4,24,896]{2,1,0:T(8,128)(2,1)S(1)} %get-tuple-element.166), channel_id=1, source_target_pairs={{0,1},{1,0},{2,3},{3,2},{4,5},{5,4},{6,7},{7,6},{8,9},{9,8},{10,11... | collective-permute-start | bytes 516104 | tf_op jit(solution)/shard_map/ppermute | solution.py:557
  94.1 13.2 %collective-permute-start.38 = (bf16[4,24,896]{2,1,0:T(8,128)(2,1)S(1)}, bf16[4,24,896]{2,1,0:T(8,128)(2,1)S(1)}, u32[]{:S(2)}, u32[]{:S(2)}) collective-permute-start(bf16[4,24,896]{2,1,0:T(8,128)(2,1)S(1)} %get-tuple-element.167), channel_id=1, source_target_pairs={{0,2},{1,3},{2,0},{3,1},{4,6},{5,7},{6,4},{7,5},{8,10},{9,11},{10,... | collective-permute-start | bytes 516104 | tf_op jit(solution)/shard_map/ppermute | solution.py:557
  95.0 12.3 %collective-permute-start.39 = (bf16[4,24,896]{2,1,0:T(8,128)(2,1)S(1)}, bf16[4,24,896]{2,1,0:T(8,128)(2,1)S(1)}, u32[]{:S(2)}, u32[]{:S(2)}) collective-permute-start(bf16[4,24,896]{2,1,0:T(8,128)(2,1)S(1)} %get-tuple-element.168), channel_id=1, source_target_pairs={{0,3},{1,2},{2,1},{3,0},{4,7},{5,6},{6,5},{7,4},{8,11},{9,10},{10,... | collective-permute-start | bytes 516104 | tf_op jit(solution)/shard_map/ppermute | solution.py:557
  96.2 15.8 %collective-permute-start.34 = (bf16[512,384]{1,0:T(8,128)(2,1)S(1)}, bf16[512,384]{1,0:T(8,128)(2,1)S(1)}, u32[]{:S(2)}, u32[]{:S(2)}) collective-permute-start(bf16[512,384]{1,0:T(8,128)(2,1)S(1)} %get-tuple-element.160), channel_id=1, source_target_pairs={{0,16},{16,0},{1,17},{17,1},{2,18},{18,2},{3,19},{19,3},{4,20},{20... | collective-permute-start | bytes 1179656 | tf_op jit(solution)/shard_map/ppermute | solution.py:549
  104.6 9.0 %collective-permute-start.35 = (bf16[512,384]{1,0:T(8,128)(2,1)S(1)}, bf16[512,384]{1,0:T(8,128)(2,1)S(1)}, u32[]{:S(2)}, u32[]{:S(2)}) collective-permute-start(bf16[512,384]{1,0:T(8,128)(2,1)S(1)} %get-tuple-element.161), channel_id=1, source_target_pairs={{0,16},{16,0},{1,17},{17,1},{2,18},{18,2},{3,19},{19,3},{4,20},{20... | collective-permute-start | bytes 1179656 | tf_op jit(solution)/shard_map/ppermute | solution.py:549
  107.4 10.2 %collective-permute-start.45 = (bf16[2,2,192,256]{3,2,1,0:T(8,128)(2,1)S(1)}, bf16[2,2,192,256]{3,2,1,0:T(8,128)(2,1)S(1)}, u32[]{:S(2)}, u32[]{:S(2)}) collective-permute-start(bf16[2,2,192,256]{3,2,1,0:T(8,128)(2,1)S(1)} %shard_map.163), channel_id=1, source_target_pairs={{0,1},{1,0},{2,3},{3,2},{4,5},{5,4},{6,7},{7,6},{8,9},{9,8},{10,11... | collective-permute-start | bytes 1179656 | tf_op jit(solution)/shard_map/ppermute | solution.py:557
  108.9 9.9 %collective-permute-start.42 = (bf16[24,2432]{1,0:T(8,128)(2,1)S(1)}, bf16[24,2432]{1,0:T(8,128)(2,1)S(1)}, u32[]{:S(2)}, u32[]{:S(2)}) collective-permute-start(bf16[24,2432]{1,0:T(8,128)(2,1)S(1)} %get-tuple-element.177), channel_id=1, source_target_pairs={{0,4},{1,5},{2,6},{3,7},{4,0},{5,1},{6,2},{7,3},{8,12},{9,13},{10,... | collective-permute-start | bytes 350216 | tf_op jit(solution)/shard_map/ppermute | solution.py:557
  111.2 10.8 %collective-permute-start.43 = (bf16[24,2432]{1,0:T(8,128)(2,1)S(1)}, bf16[24,2432]{1,0:T(8,128)(2,1)S(1)}, u32[]{:S(2)}, u32[]{:S(2)}) collective-permute-start(bf16[24,2432]{1,0:T(8,128)(2,1)S(1)} %get-tuple-element.178), channel_id=1, source_target_pairs={{0,8},{1,9},{2,10},{3,11},{4,12},{5,13},{6,14},{7,15},{8,0},{9,1},... | collective-permute-start | bytes 350216 | tf_op jit(solution)/shard_map/ppermute | solution.py:557
  112.0 10.0 %collective-permute-start.44 = (bf16[24,2432]{1,0:T(8,128)(2,1)S(1)}, bf16[24,2432]{1,0:T(8,128)(2,1)S(1)}, u32[]{:S(2)}, u32[]{:S(2)}) collective-permute-start(bf16[24,2432]{1,0:T(8,128)(2,1)S(1)} %get-tuple-element.179), channel_id=1, source_target_pairs={{0,12},{1,13},{2,14},{3,15},{4,8},{5,9},{6,10},{7,11},{8,4},{9,5},... | collective-permute-start | bytes 350216 | tf_op jit(solution)/shard_map/ppermute | solution.py:557
  (18 other events, 102.3 us)

commit v5 on v4

--- a/solution.py
+++ b/solution.py
@@ -66,12 +66,27 @@
     return scratch[...].T
 
 
-def place_columns(plan, chunk_refs, shard, width, me, cols_ref):
+def place_columns(plan, chunk_refs, shard, me, cols_ref):
     for ref, spots in zip(chunk_refs, plan):
         for index, (mask, u) in spots:
             if u == 0:
                 rows = pl.ds(pl.multiple_of((me ^ mask) * shard, 16), shard)
-                cols_ref[rows, :] = ref[index + (slice(None), slice(width, width + 128))].astype(F32)
+                vec = ref[index + (slice(ref.shape[-2] - 16, None), slice(None))].astype(F32)
+                cols_ref[rows, :] = jnp.concatenate([vec, jnp.zeros((112, 128), F32)], axis=0).T[:shard, :]
+
+
+def place_tiles(plan, own_refs, got_refs, shard, ids, targets):
+    b, me, t = ids
+    for half, refs in ((b, own_refs), (1 - b, got_refs)):
+        for ref, spots in zip(refs, plan):
+            for index, (mask, u) in spots:
+                rows = pl.ds(pl.multiple_of((me ^ mask) * shard, 16), shard)
+                for i, target in enumerate(targets):
+                    tiles = target.shape[3] // 128
+                    for j in range(tiles):
+                        start = (i * tiles + j) * shard
+                        tile = ref[index + (slice(start, start + shard), slice(None))]
+                        target[half, t ^ u, rows, j * 128 : (j + 1) * 128] = tile
 
 
 def place_weights(plan, own_refs, got_refs, shard, ids, targets):
@@ -164,8 +179,8 @@
     vec = jnp.concatenate([gain_ref[...], bias_ref[...], jnp.zeros((2, shard), F32)], axis=0)
     vec = jnp.concatenate([vec, jnp.zeros((8, 128 - shard), F32)], axis=1)
     none = jnp.zeros((8, 128), F32)
-    vec = jnp.concatenate([jnp.where(first, vec, none), jnp.where(first, none, vec), jnp.zeros((112, 128), F32)], axis=0)
-    vec = vec.T[:shard, :].astype(BF16)
+    vec = [jnp.where(first, vec, none), jnp.where(first, none, vec), jnp.zeros((shard - 16, 128), F32)]
+    vec = jnp.concatenate(vec, axis=0).astype(BF16)
     half_0 = jnp.concatenate([qkv_ref[0], qkv_ref[1]], axis=1).astype(BF16)
     half_1 = jnp.concatenate([qkv_ref[2], out_ref[...]], axis=1).astype(BF16)
     up, down = up_ref[...].astype(BF16), down_ref[...].astype(BF16)
@@ -184,9 +199,11 @@
     keep = keep_ref[...]
     query, momentum = jnp.where(first, keep, got), jnp.where(first, got, keep)
     units = second_ref.shape[1] // 2
-    first_ref[:, :width] = query[:, :width]
-    first_ref[:, width : width + 128] = keep[:, width : width + 128] + got[:, width : width + 128]
-    first_ref[:, width + 128 :] = momentum[:, :width]
+    shard, tiles = query.shape[0], width // 128
+    for i, half in enumerate((query, momentum)):
+        for j in range(tiles):
+            first_ref[pl.ds((i * tiles + j) * shard, shard), :] = half[:, j * 128 : (j + 1) * 128]
+    first_ref[2 * tiles * shard :, :] = (keep + got)[:16, width : width + 128]
     second_ref[:, :units] = query[:, width + 128 :]
     second_ref[:, units:] = momentum[:, width + 128 :]
 
@@ -214,9 +231,9 @@
         w1_ref[...] = w1_given[...]
         cols_ref[...] = columns_of(vec_q, vec_m, spare)
     else:
-        wide, w1_m = w1_ref.shape[3], spare
-        place_columns(plan, own, shard, wide, ids[1], cols_ref)
-        place_weights(plan, own, got, shard, ids, [(w1_ref, 0, 0, wide), (w1_m, 0, wide + 128, wide)])
+        w1_m = spare
+        place_columns(plan, own, shard, ids[1], cols_ref)
+        place_tiles(plan, own, got, shard, ids, (w1_ref, w1_m))
     cols = cols_ref[...]
 
     def keep(hat, rstd, normed):
@@ -260,7 +277,7 @@
     rows_low = normed.T.astype(BF16)
     acc_ref[...] = res + cols[:, 5:6]
     tensors, units = w2_ref.shape[1], w2_ref.shape[3]
-    chunk = 256
+    chunk = 768
     parts = units // chunk
 
     def step(i, carry):
@@ -270,7 +287,7 @@
         acc_ref[...] += nt(w2_ref[1, t, :, c], (pre * half).astype(BF16))
         return carry
 
-    lax.fori_loop(0, tensors * parts, step, 0, unroll=6)
+    lax.fori_loop(0, tensors * parts, step, 0, unroll=2)
     momentum, query = acc_ref[...].T.astype(BF16), query_ref[...]
     first = ids[0] == 0
     out_ref[...] = momentum
@@ -319,7 +336,7 @@
     acc_ref[...] = res + cols[:, 5:6]
     dn_ref[...] = jnp.zeros_like(dn_ref)
     tensors, width, units = w2_ref.shape[1], w2_ref.shape[2], w2_ref.shape[3]
-    chunk = 256
+    chunk = 768
     parts = units // chunk
     half_rows = width // 2
 
@@ -341,7 +358,7 @@
             store_grads(plan, ids, ref, t, later, nn(gt_ref[rows, :], hidden).astype(BF16))
         return carry
 
-    lax.fori_loop(0, tensors * parts, step, 0, unroll=6)
+    lax.fori_loop(0, tensors * parts, step, 0, unroll=2)
     out_ref[...] = acc_ref[...].T.astype(BF16)
     d_n2 = dn_ref[...]
     d_res = cot_t + norm_cols_back(d_n2, hat, rstd, cols[:, 1:2])
@@ -758,8 +775,9 @@
         gain_rows[0],
         biases[0],
     )
-    other = nseq * (2 * t + 1 - branch)
-    send_crops = lax.dynamic_slice(crops[0], (other, 0, 0), (nseq, slots, width)).reshape(rows, width)
+    def send_crops(*deps):
+        other = nseq * (2 * t + 1 - branch)
+        return lax.dynamic_slice(after(crops, *deps)[0], (other, 0, 0), (nseq, slots, width)).reshape(rows, width)
 
     if fine:
         block = ((shard, width + 128 + units), BF16)
@@ -768,7 +786,7 @@
         )
         block_1, block_2 = call(
             functools.partial(split_kernel, width),
-            [((shard, 2 * width + 128), BF16), ((shard, 2 * units), BF16)],
+            [((2 * (width // 128) * shard + 16, 128), BF16), ((shard, 2 * units), BF16)],
             [block],
             (swap_cores(send), keep),
             hbm=1,
@@ -776,12 +794,12 @@
         )
         masks = [(0, 0)] + near
         plan = [[((j,), (m ^ n, u)) for j, (m, _) in enumerate(masks)] for n, u in [(0, 0)] + both_ways]
-        got_crops = swap_cores(send_crops)
         far_1 = [exchange(block_1, *peer) for peer in near]
-        stack_1, got_crops = after((jnp.stack([block_1, *far_1]), got_crops))
+        got_crops = swap_cores(send_crops(far_1[0]))
+        stack_1 = jnp.stack([block_1, *far_1])
         own_1 = [stack_1] + [exchange(stack_1, *peer) for peer in both_ways]
         got_1 = [swap_cores(x) for x in own_1]
-        parts = after([block_2] + [exchange(block_2, *peer) for peer in near], own_1[1], own_1[2])
+        parts = after([block_2] + [exchange(block_2, *peer) for peer in near], own_1[2], own_1[3])
         stack_q, stack_a, stack_b = (
             jnp.stack([x[..., start : start + wide] for x in parts])
             for start, wide in ((0, units), (units, units // 2), (units + units // 2, units // 2))
@@ -863,7 +881,7 @@
         return (encoded, crop_grad, qkv_grad, out_grad, up_grad, down_grad, gain_grad, bias_grad)
 
     weights_1, weights_2, weights_4 = gathered(shards, on_query, me, tensors, width, units)
-    got_crops = swap_cores(send_crops)
+    got_crops = swap_cores(send_crops())
     res, res_m, cols, *saved = attention(None, weights_1, got_crops)
     out_q, keep_g2, send_g2, d_res, vgrad = query_mlp(None, weights_2, res, cols)
     crop_keep, crop_send, keep_g1, send_g1 = query_back(d_res, vgrad, cols, saved)

time: 123 us -> 121 us (0.984)
  starting transfers between devices: 39.8 us -> 37.5 us
    ppermute x27, starting transfers between devices: 35.2 us -> 33.1 us  [exchange(): return lax.ppermute(block, SPAN, pairs)]
    ppermute x19, waiting for transfers between devices: 2.18 us -> 3.98 us  [swap_cores(): return lax.ppermute(block, 'branch', [(0, 1), (1, 0)])]
  transfers between devices with their start and end apart: 46 -> 46, of which waited for: 16 -> 19; matrix products, arithmetic and copies ran while one was open for 0% -> 1% of each run, Pallas kernels for 26% -> 25%
where the time goes in v5:
time: 121 us
  waiting for transfers between devices  47.3 us (39%)
  starting transfers between devices  37.5 us (31%)
  Pallas kernels  32.7 us (27%)
  local copies, waits for them, and re-layouts  2.12 us (2%)
    ppermute x27, waiting for transfers between devices, exchange(): return lax.ppermute(block, SPAN, pairs)  43.4 us
    ppermute x27, starting transfers between devices, exchange(): return lax.ppermute(block, SPAN, pairs)  33.1 us
    pallas_call x15, Pallas kernels, call(): pl.pallas_call(kernel, grid=(1,) if stream else (), out_shape=[jax.ShapeD...  32.7 us
    ppermute x19, starting transfers between devices, swap_cores(): return lax.ppermute(block, 'branch', [(0, 1), (1, 0)])  4.43 us
    ppermute x19, waiting for transfers between devices, swap_cores(): return lax.ppermute(block, 'branch', [(0, 1), (1, 0)])  3.98 us
  transfers between devices with their start and end apart: 46, of which 19 were waited for; matrix products, arithmetic and copies ran while one was open for 1% of the time, Pallas kernels for 25%

profile of v5, /device:TPU:0, one launch (start us, length us, event | category | flops | bytes accessed | tf_op | source)
XLA Modules:
  0.0 120.8 jit_solution(15315139719108844146)
XLA Ops:
  0.6 1.9 %shard_map.152 = (bf16[48,1280]{1,0:T(8,128)(2,1)}, bf16[48,1280]{1,0:T(8,128)(2,1)}) custom-call(f32[3,48,192]{2,1,0:T(8,128)} %bitcast.60, f32[48,192]{1,0:T(8,128)} %bitcast.68, f32[48,768]{1,0:T(8,128)} %bitcast.61, f32[48,768]{1,0:T(8,128)} %bitcast.62, f32[2,48]{1,0:T(2,128)} %bitcast.70, f32[4,48]{1,0:T(4,128)} %bitcast.69), custom_call_target="tpu_custom_call" | custom-call | tf_op jit(solution)/shard_map/pallas_call | solution.py:550
  3.1 1.2 collective-permute-done.got_ref
  5.3 3.0 %collective-permute-start.4 = (bf16[304,128]{1,0:T(8,128)(2,1)S(1)}, bf16[304,128]{1,0:T(8,128)(2,1)S(1)}, u32[]{:S(2)}, u32[]{:S(2)}) collective-permute-start(bf16[304,128]{1,0:T(8,128)(2,1)S(1)} %get-tuple-element.102), channel_id=1, source_target_pairs={{0,4},{1,5},{2,6},{3,7},{4,0},{5,1},{6,2},{7,3},{8,12},{9,13},{10,... | collective-permute-start | bytes 233480 | tf_op jit(solution)/shard_map/ppermute | solution.py:574
  8.3 2.6 %collective-permute-start.5 = (bf16[304,128]{1,0:T(8,128)(2,1)S(1)}, bf16[304,128]{1,0:T(8,128)(2,1)S(1)}, u32[]{:S(2)}, u32[]{:S(2)}) collective-permute-start(bf16[304,128]{1,0:T(8,128)(2,1)S(1)} %get-tuple-element.102), channel_id=1, source_target_pairs={{0,8},{1,9},{2,10},{3,11},{4,12},{5,13},{6,14},{7,15},{8,0},{9,1},... | collective-permute-start | bytes 233480 | tf_op jit(solution)/shard_map/ppermute | solution.py:574
  11.0 6.5 %collective-permute-done.5 = bf16[304,128]{1,0:T(8,128)(2,1)S(1)} collective-permute-done((bf16[304,128]{1,0:T(8,128)(2,1)S(1)}, bf16[304,128]{1,0:T(8,128)(2,1)S(1)}, u32[]{:S(2)}, u32[]{:S(2)}) %collective-permute-start.5) | collective-permute-done | bytes 77856 | tf_op jit(solution)/shard_map/ppermute | solution.py:574
  17.5 1.6 %collective-permute-start.7 = (bf16[4,304,128]{2,1,0:T(8,128)(2,1)S(1)}, bf16[4,304,128]{2,1,0:T(8,128)(2,1)S(1)}, u32[]{:S(2)}, u32[]{:S(2)}) collective-permute-start(bf16[4,304,128]{2,1,0:T(8,128)(2,1)S(1)} %pad_maximum_fusion.refs_2_), channel_id=1, source_target_pairs={{0,1},{1,0},{2,3},{3,2},{4,5},{5,4},{6,7},{7,6},{8,9},{9,8},{10,11... | collective-permute-start | bytes 933896 | tf_op jit(solution)/shard_map/ppermute | solution.py:574
  19.1 1.4 %collective-permute-start.8 = (bf16[4,304,128]{2,1,0:T(8,128)(2,1)S(1)}, bf16[4,304,128]{2,1,0:T(8,128)(2,1)S(1)}, u32[]{:S(2)}, u32[]{:S(2)}) collective-permute-start(bf16[4,304,128]{2,1,0:T(8,128)(2,1)S(1)} %pad_maximum_fusion.refs_2_), channel_id=1, source_target_pairs={{0,3},{1,2},{2,1},{3,0},{4,7},{5,6},{6,5},{7,4},{8,11},{9,10},{10,... | collective-permute-start | bytes 933896 | tf_op jit(solution)/shard_map/ppermute | solution.py:574
  20.6 1.5 %collective-permute-start.1 = (bf16[48,1536]{1,0:T(8,128)(2,1)S(1)}, bf16[48,1536]{1,0:T(8,128)(2,1)S(1)}, u32[]{:S(2)}, u32[]{:S(2)}) collective-permute-start(bf16[48,1536]{1,0:T(8,128)(2,1)S(1)} %get-tuple-element.103), channel_id=1, source_target_pairs={{0,4},{1,5},{2,6},{3,7},{4,0},{5,1},{6,2},{7,3},{8,12},{9,13},{10,... | collective-permute-start | bytes 442376 | tf_op jit(solution)/shard_map/ppermute | solution.py:574
  22.1 1.6 %collective-permute-start.2 = (bf16[48,1536]{1,0:T(8,128)(2,1)S(1)}, bf16[48,1536]{1,0:T(8,128)(2,1)S(1)}, u32[]{:S(2)}, u32[]{:S(2)}) collective-permute-start(bf16[48,1536]{1,0:T(8,128)(2,1)S(1)} %get-tuple-element.103), channel_id=1, source_target_pairs={{0,8},{1,9},{2,10},{3,11},{4,12},{5,13},{6,14},{7,15},{8,0},{9,1},... | collective-permute-start | bytes 442376 | tf_op jit(solution)/shard_map/ppermute | solution.py:574
  23.6 1.3 %collective-permute-start.3 = (bf16[48,1536]{1,0:T(8,128)(2,1)S(1)}, bf16[48,1536]{1,0:T(8,128)(2,1)S(1)}, u32[]{:S(2)}, u32[]{:S(2)}) collective-permute-start(bf16[48,1536]{1,0:T(8,128)(2,1)S(1)} %get-tuple-element.103), channel_id=1, source_target_pairs={{0,12},{1,13},{2,14},{3,15},{4,8},{5,9},{6,10},{7,11},{8,4},{9,5},... | collective-permute-start | bytes 442376 | tf_op jit(solution)/shard_map/ppermute | solution.py:574
  25.0 1.2 constant_dynamic-slice_fusion
  27.3 7.3 %collective-permute-done.2 = bf16[48,1536]{1,0:T(8,128)(2,1)S(1)} collective-permute-done((bf16[48,1536]{1,0:T(8,128)(2,1)S(1)}, bf16[48,1536]{1,0:T(8,128)(2,1)S(1)}, u32[]{:S(2)}, u32[]{:S(2)}) %collective-permute-start.2) | collective-permute-done | bytes 147488 | tf_op jit(solution)/shard_map/ppermute | solution.py:574
  36.2 1.5 %collective-permute-start.10 = (bf16[4,48,768]{2,1,0:T(8,128)(2,1)S(1)}, bf16[4,48,768]{2,1,0:T(8,128)(2,1)S(1)}, u32[]{:S(2)}, u32[]{:S(2)}) collective-permute-start(bf16[4,48,768]{2,1,0:T(8,128)(2,1)S(1)} %pad_maximum_fusion.1.refs_2_), channel_id=1, source_target_pairs={{0,1},{1,0},{2,3},{3,2},{4,5},{5,4},{6,7},{7,6},{8,9},{9,8},{10,11... | collective-permute-start | bytes 884744 | tf_op jit(solution)/shard_map/ppermute | solution.py:574
  38.2 1.5 %collective-permute-start.9 = (bf16[4,48,768]{2,1,0:T(8,128)(2,1)S(1)}, bf16[4,48,768]{2,1,0:T(8,128)(2,1)S(1)}, u32[]{:S(2)}, u32[]{:S(2)}) collective-permute-start(bf16[4,48,768]{2,1,0:T(8,128)(2,1)S(1)} %pad_maximum_fusion.1.refs_2_), channel_id=1, source_target_pairs={{0,2},{1,3},{2,0},{3,1},{4,6},{5,7},{6,4},{7,5},{8,10},{9,11},{10,... | collective-permute-start | bytes 884744 | tf_op jit(solution)/shard_map/ppermute | solution.py:574
  40.4 1.5 %collective-permute-start.12 = (bf16[4,48,384]{2,1,0:T(8,128)(2,1)S(1)}, bf16[4,48,384]{2,1,0:T(8,128)(2,1)S(1)}, u32[]{:S(2)}, u32[]{:S(2)}) collective-permute-start(bf16[4,48,384]{2,1,0:T(8,128)(2,1)S(1)} %get-tuple-element.193), channel_id=1, source_target_pairs={{0,1},{1,0},{2,3},{3,2},{4,5},{5,4},{6,7},{7,6},{8,9},{9,8},{10,11... | collective-permute-start | bytes 442376 | tf_op jit(solution)/shard_map/ppermute | solution.py:574
  41.9 10.3 %shard_map.154 = (f32[384,512]{1,0:T(8,128)S(1)}, f32[384,512]{1,0:T(8,128)S(1)}, f32[384,128]{1,0:T(8,128)S(1)}, bf16[2,2,384,384]{3,2,1,0:T(8,128)(2,1)S(1)}, ...) custom-call(bf16[512,384]{1,0:T(8,128)(2,1)S(1)} %collective-permute, ...), custom_call_target="tpu_custom_call" | custom-call | tf_op jit(solution)/shard_map/pallas_call | solution.py:550
  52.2 4.1 %collective-permute-done.13 = bf16[4,48,384]{2,1,0:T(8,128)(2,1)S(1)} collective-permute-done((bf16[4,48,384]{2,1,0:T(8,128)(2,1)S(1)}, bf16[4,48,384]{2,1,0:T(8,128)(2,1)S(1)}, u32[]{:S(2)}, u32[]{:S(2)}) %collective-permute-start.13) | collective-permute-done | bytes 147488 | tf_op jit(solution)/shard_map/ppermute | solution.py:574
  57.4 1.3 %collective-permute-start.21 = (bf16[2,4,48,384]{3,2,1,0:T(8,128)(2,1)S(1)}, bf16[2,4,48,384]{3,2,1,0:T(8,128)(2,1)S(1)}, u32[]{:S(2)}, u32[]{:S(2)}) collective-permute-start(bf16[2,4,48,384]{3,2,1,0:T(8,128)(2,1)S(1)} %pad_maximum_fusion.3.refs_5_), channel_id=1, source_target_pairs={{0,1},{1,0},{2,3},{3,2},{4,5},{5,4},{6,7},{7,6},{8,9},{9,8},{10,11... | collective-permute-start | bytes 884744 | tf_op jit(solution)/shard_map/ppermute | solution.py:574
  59.4 6.8 %shard_map.155 = (bf16[512,384]{1,0:T(8,128)(2,1)S(1)}, bf16[4,4,24,1536]{3,2,1,0:T(8,128)(2,1)S(1)}, bf16[4,4,24,1536]{3,2,1,0:T(8,128)(2,1)S(1)}, f32[384,512]{1,0:T(8,128)S(1)}, f32[384,128]{1,0:T(8,128)S(1)}) custom-call(f32[384,512]{1,0:T(8,128)S(1)} %get-tuple-element.114.refs_0_, f32[384,128]{1,0:T(8,128)S(1)} %get-tuple-element.115.refs_1_.refs_2_, ...), custom_call_target="tpu_custom_call" | custom-call | tf_op jit(solution)/shard_map/pallas_call | solution.py:550
  72.1 3.6 %shard_map.157 = (bf16[512,384]{1,0:T(8,128)(2,1)S(1)}, bf16[512,384]{1,0:T(8,128)(2,1)S(1)}, bf16[512,384]{1,0:T(8,128)(2,1)S(1)}) custom-call(f32[384,512]{1,0:T(8,128)S(1)} %get-tuple-element.128.refs_0_, f32[384,128]{1,0:T(8,128)S(1)} %get-tuple-element.115.refs_1_.refs_2_, bf16[512,384]{1,0:T(8,128)(2,1)S(1)} %get-tuple-element.129.refs_2_, ...), custom_call_target="tpu_custom_call" | custom-call | tf_op jit(solution)/shard_map/pallas_call | solution.py:550
  75.7 3.4 %collective-permute-done.31.query_ref = bf16[512,384]{1,0:T(8,128)(2,1)S(1)} collective-permute-done((bf16[512,384]{1,0:T(8,128)(2,1)S(1)}, bf16[512,384]{1,0:T(8,128)(2,1)S(1)}, u32[]{:S(2)}, u32[]{:S(2)}) %collective-permute-start.31) | collective-permute-done | bytes 393248 | tf_op jit(solution)/shard_map/ppermute | solution.py:574
  79.9 6.0 %shard_map.158 = (f32[2,192,256]{2,1,0:T(8,128)S(1)}, bf16[2,192,256]{2,1,0:T(8,128)(2,1)S(1)}, bf16[4,4,24,896]{3,2,1,0:T(8,128)(2,1)S(1)}, bf16[4,4,24,896]{3,2,1,0:T(8,128)(2,1)S(1)}) custom-call(f32[384,512]{1,0:T(8,128)S(1)} %get-tuple-element.141.refs_0_, f32[384,128]{1,0:T(8,128)S(1)} %get-tuple-element.142.refs_1_, ...), custom_call_target="tpu_custom_call" | custom-call | tf_op jit(solution)/shard_map/pallas_call | solution.py:550
  85.9 3.4 %collective-permute-done.33.momentum_ref = bf16[512,384]{1,0:T(8,128)(2,1)S(1)} collective-permute-done((bf16[512,384]{1,0:T(8,128)(2,1)S(1)}, bf16[512,384]{1,0:T(8,128)(2,1)S(1)}, u32[]{:S(2)}, u32[]{:S(2)}) %collective-permute-start.33) | collective-permute-done | bytes 393248 | tf_op jit(solution)/shard_map/ppermute | solution.py:574
  93.0 2.2 %collective-permute-start.39 = (bf16[4,24,896]{2,1,0:T(8,128)(2,1)S(1)}, bf16[4,24,896]{2,1,0:T(8,128)(2,1)S(1)}, u32[]{:S(2)}, u32[]{:S(2)}) collective-permute-start(bf16[4,24,896]{2,1,0:T(8,128)(2,1)S(1)} %get-tuple-element.166), channel_id=1, source_target_pairs={{0,3},{1,2},{2,1},{3,0},{4,7},{5,6},{6,5},{7,4},{8,11},{9,10},{10,... | collective-permute-start | bytes 516104 | tf_op jit(solution)/shard_map/ppermute | solution.py:574
  95.3 8.2 %collective-permute-done.40.refs_1_ = bf16[4,24,1536]{2,1,0:T(8,128)(2,1)S(1)} collective-permute-done((bf16[4,24,1536]{2,1,0:T(8,128)(2,1)S(1)}, bf16[4,24,1536]{2,1,0:T(8,128)(2,1)S(1)}, u32[]{:S(2)}, u32[]{:S(2)}) %collective-permute-start.40) | collective-permute-done | bytes 294944 | tf_op jit(solution)/shard_map/ppermute | solution.py:574
  103.5 2.7 %collective-permute-done.37.refs_3_ = bf16[4,24,896]{2,1,0:T(8,128)(2,1)S(1)} collective-permute-done((bf16[4,24,896]{2,1,0:T(8,128)(2,1)S(1)}, bf16[4,24,896]{2,1,0:T(8,128)(2,1)S(1)}, u32[]{:S(2)}, u32[]{:S(2)}) %collective-permute-start.37) | collective-permute-done | bytes 172064 | tf_op jit(solution)/shard_map/ppermute | solution.py:574
  107.2 2.3 %collective-permute-start.42 = (bf16[24,2432]{1,0:T(8,128)(2,1)S(1)}, bf16[24,2432]{1,0:T(8,128)(2,1)S(1)}, u32[]{:S(2)}, u32[]{:S(2)}) collective-permute-start(bf16[24,2432]{1,0:T(8,128)(2,1)S(1)} %get-tuple-element.175), channel_id=1, source_target_pairs={{0,4},{1,5},{2,6},{3,7},{4,0},{5,1},{6,2},{7,3},{8,12},{9,13},{10,... | collective-permute-start | bytes 350216 | tf_op jit(solution)/shard_map/ppermute | solution.py:574
  110.1 1.8 %collective-permute-start.44 = (bf16[24,2432]{1,0:T(8,128)(2,1)S(1)}, bf16[24,2432]{1,0:T(8,128)(2,1)S(1)}, u32[]{:S(2)}, u32[]{:S(2)}) collective-permute-start(bf16[24,2432]{1,0:T(8,128)(2,1)S(1)} %get-tuple-element.177), channel_id=1, source_target_pairs={{0,12},{1,13},{2,14},{3,15},{4,8},{5,9},{6,10},{7,11},{8,4},{9,5},... | collective-permute-start | bytes 350216 | tf_op jit(solution)/shard_map/ppermute | solution.py:574
  112.0 1.2 shard_map.160
  113.1 3.3 %collective-permute-done.45.far_ref = bf16[2,2,192,256]{3,2,1,0:T(8,128)(2,1)S(1)} collective-permute-done((bf16[2,2,192,256]{3,2,1,0:T(8,128)(2,1)S(1)}, bf16[2,2,192,256]{3,2,1,0:T(8,128)(2,1)S(1)}, u32[]{:S(2)}, u32[]{:S(2)}) %collective-permute-start.45) | collective-permute-done | bytes 393248 | tf_op jit(solution)/shard_map/ppermute | solution.py:574
  116.4 1.3 %shard_map.165 = f32[2,2,2,192,256]{4,3,2,1,0:T(8,128)} custom-call(f32[2,192,256]{2,1,0:T(8,128)S(1)} %get-tuple-element.168.keep_ref, bf16[2,192,256]{2,1,0:T(8,128)(2,1)S(1)} %collective-permute-done.41.got_ref, bf16[2,2,192,256]{3,2,1,0:T(8,128)(2,1)S(1)} %collective-permute-done.45.far_ref), custom_call_target="tpu_custom_call" | custom-call | tf_op jit(solution)/shard_map/pallas_call | solution.py:550
  117.7 2.4 %collective-permute-done.43.refs_2_ = bf16[24,2432]{1,0:T(8,128)(2,1)S(1)} collective-permute-done((bf16[24,2432]{1,0:T(8,128)(2,1)S(1)}, bf16[24,2432]{1,0:T(8,128)(2,1)S(1)}, u32[]{:S(2)}, u32[]{:S(2)}) %collective-permute-start.43) | collective-permute-done | bytes 116768 | tf_op jit(solution)/shard_map/ppermute | solution.py:574
  (94 shorter events, 20.2 us)
Async XLA Ops:
  5.3 5.7 %collective-permute-start.4 = (bf16[304,128]{1,0:T(8,128)(2,1)S(1)}, bf16[304,128]{1,0:T(8,128)(2,1)S(1)}, u32[]{:S(2)}, u32[]{:S(2)}) collective-permute-start(bf16[304,128]{1,0:T(8,128)(2,1)S(1)} %get-tuple-element.102), channel_id=1, source_target_pairs={{0,4},{1,5},{2,6},{3,7},{4,0},{5,1},{6,2},{7,3},{8,12},{9,13},{10,... | collective-permute-start | bytes 233480 | tf_op jit(solution)/shard_map/ppermute | solution.py:574
  8.3 9.2 %collective-permute-start.5 = (bf16[304,128]{1,0:T(8,128)(2,1)S(1)}, bf16[304,128]{1,0:T(8,128)(2,1)S(1)}, u32[]{:S(2)}, u32[]{:S(2)}) collective-permute-start(bf16[304,128]{1,0:T(8,128)(2,1)S(1)} %get-tuple-element.102), channel_id=1, source_target_pairs={{0,8},{1,9},{2,10},{3,11},{4,12},{5,13},{6,14},{7,15},{8,0},{9,1},... | collective-permute-start | bytes 233480 | tf_op jit(solution)/shard_map/ppermute | solution.py:574
  10.9 6.6 %collective-permute-start.6 = (bf16[304,128]{1,0:T(8,128)(2,1)S(1)}, bf16[304,128]{1,0:T(8,128)(2,1)S(1)}, u32[]{:S(2)}, u32[]{:S(2)}) collective-permute-start(bf16[304,128]{1,0:T(8,128)(2,1)S(1)} %get-tuple-element.102), channel_id=1, source_target_pairs={{0,12},{1,13},{2,14},{3,15},{4,8},{5,9},{6,10},{7,11},{8,4},{9,5},... | collective-permute-start | bytes 233480 | tf_op jit(solution)/shard_map/ppermute | solution.py:574
  17.5 17.6 %collective-permute-start.7 = (bf16[4,304,128]{2,1,0:T(8,128)(2,1)S(1)}, bf16[4,304,128]{2,1,0:T(8,128)(2,1)S(1)}, u32[]{:S(2)}, u32[]{:S(2)}) collective-permute-start(bf16[4,304,128]{2,1,0:T(8,128)(2,1)S(1)} %pad_maximum_fusion.refs_2_), channel_id=1, source_target_pairs={{0,1},{1,0},{2,3},{3,2},{4,5},{5,4},{6,7},{7,6},{8,9},{9,8},{10,11... | collective-permute-start | bytes 933896 | tf_op jit(solution)/shard_map/ppermute | solution.py:574
  19.1 16.0 %collective-permute-start.8 = (bf16[4,304,128]{2,1,0:T(8,128)(2,1)S(1)}, bf16[4,304,128]{2,1,0:T(8,128)(2,1)S(1)}, u32[]{:S(2)}, u32[]{:S(2)}) collective-permute-start(bf16[4,304,128]{2,1,0:T(8,128)(2,1)S(1)} %pad_maximum_fusion.refs_2_), channel_id=1, source_target_pairs={{0,3},{1,2},{2,1},{3,0},{4,7},{5,6},{6,5},{7,4},{8,11},{9,10},{10,... | collective-permute-start | bytes 933896 | tf_op jit(solution)/shard_map/ppermute | solution.py:574
  20.6 6.2 %collective-permute-start.1 = (bf16[48,1536]{1,0:T(8,128)(2,1)S(1)}, bf16[48,1536]{1,0:T(8,128)(2,1)S(1)}, u32[]{:S(2)}, u32[]{:S(2)}) collective-permute-start(bf16[48,1536]{1,0:T(8,128)(2,1)S(1)} %get-tuple-element.103), channel_id=1, source_target_pairs={{0,4},{1,5},{2,6},{3,7},{4,0},{5,1},{6,2},{7,3},{8,12},{9,13},{10,... | collective-permute-start | bytes 442376 | tf_op jit(solution)/shard_map/ppermute | solution.py:574
  22.1 12.5 %collective-permute-start.2 = (bf16[48,1536]{1,0:T(8,128)(2,1)S(1)}, bf16[48,1536]{1,0:T(8,128)(2,1)S(1)}, u32[]{:S(2)}, u32[]{:S(2)}) collective-permute-start(bf16[48,1536]{1,0:T(8,128)(2,1)S(1)} %get-tuple-element.103), channel_id=1, source_target_pairs={{0,8},{1,9},{2,10},{3,11},{4,12},{5,13},{6,14},{7,15},{8,0},{9,1},... | collective-permute-start | bytes 442376 | tf_op jit(solution)/shard_map/ppermute | solution.py:574
  23.6 11.0 %collective-permute-start.3 = (bf16[48,1536]{1,0:T(8,128)(2,1)S(1)}, bf16[48,1536]{1,0:T(8,128)(2,1)S(1)}, u32[]{:S(2)}, u32[]{:S(2)}) collective-permute-start(bf16[48,1536]{1,0:T(8,128)(2,1)S(1)} %get-tuple-element.103), channel_id=1, source_target_pairs={{0,12},{1,13},{2,14},{3,15},{4,8},{5,9},{6,10},{7,11},{8,4},{9,5},... | collective-permute-start | bytes 442376 | tf_op jit(solution)/shard_map/ppermute | solution.py:574
  26.7 9.0 %collective-permute-start.15 = (bf16[4,304,128]{2,1,0:T(8,128)(2,1)S(1)}, bf16[4,304,128]{2,1,0:T(8,128)(2,1)S(1)}, u32[]{:S(2)}, u32[]{:S(2)}) collective-permute-start(bf16[4,304,128]{2,1,0:T(8,128)(2,1)S(1)} %pad_maximum_fusion.refs_2_), channel_id=1, source_target_pairs={{0,2},{1,3},{2,0},{3,1},{4,6},{5,7},{6,4},{7,5},{8,10},{9,11},{10,... | collective-permute-start | bytes 933896 | tf_op jit(solution)/shard_map/ppermute | solution.py:574
  35.2 4.6 %collective-permute-start.19 = (bf16[4,304,128]{2,1,0:T(8,128)(2,1)S(1)}, bf16[4,304,128]{2,1,0:T(8,128)(2,1)S(1)}, u32[]{:S(2)}, u32[]{:S(2)}) collective-permute-start(bf16[4,304,128]{2,1,0:T(8,128)(2,1)S(1)} %collective-permute-done.8.refs_5_), channel_id=1, source_target_pairs={{0,16},{16,0},{1,17},{17,1},{2,18},{18,2},{3,19},{19,3},{4,20},{20... | collective-permute-start | bytes 933896 | tf_op jit(solution)/shard_map/ppermute | solution.py:566
  35.7 4.7 %collective-permute-start.17 = (bf16[4,304,128]{2,1,0:T(8,128)(2,1)S(1)}, bf16[4,304,128]{2,1,0:T(8,128)(2,1)S(1)}, u32[]{:S(2)}, u32[]{:S(2)}) collective-permute-start(bf16[4,304,128]{2,1,0:T(8,128)(2,1)S(1)} %collective-permute-done.15.refs_3_), channel_id=1, source_target_pairs={{0,16},{16,0},{1,17},{17,1},{2,18},{18,2},{3,19},{19,3},{4,20},{20... | collective-permute-start | bytes 933896 | tf_op jit(solution)/shard_map/ppermute | solution.py:566
  36.2 20.1 %collective-permute-start.10 = (bf16[4,48,768]{2,1,0:T(8,128)(2,1)S(1)}, bf16[4,48,768]{2,1,0:T(8,128)(2,1)S(1)}, u32[]{:S(2)}, u32[]{:S(2)}) collective-permute-start(bf16[4,48,768]{2,1,0:T(8,128)(2,1)S(1)} %pad_maximum_fusion.1.refs_2_), channel_id=1, source_target_pairs={{0,1},{1,0},{2,3},{3,2},{4,5},{5,4},{6,7},{7,6},{8,9},{9,8},{10,11... | collective-permute-start | bytes 884744 | tf_op jit(solution)/shard_map/ppermute | solution.py:574
  37.7 18.6 %collective-permute-start.11 = (bf16[4,48,768]{2,1,0:T(8,128)(2,1)S(1)}, bf16[4,48,768]{2,1,0:T(8,128)(2,1)S(1)}, u32[]{:S(2)}, u32[]{:S(2)}) collective-permute-start(bf16[4,48,768]{2,1,0:T(8,128)(2,1)S(1)} %pad_maximum_fusion.1.refs_2_), channel_id=1, source_target_pairs={{0,3},{1,2},{2,1},{3,0},{4,7},{5,6},{6,5},{7,4},{8,11},{9,10},{10,... | collective-permute-start | bytes 884744 | tf_op jit(solution)/shard_map/ppermute | solution.py:574
  38.2 18.1 %collective-permute-start.9 = (bf16[4,48,768]{2,1,0:T(8,128)(2,1)S(1)}, bf16[4,48,768]{2,1,0:T(8,128)(2,1)S(1)}, u32[]{:S(2)}, u32[]{:S(2)}) collective-permute-start(bf16[4,48,768]{2,1,0:T(8,128)(2,1)S(1)} %pad_maximum_fusion.1.refs_2_), channel_id=1, source_target_pairs={{0,2},{1,3},{2,0},{3,1},{4,6},{5,7},{6,4},{7,5},{8,10},{9,11},{10,... | collective-permute-start | bytes 884744 | tf_op jit(solution)/shard_map/ppermute | solution.py:574
  39.8 16.5 %collective-permute-start.13 = (bf16[4,48,384]{2,1,0:T(8,128)(2,1)S(1)}, bf16[4,48,384]{2,1,0:T(8,128)(2,1)S(1)}, u32[]{:S(2)}, u32[]{:S(2)}) collective-permute-start(bf16[4,48,384]{2,1,0:T(8,128)(2,1)S(1)} %get-tuple-element.191), channel_id=1, source_target_pairs={{0,2},{1,3},{2,0},{3,1},{4,6},{5,7},{6,4},{7,5},{8,10},{9,11},{10,... | collective-permute-start | bytes 442376 | tf_op jit(solution)/shard_map/ppermute | solution.py:574
  40.4 15.9 %collective-permute-start.12 = (bf16[4,48,384]{2,1,0:T(8,128)(2,1)S(1)}, bf16[4,48,384]{2,1,0:T(8,128)(2,1)S(1)}, u32[]{:S(2)}, u32[]{:S(2)}) collective-permute-start(bf16[4,48,384]{2,1,0:T(8,128)(2,1)S(1)} %get-tuple-element.193), channel_id=1, source_target_pairs={{0,1},{1,0},{2,3},{3,2},{4,5},{5,4},{6,7},{7,6},{8,9},{9,8},{10,11... | collective-permute-start | bytes 442376 | tf_op jit(solution)/shard_map/ppermute | solution.py:574
  57.4 9.1 %collective-permute-start.21 = (bf16[2,4,48,384]{3,2,1,0:T(8,128)(2,1)S(1)}, bf16[2,4,48,384]{3,2,1,0:T(8,128)(2,1)S(1)}, u32[]{:S(2)}, u32[]{:S(2)}) collective-permute-start(bf16[2,4,48,384]{3,2,1,0:T(8,128)(2,1)S(1)} %pad_maximum_fusion.3.refs_5_), channel_id=1, source_target_pairs={{0,1},{1,0},{2,3},{3,2},{4,5},{5,4},{6,7},{7,6},{8,9},{9,8},{10,11... | collective-permute-start | bytes 884744 | tf_op jit(solution)/shard_map/ppermute | solution.py:574
  58.8 8.8 %collective-permute-start.20 = (bf16[2,4,48,384]{3,2,1,0:T(8,128)(2,1)S(1)}, bf16[2,4,48,384]{3,2,1,0:T(8,128)(2,1)S(1)}, u32[]{:S(2)}, u32[]{:S(2)}) collective-permute-start(bf16[2,4,48,384]{3,2,1,0:T(8,128)(2,1)S(1)} %pad_maximum_fusion.2.refs_3_), channel_id=1, source_target_pairs={{0,2},{1,3},{2,0},{3,1},{4,6},{5,7},{6,4},{7,5},{8,10},{9,11},{10,... | collective-permute-start | bytes 884744 | tf_op jit(solution)/shard_map/ppermute | solution.py:574
  68.1 11.0 %collective-permute-start.31 = (bf16[512,384]{1,0:T(8,128)(2,1)S(1)}, bf16[512,384]{1,0:T(8,128)(2,1)S(1)}, u32[]{:S(2)}, u32[]{:S(2)}) collective-permute-start(bf16[512,384]{1,0:T(8,128)(2,1)S(1)} %get-tuple-element.129.refs_2_), channel_id=1, source_target_pairs={{0,1},{1,0},{2,3},{3,2},{4,5},{5,4},{6,7},{7,6},{8,9},{9,8},{10,11... | collective-permute-start | bytes 1179656 | tf_op jit(solution)/shard_map/ppermute | solution.py:574
  70.9 18.4 %collective-permute-start.32 = (bf16[2,4,24,1536]{3,2,1,0:T(8,128)(2,1)S(1)}, bf16[2,4,24,1536]{3,2,1,0:T(8,128)(2,1)S(1)}, u32[]{:S(2)}, u32[]{:S(2)}) collective-permute-start(bf16[2,4,24,1536]{3,2,1,0:T(8,128)(2,1)S(1)} %get-tuple-element.138), channel_id=1, source_target_pairs={{0,2},{1,3},{2,0},{3,1},{4,6},{5,7},{6,4},{7,5},{8,10},{9,11},{10,... | collective-permute-start | bytes 1769480 | tf_op jit(solution)/shard_map/ppermute | solution.py:574
  79.1 10.2 %collective-permute-start.33 = (bf16[512,384]{1,0:T(8,128)(2,1)S(1)}, bf16[512,384]{1,0:T(8,128)(2,1)S(1)}, u32[]{:S(2)}, u32[]{:S(2)}) collective-permute-start(bf16[512,384]{1,0:T(8,128)(2,1)S(1)} %get-tuple-element.139), channel_id=1, source_target_pairs={{0,1},{1,0},{2,3},{3,2},{4,5},{5,4},{6,7},{7,6},{8,9},{9,8},{10,11... | collective-permute-start | bytes 1179656 | tf_op jit(solution)/shard_map/ppermute | solution.py:574
  89.3 5.9 %collective-permute-start.41 = (bf16[2,192,256]{2,1,0:T(8,128)(2,1)S(1)}, bf16[2,192,256]{2,1,0:T(8,128)(2,1)S(1)}, u32[]{:S(2)}, u32[]{:S(2)}) collective-permute-start(bf16[2,192,256]{2,1,0:T(8,128)(2,1)S(1)} %get-tuple-element.169), channel_id=1, source_target_pairs={{0,16},{16,0},{1,17},{17,1},{2,18},{18,2},{3,19},{19,3},{4,20},{20... | collective-permute-start | bytes 589832 | tf_op jit(solution)/shard_map/ppermute | solution.py:566
  89.9 13.6 %collective-permute-start.40 = (bf16[4,24,1536]{2,1,0:T(8,128)(2,1)S(1)}, bf16[4,24,1536]{2,1,0:T(8,128)(2,1)S(1)}, u32[]{:S(2)}, u32[]{:S(2)}) collective-permute-start(bf16[4,24,1536]{2,1,0:T(8,128)(2,1)S(1)} %get-tuple-element.167), channel_id=1, source_target_pairs={{0,1},{1,0},{2,3},{3,2},{4,5},{5,4},{6,7},{7,6},{8,9},{9,8},{10,11... | collective-permute-start | bytes 884744 | tf_op jit(solution)/shard_map/ppermute | solution.py:574
  91.6 14.7 %collective-permute-start.37 = (bf16[4,24,896]{2,1,0:T(8,128)(2,1)S(1)}, bf16[4,24,896]{2,1,0:T(8,128)(2,1)S(1)}, u32[]{:S(2)}, u32[]{:S(2)}) collective-permute-start(bf16[4,24,896]{2,1,0:T(8,128)(2,1)S(1)} %get-tuple-element.164), channel_id=1, source_target_pairs={{0,1},{1,0},{2,3},{3,2},{4,5},{5,4},{6,7},{7,6},{8,9},{9,8},{10,11... | collective-permute-start | bytes 516104 | tf_op jit(solution)/shard_map/ppermute | solution.py:574
  92.4 13.8 %collective-permute-start.38 = (bf16[4,24,896]{2,1,0:T(8,128)(2,1)S(1)}, bf16[4,24,896]{2,1,0:T(8,128)(2,1)S(1)}, u32[]{:S(2)}, u32[]{:S(2)}) collective-permute-start(bf16[4,24,896]{2,1,0:T(8,128)(2,1)S(1)} %get-tuple-element.165), channel_id=1, source_target_pairs={{0,2},{1,3},{2,0},{3,1},{4,6},{5,7},{6,4},{7,5},{8,10},{9,11},{10,... | collective-permute-start | bytes 516104 | tf_op jit(solution)/shard_map/ppermute | solution.py:574
  93.0 13.3 %collective-permute-start.39 = (bf16[4,24,896]{2,1,0:T(8,128)(2,1)S(1)}, bf16[4,24,896]{2,1,0:T(8,128)(2,1)S(1)}, u32[]{:S(2)}, u32[]{:S(2)}) collective-permute-start(bf16[4,24,896]{2,1,0:T(8,128)(2,1)S(1)} %get-tuple-element.166), channel_id=1, source_target_pairs={{0,3},{1,2},{2,1},{3,0},{4,7},{5,6},{6,5},{7,4},{8,11},{9,10},{10,... | collective-permute-start | bytes 516104 | tf_op jit(solution)/shard_map/ppermute | solution.py:574
  95.2 15.0 %collective-permute-start.34 = (bf16[512,384]{1,0:T(8,128)(2,1)S(1)}, bf16[512,384]{1,0:T(8,128)(2,1)S(1)}, u32[]{:S(2)}, u32[]{:S(2)}) collective-permute-start(bf16[512,384]{1,0:T(8,128)(2,1)S(1)} %get-tuple-element.158), channel_id=1, source_target_pairs={{0,16},{16,0},{1,17},{17,1},{2,18},{18,2},{3,19},{19,3},{4,20},{20... | collective-permute-start | bytes 1179656 | tf_op jit(solution)/shard_map/ppermute | solution.py:566
  103.5 8.4 %collective-permute-start.35 = (bf16[512,384]{1,0:T(8,128)(2,1)S(1)}, bf16[512,384]{1,0:T(8,128)(2,1)S(1)}, u32[]{:S(2)}, u32[]{:S(2)}) collective-permute-start(bf16[512,384]{1,0:T(8,128)(2,1)S(1)} %get-tuple-element.159), channel_id=1, source_target_pairs={{0,16},{16,0},{1,17},{17,1},{2,18},{18,2},{3,19},{19,3},{4,20},{20... | collective-permute-start | bytes 1179656 | tf_op jit(solution)/shard_map/ppermute | solution.py:566
  106.3 10.2 %collective-permute-start.45 = (bf16[2,2,192,256]{3,2,1,0:T(8,128)(2,1)S(1)}, bf16[2,2,192,256]{3,2,1,0:T(8,128)(2,1)S(1)}, u32[]{:S(2)}, u32[]{:S(2)}) collective-permute-start(bf16[2,2,192,256]{3,2,1,0:T(8,128)(2,1)S(1)} %shard_map.163), channel_id=1, source_target_pairs={{0,1},{1,0},{2,3},{3,2},{4,5},{5,4},{6,7},{7,6},{8,9},{9,8},{10,11... | collective-permute-start | bytes 1179656 | tf_op jit(solution)/shard_map/ppermute | solution.py:574
  107.2 10.5 %collective-permute-start.42 = (bf16[24,2432]{1,0:T(8,128)(2,1)S(1)}, bf16[24,2432]{1,0:T(8,128)(2,1)S(1)}, u32[]{:S(2)}, u32[]{:S(2)}) collective-permute-start(bf16[24,2432]{1,0:T(8,128)(2,1)S(1)} %get-tuple-element.175), channel_id=1, source_target_pairs={{0,4},{1,5},{2,6},{3,7},{4,0},{5,1},{6,2},{7,3},{8,12},{9,13},{10,... | collective-permute-start | bytes 350216 | tf_op jit(solution)/shard_map/ppermute | solution.py:574
  109.5 10.6 %collective-permute-start.43 = (bf16[24,2432]{1,0:T(8,128)(2,1)S(1)}, bf16[24,2432]{1,0:T(8,128)(2,1)S(1)}, u32[]{:S(2)}, u32[]{:S(2)}) collective-permute-start(bf16[24,2432]{1,0:T(8,128)(2,1)S(1)} %get-tuple-element.176), channel_id=1, source_target_pairs={{0,8},{1,9},{2,10},{3,11},{4,12},{5,13},{6,14},{7,15},{8,0},{9,1},... | collective-permute-start | bytes 350216 | tf_op jit(solution)/shard_map/ppermute | solution.py:574
  110.1 9.9 %collective-permute-start.44 = (bf16[24,2432]{1,0:T(8,128)(2,1)S(1)}, bf16[24,2432]{1,0:T(8,128)(2,1)S(1)}, u32[]{:S(2)}, u32[]{:S(2)}) collective-permute-start(bf16[24,2432]{1,0:T(8,128)(2,1)S(1)} %get-tuple-element.177), channel_id=1, source_target_pairs={{0,12},{1,13},{2,14},{3,15},{4,8},{5,9},{6,10},{7,11},{8,4},{9,5},... | collective-permute-start | bytes 350216 | tf_op jit(solution)/shard_map/ppermute | solution.py:574
  (18 other events, 87.7 us)
